TPU v7x, 32 devices: a whole 2x2x4 slice. The times are simulated.
32 devices in a mesh: groups: 2 (over y), space: 4 (over x, core), filt: 4 (over z).
Axes of the slice: x: 2, y: 2, z: 4, core: 2. Of those that a mesh axis runs over, the one named last changes fastest.
Arguments:
- volume: bfloat16 [64, 16, 32, 512], P('filt', ('groups', 'space')), parts along dimension 1, may hold values from -6 to 6
- conv_weight: bfloat16 [3, 3, 3, 4096], replicated, may hold values from -0.15625 to 0.15625
- down_weight: bfloat16 [3, 3, 3, 8192], replicated, may hold values from -0.15625 to 0.15625
Outputs:
- coarse: bfloat16 [128, 8, 16, 256], P(None, ('groups', 'space'), 'filt'), parts along dimension 1
There are 2 independent parts, one for each index of `groups`. A program takes and returns all parts, laid end to end along the dimension named above; an argument that names none is the same for every part. Nothing has to cross between parts.
All inputs are finite; a program needn't handle non-finite values.
Results may differ from a plain program's by a relative error of at most 0.0049.
Values may be sent and summed in bfloat16 or wider, within the bound.
No kernel may reach another device: no remote copies, remote signals or barrier semaphores. Data moves between devices by JAX's collectives and lax.ppermute only.
A program may use at most 128 MiB of HBM per device.

v0:
```python
import jax
import jax.numpy as jnp
from jax import lax
from jax.sharding import PartitionSpec as P

C = 64


negative_slope = 0.01


def extended_2(block, sides, width):
    for axis, dim in sides:
        count = lax.axis_size(axis)
        forward = [(i, i + 1) for i in range(count - 1)]
        backward = [(target, source) for source, target in forward]
        low = lax.ppermute(
            lax.slice_in_dim(block, block.shape[dim] - width, None, axis=dim), axis, forward
        )
        high = lax.ppermute(lax.slice_in_dim(block, 0, width, axis=dim), axis, backward)
        block = jnp.concatenate([low, block, high], axis=dim)
    return block


def from_behind(shard, axis, by):
    count = lax.axis_size(axis)
    pairs = [(i, i + by) for i in range(count) if 0 <= i + by < count]
    return lax.ppermute(shard, axis, pairs)


def unflatten(weight, in_count):
    out_count = weight.shape[3] // in_count
    shaped = weight.reshape(3, 3, 3, out_count, in_count)
    return jnp.transpose(shaped, (3, 4, 0, 1, 2))


def conv_valid(field, kernel, strides):
    result = lax.conv_general_dilated(
        field[None],
        kernel,
        strides,
        "VALID",
        dimension_numbers=("NCDHW", "OIDHW", "NCDHW"),
        preferred_element_type=jnp.float32,
    )
    return result[0]


def local(volume, conv_weight, down_weight):
    in_count = C
    conv_kernel = unflatten(conv_weight, in_count)
    down_kernel = unflatten(down_weight, in_count)
    gathered = lax.all_to_all(volume, "filt", split_axis=2, concat_axis=0, tiled=True)
    padded = extended_2(gathered, (("space", 1), ("filt", 2)), 1)
    padded = jnp.pad(padded, ((0, 0), (0, 0), (0, 0), (1, 1)))
    feature = conv_valid(padded, conv_kernel, (1, 1, 1))
    hidden = jnp.where(feature > 0, feature, negative_slope * feature).astype(jnp.bfloat16)
    below_plane = from_behind(hidden[:, -1:], "space", 1)
    extended = jnp.concatenate([below_plane, hidden], axis=1)
    below_row = from_behind(extended[:, :, -1:], "filt", 1)
    extended = jnp.concatenate([below_row, extended], axis=2)
    extended = jnp.pad(extended, ((0, 0), (0, 0), (0, 0), (1, 0)))
    coarse = conv_valid(extended, down_kernel, (2, 2, 2))
    return coarse.astype(jnp.bfloat16)


def solution(mesh):
    return jax.shard_map(
        local,
        mesh=mesh,
        in_specs=(P("filt", ("groups", "space"), None, None), P(), P()),
        out_specs=P(None, ("groups", "space"), "filt", None),
        check_vma=False,
    )
```

profile of v0, /device:TPU:1, one launch (start us, length us, event | category | flops | bytes accessed | tf_op | source)
XLA Modules:
  0.0 159.4 jit_solution(6482182004897351846)
XLA Ops:
  0.0 1.8 %copy.32 = bf16[16,2,32,512]{3,0,1,2:T(8,128)(2,1)S(1)} copy(bf16[16,2,32,512]{3,2,1,0:T(8,128)(2,1)} %param.3) | data formatting | bytes 2097152 | tf_op args[0]
  1.8 30.2 %all_to_all.18 = bf16[16,2,32,512]{3,0,1,2:T(8,128)(2,1)S(1)} all-to-all(bf16[16,2,32,512]{3,0,1,2:T(8,128)(2,1)S(1)} %copy.32), channel_id=1, replica_groups=mesh['groups'=2,'space'=4,'filt'=4] {'filt'}, dimensions={2} | all-to-all | bytes 2097152 | tf_op jit(solution)/shard_map/all_to_all | solution.py:53
  32.7 4.8 %collective-permute-start = (bf16[64,1,8,512]{3,2,1,0:T(8,128)(2,1)S(1)}, bf16[64,1,8,512]{3,2,1,0:T(8,128)(2,1)S(1)}, u32[]{:S(2)}, u32[]{:S(2)}) collective-permute-start(bf16[64,1,8,512]{3,2,1,0:T(8,128)(2,1)S(1)} %get-tuple-element.7), channel_id=1, source_target_pairs={{0,4},{4,8},{8,12},{1,5},{5,9},{9,13},{2,6},{6,10},{10,14},{3,7},{... | collective-permute-start | bytes 1572872 | tf_op jit(solution)/shard_map/ppermute | solution.py:17
  37.5 1.9 %collective-permute-start.1 = (bf16[64,1,8,512]{3,2,1,0:T(8,128)(2,1)S(1)}, bf16[64,1,8,512]{3,2,1,0:T(8,128)(2,1)S(1)}, u32[]{:S(2)}, u32[]{:S(2)}) collective-permute-start(bf16[64,1,8,512]{3,2,1,0:T(8,128)(2,1)S(1)} %get-tuple-element.8), channel_id=1, source_target_pairs={{4,0},{8,4},{12,8},{5,1},{9,5},{13,9},{6,2},{10,6},{14,10},{7,3},{... | collective-permute-start | bytes 1572872 | tf_op jit(solution)/shard_map/ppermute | solution.py:20
  39.5 4.2 %collective-permute-done = bf16[64,1,8,512]{3,2,1,0:T(8,128)(2,1)S(1)} collective-permute-done((bf16[64,1,8,512]{3,2,1,0:T(8,128)(2,1)S(1)}, bf16[64,1,8,512]{3,2,1,0:T(8,128)(2,1)S(1)}, u32[]{:S(2)}, u32[]{:S(2)}) %collective-permute-start) | collective-permute-done | bytes 524320 | tf_op jit(solution)/shard_map/ppermute | solution.py:17
  43.6 4.4 %collective-permute-done.1 = bf16[64,1,8,512]{3,2,1,0:T(8,128)(2,1)S(1)} collective-permute-done((bf16[64,1,8,512]{3,2,1,0:T(8,128)(2,1)S(1)}, bf16[64,1,8,512]{3,2,1,0:T(8,128)(2,1)S(1)}, u32[]{:S(2)}, u32[]{:S(2)}) %collective-permute-start.1) | collective-permute-done | bytes 524320 | tf_op jit(solution)/shard_map/ppermute | solution.py:20
  48.0 1.7 %pad_maximum_fusion.2 = (bf16[64,4,1,512]{3,2,1,0:T(2,128)(2,1)}, bf16[64,4,1,512]{3,2,1,0:T(2,128)(2,1)}) fusion(bf16[64,1,8,512]{3,2,1,0:T(8,128)(2,1)S(1)} %collective-permute-done.1, bf16[64,2,8,512]{3,2,1,0:T(8,128)(2,1)S(1)} %bitcast.44, bf16[64,1,8,512]{3,2,1,0:T(8,128)(2,1)S(1)} %collective-permute-done), kind=kLoop, calls=%fused_computation.44 | loop fusion | flops 1572864 | bytes 2621440 | tf_op jit(solution)/shard_map/slice | solution.py:18
  49.7 2.2 %collective-permute-start.2 = (bf16[64,4,1,512]{3,2,1,0:T(2,128)(2,1)}, bf16[64,4,1,512]{3,2,1,0:T(2,128)(2,1)S(1)}, u32[]{:S(2)}, u32[]{:S(2)}) collective-permute-start(bf16[64,4,1,512]{3,2,1,0:T(2,128)(2,1)} %get-tuple-element.5), channel_id=1, source_target_pairs={{0,1},{1,2},{2,3},{4,5},{5,6},{6,7},{8,9},{9,10},{10,11},{12,13},{... | collective-permute-start | bytes 786440 | tf_op jit(solution)/shard_map/ppermute | solution.py:17
  51.9 1.3 collective-permute-start.3
  53.2 1.2 reshape.19
  54.4 3.9 %collective-permute-done.2 = bf16[64,4,1,512]{3,2,1,0:T(2,128)(2,1)S(1)} collective-permute-done((bf16[64,4,1,512]{3,2,1,0:T(2,128)(2,1)}, bf16[64,4,1,512]{3,2,1,0:T(2,128)(2,1)S(1)}, u32[]{:S(2)}, u32[]{:S(2)}) %collective-permute-start.2) | collective-permute-done | bytes 262176 | tf_op jit(solution)/shard_map/ppermute | solution.py:17
  58.2 3.7 %collective-permute-done.3 = bf16[64,4,1,512]{3,2,1,0:T(2,128)(2,1)S(1)} collective-permute-done((bf16[64,4,1,512]{3,2,1,0:T(2,128)(2,1)}, bf16[64,4,1,512]{3,2,1,0:T(2,128)(2,1)S(1)}, u32[]{:S(2)}, u32[]{:S(2)}) %collective-permute-start.3) | collective-permute-done | bytes 262176 | tf_op jit(solution)/shard_map/ppermute | solution.py:20
  62.0 7.5 %fusion.10 = bf16[64,4,10,1,514]{4,2,1,0,3:T(8,128)(2,1)S(1)} fusion(bf16[64,4,1,512]{3,2,1,0:T(2,128)(2,1)S(1)} %collective-permute-done.3, bf16[64,4,1,512]{3,2,1,0:T(2,128)(2,1)S(1)} %collective-permute-done.2, bf16[64,1,8,512]{3,2,1,0:T(8,128)(2,1)S(1)} %collective-permute-done.1, bf16[64,2,8,512]{3,2,1,0:T(8,128)(2,1)S(1)} %bitcast.45, ...), kind=kLoop, calls=%fused_computation.15 | loop fusion | flops 23685120 | bytes 5253120 | tf_op jit(solution)/shard_map/broadcast_in_dim | solution.py:39
  69.5 3.4 %pad.10 = bf16[64,4,10,1,520]{4,2,1,0,3:T(8,128)(2,1)} pad(bf16[64,4,10,1,514]{4,2,1,0,3:T(8,128)(2,1)S(1)} %fusion.10, bf16[]{:T(256)} %constant.1.clone.1), padding=0_0x0_0x0_0x0_0x0_6 | pad | bytes 5294082 | tf_op jit(solution)/shard_map/broadcast_in_dim | solution.py:39
  72.8 10.6 %reshape.45 = bf16[64,4,10,1,8,65]{5,4,2,1,0,3:T(8,128)(2,1)} reshape(bf16[64,4,10,1,520]{4,2,1,0,3:T(8,128)(2,1)} %pad.10) | data formatting | bytes 5324800 | tf_op jit(solution)/shard_map/conv_general_dilated | solution.py:38
  83.5 9.3 %copy.37 = bf16[64,4,10,1,8,65]{0,4,5,2,1,3:T(8,128)(2,1)} copy(bf16[64,4,10,1,8,65]{5,4,2,1,0,3:T(8,128)(2,1)} %reshape.45) | data formatting | bytes 5324800 | tf_op jit(solution)/shard_map/conv_general_dilated | solution.py:38
  92.8 1.0 slice.30
  93.7 19.4 %broadcast_select_fusion = f32[2,8,8,65,64]{4,2,3,1,0:T(8,128)} fusion(pred[8,65]{0,1:T(8,128)(4,1)S(1)} %copy-done.3, bf16[3,3,3,64,64]{4,3,2,1,0:T(8,128)(2,1)S(1)} %copy-done.1, bf16[64,4,10,1,7,2]{0,4,5,2,1,3:T(8,128)(2,1)S(1)} %slice.30, bf16[64,4,10,1,8,65]{0,4,5,2,1,3:T(8,128)(2,1)} %copy.37), kind=kOutput, calls=%fused_computation.36 | convolution fusion | flops 1849016320 | bytes 5085704 | tf_op jit(solution)/shard_map/conv_general_dilated | solution.py:38
  113.2 5.4 %copy.38 = f32[2,8,8,65,64]{3,2,4,1,0:T(8,128)} copy(f32[2,8,8,65,64]{4,2,3,1,0:T(8,128)} %broadcast_select_fusion) | data formatting | bytes 4259840 | tf_op jit(solution)/shard_map/conv_general_dilated | solution.py:38
  118.6 5.1 %reshape.27 = f32[2,8,1,520,64]{3,4,1,0,2:T(8,128)} reshape(f32[2,8,8,65,64]{3,2,4,1,0:T(8,128)} %copy.38) | data formatting | bytes 4259840 | tf_op jit(solution)/shard_map/conv_general_dilated | solution.py:38
  123.7 1.9 %fusion.30 = bf16[64,2,8,512]{3,0,2,1:T(8,128)(2,1)S(1)} fusion(f32[2,8,1,520,64]{3,4,1,0,2:T(8,128)} %reshape.27), kind=kLoop, calls=%fused_computation.37 | loop fusion | flops 2097152 | bytes 3145728 | tf_op jit(solution)/shard_map/convert_element_type | solution.py:57
  125.6 2.9 %collective-permute-start.4 = (bf16[64,1,8,512]{3,0,2,1:T(8,128)(2,1)S(1)}, bf16[64,1,8,512]{3,0,2,1:T(8,128)(2,1)S(1)}, u32[]{:S(2)}, u32[]{:S(2)}) collective-permute-start(bf16[64,1,8,512]{3,0,2,1:T(8,128)(2,1)S(1)} %slice.32), channel_id=1, source_target_pairs={{0,4},{4,8},{8,12},{1,5},{5,9},{9,13},{2,6},{6,10},{10,14},{3,7},{... | collective-permute-start | bytes 1572872 | tf_op jit(solution)/shard_map/ppermute | solution.py:28
  128.5 6.1 %collective-permute-done.4 = bf16[64,1,8,512]{3,0,2,1:T(8,128)(2,1)S(1)} collective-permute-done((bf16[64,1,8,512]{3,0,2,1:T(8,128)(2,1)S(1)}, bf16[64,1,8,512]{3,0,2,1:T(8,128)(2,1)S(1)}, u32[]{:S(2)}, u32[]{:S(2)}) %collective-permute-start.4) | collective-permute-done | bytes 524320 | tf_op jit(solution)/shard_map/ppermute | solution.py:28
  134.6 2.2 %collective-permute-start.5 = (bf16[64,3,1,512]{3,0,2,1:T(8,128)(2,1)S(1)}, bf16[64,3,1,512]{3,0,2,1:T(8,128)(2,1)S(1)}, u32[]{:S(2)}, u32[]{:S(2)}) collective-permute-start(bf16[64,3,1,512]{3,0,2,1:T(8,128)(2,1)S(1)} %pad_maximum_fusion.3), channel_id=1, source_target_pairs={{0,1},{1,2},{2,3},{4,5},{5,6},{6,7},{8,9},{9,10},{10,11},{12,13},{... | collective-permute-start | bytes 589832 | tf_op jit(solution)/shard_map/ppermute | solution.py:28
  136.8 1.6 %reshape.20 = bf16[3,3,3,128,64]{4,3,2,1,0:T(8,128)(2,1)} reshape(bf16[3,3,3,8192]{3,2,1,0:T(4,128)(2,1)S(1)} %copy-done) | data formatting | bytes 884736 | tf_op jit(solution)/shard_map/reshape | solution.py:33
  138.5 0.9 collective-permute-done.5
  139.4 1.2 fusion.28
  140.6 1.6 %pad.12 = bf16[64,3,9,1,528]{4,0,2,1,3:T(8,128)(2,1)} pad(bf16[64,3,9,1,513]{4,0,2,1,3:T(8,128)(2,1)S(1)} %fusion.28, bf16[]{:T(256)} %constant.1.clone.1), padding=0_0x0_0x0_0x0_0x0_15 | pad | bytes 3597698 | tf_op jit(solution)/shard_map/broadcast_in_dim | solution.py:39
  142.3 5.5 %reshape.30 = bf16[64,3,9,1,8,66]{5,4,0,2,1,3:T(8,128)(2,1)S(1)} reshape(bf16[64,3,9,1,528]{4,0,2,1,3:T(8,128)(2,1)} %pad.12) | data formatting | bytes 3649536 | tf_op jit(solution)/shard_map/conv_general_dilated | solution.py:38
  147.8 5.2 %copy.40 = bf16[64,3,9,1,8,66]{0,4,5,2,1,3:T(8,128)(2,1)} copy(bf16[64,3,9,1,8,66]{5,4,0,2,1,3:T(8,128)(2,1)S(1)} %reshape.30) | data formatting | bytes 3649536 | tf_op jit(solution)/shard_map/conv_general_dilated | solution.py:38
  153.0 0.9 slice.33
  153.9 4.3 %fusion.37 = bf16[1,4,8,33,128]{4,2,3,1,0:T(8,128)(2,1)S(1)} fusion(bf16[3,3,3,128,64]{4,3,2,1,0:T(8,128)(2,1)} %reshape.20, bf16[64,3,9,1,7,2]{0,4,5,2,1,3:T(8,128)(2,1)S(1)} %slice.33, bf16[64,3,9,1,8,66]{0,4,5,2,1,3:T(8,128)(2,1)} %copy.40, pred[8,33]{0,1:T(8,128)(4,1)S(1)} %copy-done.4), kind=kOutput, calls=%fused_computation.41 | convolution fusion | flops 473051136 | bytes 2586120 | tf_op jit(solution)/shard_map/conv_general_dilated | solution.py:38
  (17 shorter events, 1.8 us)
Async XLA Ops:
  1.8 51.4 %copy-start.2 = (bf16[3,3,3,4096]{3,2,1,0:T(4,128)(2,1)S(1)}, bf16[3,3,3,4096]{3,2,1,0:T(4,128)(2,1)}, u32[]{:S(2)}) copy-start(bf16[3,3,3,4096]{3,2,1,0:T(4,128)(2,1)} %param.4) | copy-start | bytes 663556
  32.7 10.9 %collective-permute-start = (bf16[64,1,8,512]{3,2,1,0:T(8,128)(2,1)S(1)}, bf16[64,1,8,512]{3,2,1,0:T(8,128)(2,1)S(1)}, u32[]{:S(2)}, u32[]{:S(2)}) collective-permute-start(bf16[64,1,8,512]{3,2,1,0:T(8,128)(2,1)S(1)} %get-tuple-element.7), channel_id=1, source_target_pairs={{0,4},{4,8},{8,12},{1,5},{5,9},{9,13},{2,6},{6,10},{10,14},{3,7},{... | collective-permute-start | bytes 1572872 | tf_op jit(solution)/shard_map/ppermute | solution.py:17
  37.5 10.5 %collective-permute-start.1 = (bf16[64,1,8,512]{3,2,1,0:T(8,128)(2,1)S(1)}, bf16[64,1,8,512]{3,2,1,0:T(8,128)(2,1)S(1)}, u32[]{:S(2)}, u32[]{:S(2)}) collective-permute-start(bf16[64,1,8,512]{3,2,1,0:T(8,128)(2,1)S(1)} %get-tuple-element.8), channel_id=1, source_target_pairs={{4,0},{8,4},{12,8},{5,1},{9,5},{13,9},{6,2},{10,6},{14,10},{7,3},{... | collective-permute-start | bytes 1572872 | tf_op jit(solution)/shard_map/ppermute | solution.py:20
  49.7 8.6 %collective-permute-start.2 = (bf16[64,4,1,512]{3,2,1,0:T(2,128)(2,1)}, bf16[64,4,1,512]{3,2,1,0:T(2,128)(2,1)S(1)}, u32[]{:S(2)}, u32[]{:S(2)}) collective-permute-start(bf16[64,4,1,512]{3,2,1,0:T(2,128)(2,1)} %get-tuple-element.5), channel_id=1, source_target_pairs={{0,1},{1,2},{2,3},{4,5},{5,6},{6,7},{8,9},{9,10},{10,11},{12,13},{... | collective-permute-start | bytes 786440 | tf_op jit(solution)/shard_map/ppermute | solution.py:17
  51.9 10.1 %collective-permute-start.3 = (bf16[64,4,1,512]{3,2,1,0:T(2,128)(2,1)}, bf16[64,4,1,512]{3,2,1,0:T(2,128)(2,1)S(1)}, u32[]{:S(2)}, u32[]{:S(2)}) collective-permute-start(bf16[64,4,1,512]{3,2,1,0:T(2,128)(2,1)} %get-tuple-element.6), channel_id=1, source_target_pairs={{1,0},{2,1},{3,2},{5,4},{6,5},{7,6},{9,8},{10,9},{11,10},{13,12},{... | collective-permute-start | bytes 786440 | tf_op jit(solution)/shard_map/ppermute | solution.py:20
  83.5 10.2 %copy-start.1 = (bf16[3,3,3,64,64]{4,3,2,1,0:T(8,128)(2,1)S(1)}, bf16[3,3,3,64,64]{4,3,2,1,0:T(8,128)(2,1)}, u32[]{:S(2)}) copy-start(bf16[3,3,3,64,64]{4,3,2,1,0:T(8,128)(2,1)} %reshape.19) | copy-start | bytes 663556
  83.5 10.2 %copy-start.3 = (pred[8,65]{0,1:T(8,128)(4,1)S(1)}, pred[8,65]{0,1:T(8,128)(4,1)}, u32[]{:S(2)}) copy-start(pred[8,65]{0,1:T(8,128)(4,1)} %constant.21) | copy-start | bytes 1564
  118.6 18.2 %copy-start = (bf16[3,3,3,8192]{3,2,1,0:T(4,128)(2,1)S(1)}, bf16[3,3,3,8192]{3,2,1,0:T(4,128)(2,1)}, u32[]{:S(2)}) copy-start(bf16[3,3,3,8192]{3,2,1,0:T(4,128)(2,1)} %param.5) | copy-start | bytes 1327108
  125.6 9.0 %collective-permute-start.4 = (bf16[64,1,8,512]{3,0,2,1:T(8,128)(2,1)S(1)}, bf16[64,1,8,512]{3,0,2,1:T(8,128)(2,1)S(1)}, u32[]{:S(2)}, u32[]{:S(2)}) collective-permute-start(bf16[64,1,8,512]{3,0,2,1:T(8,128)(2,1)S(1)} %slice.32), channel_id=1, source_target_pairs={{0,4},{4,8},{8,12},{1,5},{5,9},{9,13},{2,6},{6,10},{10,14},{3,7},{... | collective-permute-start | bytes 1572872 | tf_op jit(solution)/shard_map/ppermute | solution.py:28
  134.6 4.8 %collective-permute-start.5 = (bf16[64,3,1,512]{3,0,2,1:T(8,128)(2,1)S(1)}, bf16[64,3,1,512]{3,0,2,1:T(8,128)(2,1)S(1)}, u32[]{:S(2)}, u32[]{:S(2)}) collective-permute-start(bf16[64,3,1,512]{3,0,2,1:T(8,128)(2,1)S(1)} %pad_maximum_fusion.3), channel_id=1, source_target_pairs={{0,1},{1,2},{2,3},{4,5},{5,6},{6,7},{8,9},{9,10},{10,11},{12,13},{... | collective-permute-start | bytes 589832 | tf_op jit(solution)/shard_map/ppermute | solution.py:28
  142.3 11.7 %copy-start.4 = (pred[8,33]{0,1:T(8,128)(4,1)S(1)}, pred[8,33]{0,1:T(8,128)(4,1)}, u32[]{:S(2)}) copy-start(pred[8,33]{0,1:T(8,128)(4,1)} %constant.20) | copy-start | bytes 796
where the time goes:
time: 162 us; the launch traced here: 159 us
  local copies, waits for them, and re-layouts  54.5 us (34%)
  blocking collectives  30.2 us (19%)
  matrix products  23.8 us (15%)
  waiting for transfers between devices  23.2 us (14%)
  starting transfers between devices  15.2 us (9%)
  other arithmetic  12.3 us (8%)
    conv_general_dilated x8, local copies, waits for them, and re-layouts, conv_valid(): lax.conv_general_dilated(field[None], kernel, strides, 'VALID', dimension...  43.1 us
    all_to_all x1, blocking collectives, local(): lax.all_to_all(volume, 'filt', split_axis=2, concat_axis=0, tiled=True)  30.2 us
    conv_general_dilated x2, matrix products, conv_valid(): lax.conv_general_dilated(field[None], kernel, strides, 'VALID', dimension...  23.8 us
    broadcast_in_dim x2, other arithmetic, conv_valid(): field[None]  8.7 us
    ppermute x2, waiting for transfers between devices, extended_2(): lax.ppermute(lax.slice_in_dim(block, 0, width, axis=dim), axis, backward)  8.14 us
    ppermute x2, waiting for transfers between devices, extended_2(): lax.ppermute(lax.slice_in_dim(block, block.shape[dim] - width, None, axis...  8.07 us
    ppermute x2, waiting for transfers between devices, from_behind(): return lax.ppermute(shard, axis, pairs)  7.03 us
    ppermute x2, starting transfers between devices, extended_2(): lax.ppermute(lax.slice_in_dim(block, block.shape[dim] - width, None, axis...  6.97 us
  transfers between devices with their start and end apart: 6, of which 6 were waited for; matrix products, arithmetic and copies ran while one was open for 2% of the time, Pallas kernels for 0%

commit v1 on v0

v1 whole, which is shorter than its diff:
```python
import functools

import jax
import jax.numpy as jnp
from jax import lax
from jax.experimental import pallas as pl
from jax.experimental.pallas import tpu as pltpu
from jax.sharding import PartitionSpec as P

C = 64
C2 = 128
negative_slope = 0.01
VMEM_LIMIT = 56 * 1024 * 1024


def split_matrix(width):
    half = width // 2
    source = lax.broadcasted_iota(jnp.int32, (width, width), 0)
    column = lax.broadcasted_iota(jnp.int32, (width, width), 1)
    wanted = jnp.where(column < half, 2 * column, 2 * (column - half) + 1)
    return jnp.where(source == wanted, 1.0, 0.0).astype(jnp.bfloat16)


def gather_kernel(*refs):
    order_ref, pieces, out_ref = refs[0], refs[1:-1], refs[-1]
    rows, planes, count, width = pieces[0].shape
    split = split_matrix(width)
    for d, piece in enumerate(pieces):
        flat = piece[...].reshape(rows * planes * count, width)
        moved = jnp.dot(flat, split, preferred_element_type=jnp.float32)
        at = pl.multiple_of(order_ref[d] * count, count)
        out_ref[:, :, pl.ds(at, count), :] = moved.astype(jnp.bfloat16).reshape(
            rows, planes, count, width
        )


def conv_kernel(edge_ref, low_ref, own_ref, high_ref, first_ref, second_ref, out_ref, taps_ref, hid_ref):
    rows = own_ref.shape[0]
    half = own_ref.shape[3] // 2
    hid_rows = rows - 2
    lane = lax.broadcasted_iota(jnp.int32, (C, half), 1)
    for r in range(rows):
        for p in range(5):
            if p < 2:
                cell = low_ref[r, p]
            elif p < 4:
                cell = own_ref[r, p - 2]
            else:
                cell = high_ref[r, 0]
            even, odd = cell[:, :half], cell[:, half:]
            zero = jnp.zeros((C, half), jnp.float32)
            before = jnp.where(lane == 0, zero, pltpu.roll(odd.astype(jnp.float32), 1, 1))
            after = jnp.where(lane == half - 1, zero, pltpu.roll(even.astype(jnp.float32), half - 1, 1))
            base = r * 4 * C
            taps_ref[p, pl.ds(base, C), :] = before.astype(jnp.bfloat16)
            taps_ref[p, pl.ds(base + C, C), :] = even
            taps_ref[p, pl.ds(base + 2 * C, C), :] = odd
            taps_ref[p, pl.ds(base + 3 * C, C), :] = after.astype(jnp.bfloat16)
    size = 2 * C
    for y in range(hid_rows):
        total = [None] * 3
        for p in range(5):
            z_low, z_high = max(0, p - 2), min(2, p)
            first = 2 - (p - z_low)
            weight = first_ref[pl.ds(first * size, (z_high - z_low + 1) * size), :]
            part = jnp.dot(
                weight, taps_ref[p, pl.ds(y * 4 * C, 12 * C), :], preferred_element_type=jnp.float32
            )
            for z in range(z_low, z_high + 1):
                piece = part[(z - z_low) * size : (z - z_low + 1) * size]
                total[z] = piece if total[z] is None else total[z] + piece
        for z in range(3):
            value = total[z]
            value = jnp.where(value > 0, value, negative_slope * value)
            if z == 0:
                value = jnp.where(edge_ref[0] > 0, value, 0.0)
            if y == 0:
                value = jnp.where(edge_ref[1] > 0, value, 0.0)
            value = value.astype(jnp.bfloat16)
            odd = value[C:]
            before = jnp.where(lane == 0, 0.0, pltpu.roll(odd.astype(jnp.float32), 1, 1))
            base = (y * 3 + z) * 3 * C
            hid_ref[pl.ds(base, C), :] = before.astype(jnp.bfloat16)
            hid_ref[pl.ds(base + C, 2 * C), :] = value
    for y in range(out_ref.shape[0]):
        out_ref[y] = jnp.dot(
            second_ref[...], hid_ref[pl.ds(2 * y * 9 * C, 27 * C), :], preferred_element_type=jnp.float32
        ).astype(jnp.bfloat16)


def first_weights(conv_weight):
    shaped = jnp.transpose(conv_weight.reshape(3, 3, 3, C, C), (0, 3, 1, 2, 4))
    shaped = shaped[::-1]
    even = jnp.pad(shaped, ((0, 0), (0, 0), (0, 0), (0, 1), (0, 0)))
    odd = jnp.pad(shaped, ((0, 0), (0, 0), (0, 0), (1, 0), (0, 0)))
    return jnp.stack([even, odd], axis=1).reshape(3 * 2 * C, 12 * C)


def second_weights(down_weight):
    shaped = down_weight.reshape(3, 3, 3, C2, C)
    return jnp.transpose(shaped, (3, 1, 0, 2, 4)).reshape(C2, 27 * C)


def shifted(block, axis, by):
    count = lax.axis_size(axis)
    return lax.ppermute(block, axis, [(i, i + by) for i in range(count) if 0 <= i + by < count])


def local(volume, conv_weight, down_weight):
    bands = lax.axis_size("filt")
    me = lax.axis_index("filt")
    count, planes, all_rows, width = volume.shape
    band = all_rows // bands
    window = band + 3
    field = jnp.transpose(volume, (2, 1, 0, 3))
    field = jnp.pad(field, ((2, 1), (0, 0), (0, 0), (0, 0)))
    vmem = pl.BlockSpec(memory_space=pltpu.VMEM)
    smem = pl.BlockSpec(memory_space=pltpu.SMEM)
    params = pltpu.CompilerParams(vmem_limit_bytes=VMEM_LIMIT)
    if count % 16 == 0:
        pieces = []
        for d in range(bands):
            target = lax.rem(me + d, bands)
            piece = lax.dynamic_slice_in_dim(field, target * band, window, 0)
            if d:
                piece = lax.ppermute(piece, "filt", [(i, (i + d) % bands) for i in range(bands)])
            pieces.append(piece)
        order = lax.rem(me - jnp.arange(bands, dtype=jnp.int32) + bands, bands)
    else:
        sent = jnp.stack([field[t * band : t * band + window] for t in range(bands)])
        got = lax.all_to_all(sent, "filt", split_axis=0, concat_axis=0, tiled=True)
        pieces = [jnp.transpose(got, (1, 2, 0, 3, 4)).reshape(window, planes, C, width)]
        order = jnp.zeros((1,), jnp.int32)
    own = pl.pallas_call(
        gather_kernel,
        out_shape=jax.ShapeDtypeStruct((window, planes, C, width), jnp.bfloat16),
        in_specs=[smem] + [vmem] * len(pieces),
        out_specs=vmem,
        compiler_params=params,
    )(order, *pieces)
    low = shifted(own, "space", 1)
    high = shifted(own[:, :1], "space", -1)
    edge = jnp.stack([lax.axis_index("space"), me]).astype(jnp.int32)
    coarse = pl.pallas_call(
        conv_kernel,
        out_shape=jax.ShapeDtypeStruct((band // 2, C2, width // 2), jnp.bfloat16),
        in_specs=[smem] + [vmem] * 5,
        out_specs=vmem,
        scratch_shapes=[
            pltpu.VMEM((5, window * 4 * C, width // 2), jnp.bfloat16),
            pltpu.VMEM(((band + 1) * 9 * C, width // 2), jnp.bfloat16),
        ],
        compiler_params=params,
    )(edge, low, own, high, first_weights(conv_weight), second_weights(down_weight))
    return jnp.transpose(coarse, (1, 0, 2))[:, None]


def solution(mesh):
    return jax.shard_map(
        local,
        mesh=mesh,
        in_specs=(P("filt", ("groups", "space"), None, None), P(), P()),
        out_specs=P(None, ("groups", "space"), "filt", None),
        check_vma=False,
    )
```

time: 162 us -> 73.5 us (0.45); the launches traced: 159 us -> 73.2 us
  local copies, waits for them, and re-layouts: 54.5 us -> 14.9 us
  blocking collectives: 30.2 us -> 0 us
  matrix products: 23.8 us -> 0 us
  Pallas kernels: 0 us -> 11.4 us
  other arithmetic: 12.3 us -> 2.21 us
  waiting for transfers between devices: 23.2 us -> 33.1 us
  starting transfers between devices: 15.2 us -> 11.4 us
    conv_general_dilated x8 -> x0, local copies, waits for them, and re-layouts: 43.1 us -> none  [conv_valid(): lax.conv_general_dilated(field[None], kernel, strides, 'VALID', dimension...]
    all_to_all x1 -> x0, blocking collectives: 30.2 us -> none  [local(): lax.all_to_all(volume, 'filt', split_axis=2, concat_axis=0, tiled=True)]
    conv_general_dilated x2 -> x0, matrix products: 23.8 us -> none  [conv_valid(): lax.conv_general_dilated(field[None], kernel, strides, 'VALID', dimension...]
    pallas_call x0 -> x2, Pallas kernels: none -> 11.4 us  [the longest x1 8.05 us: local(): pl.pallas_call(conv_kernel, out_shape=jax.ShapeDtypeStruct((band // 2, C2...]
    ppermute x6 -> x5, waiting for transfers between devices: 23.2 us -> 33.1 us  [the longest x3 29.1 us: local(): lax.ppermute(piece, 'filt', [(i, (i + d) % bands) for i in range(bands)])]
    broadcast_in_dim x2 -> x0, other arithmetic: 8.7 us -> none  [conv_valid(): field[None]]
    ppermute x6 -> x5, starting transfers between devices: 15.2 us -> 11.4 us  [the longest x2 6.76 us: shifted(): lax.ppermute(block, axis, [(i, i + by) for i in range(count) if 0 <= i +...]
    broadcast_in_dim x2 -> x1, local copies, waits for them, and re-layouts: 4.98 us -> 1.86 us  [local(): return jnp.transpose(coarse, (1, 0, 2))[:, None]]
  transfers between devices with their start and end apart: 6 -> 5, of which waited for: 6 -> 5; matrix products, arithmetic and copies ran while one was open for 2% -> 15% of each run, Pallas kernels for 0% -> 0%
where the time goes in v1:
time: 73.5 us; the launch traced here: 73.2 us
  waiting for transfers between devices  33.1 us (45%)
  local copies, waits for them, and re-layouts  14.9 us (20%)
  starting transfers between devices  11.4 us (16%)
  Pallas kernels  11.4 us (16%)
  other arithmetic  2.21 us (3%)
    ppermute x3, waiting for transfers between devices, local(): lax.ppermute(piece, 'filt', [(i, (i + d) % bands) for i in range(bands)])  29.1 us
    pallas_call x1, Pallas kernels, local(): pl.pallas_call(conv_kernel, out_shape=jax.ShapeDtypeStruct((band // 2, C2...  8.05 us
    ppermute x2, starting transfers between devices, shifted(): lax.ppermute(block, axis, [(i, i + by) for i in range(count) if 0 <= i +...  6.76 us
    ppermute x3, starting transfers between devices, local(): lax.ppermute(piece, 'filt', [(i, (i + d) % bands) for i in range(bands)])  4.6 us
    ppermute x2, waiting for transfers between devices, shifted(): lax.ppermute(block, axis, [(i, i + by) for i in range(count) if 0 <= i +...  3.99 us
    unnamed x13, local copies, waits for them, and re-layouts  3.65 us
    pallas_call x1, Pallas kernels, local(): pl.pallas_call(gather_kernel, out_shape=jax.ShapeDtypeStruct((window, pla...  3.37 us
    slice x1, local copies, waits for them, and re-layouts, local(): high = shifted(own[:, :1], 'space', -1)  2.05 us
  transfers between devices with their start and end apart: 5, of which 5 were waited for; matrix products, arithmetic and copies ran while one was open for 15% of the time, Pallas kernels for 0%

profile of v1, /device:TPU:1, one launch (start us, length us, event | category | flops | bytes accessed | tf_op | source)
XLA Modules:
  0.0 73.2 jit_solution(11746619530101516136)
XLA Ops:
  0.0 1.8 %copy.17 = bf16[16,2,32,512]{3,0,1,2:T(8,128)(2,1)S(1)} copy(bf16[16,2,32,512]{3,2,1,0:T(8,128)(2,1)} %param.3) | data formatting | bytes 2097152 | tf_op args[0]
  1.8 1.0 %pad_dynamic-slice_fusion = (bf16[11,2,16,512]{3,2,1,0:T(8,128)(2,1)S(1)}, bf16[11,2,16,512]{3,2,1,0:T(8,128)(2,1)S(1)}, bf16[11,2,16,512]{3,2,1,0:T(8,128)(2,1)S(1)}, bf16[11,2,16,512]{3,2,1,0:T(8,128)(2,1)}) fusion(s32[]{:T(128)S(6)} %select_n.15, bf16[32,2,16,512]{3,2,1,0:T(8,128)(2,1)S(1)} %bitcast.19, s32[]{:T(128)S(6)} %select_n.13, s32[]{:T(128)S(6)} %select_n.14, ...), kind=kLoop, calls=%fused_computation.2 | loop fusion | bytes 2490384 | tf_op jit(solution)/shard_map/dynamic_slice | solution.py:124
  2.8 4.2 %collective-permute-start.2 = (bf16[11,2,16,512]{3,2,1,0:T(8,128)(2,1)S(1)}, bf16[11,2,16,512]{3,2,1,0:T(8,128)(2,1)S(1)}, u32[]{:S(2)}, u32[]{:S(2)}) collective-permute-start(bf16[11,2,16,512]{3,2,1,0:T(8,128)(2,1)S(1)} %get-tuple-element.5), channel_id=1, source_target_pairs={{0,3},{1,0},{2,1},{3,2},{4,7},{5,4},{6,5},{7,6},{8,11},{9,8},{10,9... | collective-permute-start | bytes 1081352 | tf_op jit(solution)/shard_map/ppermute | solution.py:126
  7.0 0.0 collective-permute-start
  7.0 0.5 collective-permute-start.1
  7.4 0.6 compare_select_fusion.refs_0_
  8.0 6.1 %collective-permute-done.2.refs_4_ = bf16[11,2,16,512]{3,2,1,0:T(8,128)(2,1)S(1)} collective-permute-done((bf16[11,2,16,512]{3,2,1,0:T(8,128)(2,1)S(1)}, bf16[11,2,16,512]{3,2,1,0:T(8,128)(2,1)S(1)}, u32[]{:S(2)}, u32[]{:S(2)}) %collective-permute-start.2) | collective-permute-done | bytes 360480 | tf_op jit(solution)/shard_map/ppermute | solution.py:126
  14.1 8.6 %collective-permute-done.refs_2_ = bf16[11,2,16,512]{3,2,1,0:T(8,128)(2,1)S(1)} collective-permute-done((bf16[11,2,16,512]{3,2,1,0:T(8,128)(2,1)S(1)}, bf16[11,2,16,512]{3,2,1,0:T(8,128)(2,1)S(1)}, u32[]{:S(2)}, u32[]{:S(2)}) %collective-permute-start) | collective-permute-done | bytes 360480 | tf_op jit(solution)/shard_map/ppermute | solution.py:126
  22.7 14.4 %collective-permute-done.1.refs_3_ = bf16[11,2,16,512]{3,2,1,0:T(8,128)(2,1)S(1)} collective-permute-done((bf16[11,2,16,512]{3,2,1,0:T(8,128)(2,1)S(1)}, bf16[11,2,16,512]{3,2,1,0:T(8,128)(2,1)S(1)}, u32[]{:S(2)}, u32[]{:S(2)}) %collective-permute-start.1) | collective-permute-done | bytes 360480 | tf_op jit(solution)/shard_map/ppermute | solution.py:126
  37.1 0.0 copy-done.2
  37.1 0.0 copy-done.3
  37.1 0.7 %copy-done.4 = bf16[11,2,16,512]{3,2,1,0:T(8,128)(2,1)} copy-done((bf16[11,2,16,512]{3,2,1,0:T(8,128)(2,1)}, bf16[11,2,16,512]{3,2,1,0:T(8,128)(2,1)S(1)}, u32[]{:S(2)}) %copy-start.4) | copy-done | bytes 360472
  37.8 3.4 %shard_map.37.own_ref = bf16[11,2,64,512]{3,2,1,0:T(8,128)(2,1)} custom-call(s32[4]{0:T(128)} %compare_select_fusion.refs_0_, bf16[11,2,16,512]{3,2,1,0:T(8,128)(2,1)} %get-tuple-element.8.refs_1_, bf16[11,2,16,512]{3,2,1,0:T(8,128)(2,1)} %copy-done.3, bf16[11,2,16,512]{3,2,1,0:T(8,128)(2,1)} %copy-done.4, bf16[11,2,16,512]{3,2,1,0:T(8,128)(2,1)} %copy-done.2), custom_call_target="tpu_custom_call" | custom-call | tf_op jit(solution)/shard_map/pallas_call | solution.py:134
  41.2 4.7 %collective-permute-start.3 = (bf16[11,2,64,512]{3,2,1,0:T(8,128)(2,1)}, bf16[11,2,64,512]{3,2,1,0:T(8,128)(2,1)S(1)}, u32[]{:S(2)}, u32[]{:S(2)}) collective-permute-start(bf16[11,2,64,512]{3,2,1,0:T(8,128)(2,1)} %shard_map.37.own_ref), channel_id=1, source_target_pairs={{0,4},{4,8},{8,12},{1,5},{5,9},{9,13},{2,6},{6,10},{10,14},{3,7},{... | collective-permute-start | bytes 4325384 | tf_op jit(solution)/shard_map/ppermute | solution.py:106
  45.9 2.1 %slice.4 = bf16[11,1,64,512]{3,2,1,0:T(8,128)(2,1)} slice(bf16[11,2,64,512]{3,2,1,0:T(8,128)(2,1)} %shard_map.37.own_ref), slice={[0:11], [0:1], [0:64], [0:512]} | slice | bytes 1441792 | tf_op jit(solution)/shard_map/slice | solution.py:142
  47.9 2.1 %collective-permute-start.4 = (bf16[11,1,64,512]{3,2,1,0:T(8,128)(2,1)}, bf16[11,1,64,512]{3,2,1,0:T(8,128)(2,1)S(1)}, u32[]{:S(2)}, u32[]{:S(2)}) collective-permute-start(bf16[11,1,64,512]{3,2,1,0:T(8,128)(2,1)} %slice.4), channel_id=1, source_target_pairs={{4,0},{8,4},{12,8},{5,1},{9,5},{13,9},{6,2},{10,6},{14,10},{7,3},{... | collective-permute-start | bytes 2162696 | tf_op jit(solution)/shard_map/ppermute | solution.py:106
  50.0 0.0 copy-done.5
  50.0 0.4 reshape.12
  50.5 0.4 copy.18
  50.9 0.2 rev.3
  51.1 0.7 pad_bitcast_fusion.1
  51.8 1.0 %pad_maximum_fusion = bf16[3,2,64,3,4,64]{5,4,3,2,1,0:T(4,128)(2,1)S(1)} fusion(bf16[3,1,64,3,4,64]{5,4,3,2,1,0:T(4,128)(2,1)S(1)} %get-tuple-element.10, bf16[3,1,64,3,4,64]{5,4,3,2,1,0:T(4,128)(2,1)S(1)} %get-tuple-element.9), kind=kLoop, calls=%fused_computation | loop fusion | flops 294912 | bytes 1179648 | tf_op jit(solution)/shard_map/stack | solution.py:96
  52.7 1.5 %reshape.13.first_ref = bf16[384,768]{1,0:T(8,128)(2,1)} reshape(bf16[3,2,64,3,4,64]{5,4,3,2,1,0:T(4,128)(2,1)S(1)} %pad_maximum_fusion) | data formatting | bytes 1179648 | tf_op jit(solution)/shard_map/reshape | solution.py:96
  54.2 1.9 %reshape.14 = bf16[3,3,3,128,64]{4,3,2,1,0:T(8,128)(2,1)S(1)} reshape(bf16[3,3,3,8192]{3,2,1,0:T(4,128)(2,1)} %param.5) | data formatting | bytes 884736 | tf_op jit(solution)/shard_map/reshape | solution.py:100
  56.1 0.3 copy.12
  56.5 1.0 %copy.13.second_ref = bf16[128,1728]{1,0:T(8,128)(2,1)} copy(bf16[128,1728]{0,1:T(8,128)(2,1)S(1)} %bitcast.22) | data formatting | bytes 884736 | tf_op jit(solution)/shard_map/reshape | solution.py:101
  57.5 0.7 pad_add_fusion.edge_ref
  58.1 2.6 %collective-permute-done.4.high_ref = bf16[11,1,64,512]{3,2,1,0:T(8,128)(2,1)S(1)} collective-permute-done((bf16[11,1,64,512]{3,2,1,0:T(8,128)(2,1)}, bf16[11,1,64,512]{3,2,1,0:T(8,128)(2,1)S(1)}, u32[]{:S(2)}, u32[]{:S(2)}) %collective-permute-start.4) | collective-permute-done | bytes 720928 | tf_op jit(solution)/shard_map/ppermute | solution.py:106
  60.7 1.4 %collective-permute-done.3.low_ref = bf16[11,2,64,512]{3,2,1,0:T(8,128)(2,1)S(1)} collective-permute-done((bf16[11,2,64,512]{3,2,1,0:T(8,128)(2,1)}, bf16[11,2,64,512]{3,2,1,0:T(8,128)(2,1)S(1)}, u32[]{:S(2)}, u32[]{:S(2)}) %collective-permute-start.3) | collective-permute-done | bytes 1441824 | tf_op jit(solution)/shard_map/ppermute | solution.py:106
  62.1 1.1 %copy-done = bf16[11,2,64,512]{3,2,1,0:T(8,128)(2,1)} copy-done((bf16[11,2,64,512]{3,2,1,0:T(8,128)(2,1)}, bf16[11,2,64,512]{3,2,1,0:T(8,128)(2,1)S(1)}, u32[]{:S(2)}) %copy-start) | copy-done | bytes 1441816
  63.2 8.1 %shard_map.38 = bf16[4,128,256]{2,1,0:T(8,128)(2,1)} custom-call(s32[2]{0:T(128)} %pad_add_fusion.edge_ref, bf16[11,2,64,512]{3,2,1,0:T(8,128)(2,1)} %copy-done, bf16[11,2,64,512]{3,2,1,0:T(8,128)(2,1)} %shard_map.37.own_ref, bf16[11,1,64,512]{3,2,1,0:T(8,128)(2,1)} %copy-done.1, bf16[384,768]{1,0:T(8,128)(2,1)} %reshape.13.first_ref, ...), custom_call_target="tpu_custom_call" | custom-call | tf_op jit(solution)/shard_map/pallas_call | solution.py:144
  71.3 1.9 %copy.14 = bf16[128,1,4,256]{3,2,1,0:T(4,128)(2,1)} copy(bf16[128,1,4,256]{3,0,2,1:T(8,128)(2,1)} %bitcast.23) | data formatting | bytes 524288 | tf_op jit(solution)/shard_map/broadcast_in_dim | solution.py:155
  (7 shorter events, 0.0 us)
Async XLA Ops:
  2.8 11.3 %collective-permute-start.2 = (bf16[11,2,16,512]{3,2,1,0:T(8,128)(2,1)S(1)}, bf16[11,2,16,512]{3,2,1,0:T(8,128)(2,1)S(1)}, u32[]{:S(2)}, u32[]{:S(2)}) collective-permute-start(bf16[11,2,16,512]{3,2,1,0:T(8,128)(2,1)S(1)} %get-tuple-element.5), channel_id=1, source_target_pairs={{0,3},{1,0},{2,1},{3,2},{4,7},{5,4},{6,5},{7,6},{8,11},{9,8},{10,9... | collective-permute-start | bytes 1081352 | tf_op jit(solution)/shard_map/ppermute | solution.py:126
  7.0 15.8 %collective-permute-start = (bf16[11,2,16,512]{3,2,1,0:T(8,128)(2,1)S(1)}, bf16[11,2,16,512]{3,2,1,0:T(8,128)(2,1)S(1)}, u32[]{:S(2)}, u32[]{:S(2)}) collective-permute-start(bf16[11,2,16,512]{3,2,1,0:T(8,128)(2,1)S(1)} %get-tuple-element.6), channel_id=1, source_target_pairs={{0,1},{1,2},{2,3},{3,0},{4,5},{5,6},{6,7},{7,4},{8,9},{9,10},{10,1... | collective-permute-start | bytes 1081352 | tf_op jit(solution)/shard_map/ppermute | solution.py:126
  7.0 30.1 %collective-permute-start.1 = (bf16[11,2,16,512]{3,2,1,0:T(8,128)(2,1)S(1)}, bf16[11,2,16,512]{3,2,1,0:T(8,128)(2,1)S(1)}, u32[]{:S(2)}, u32[]{:S(2)}) collective-permute-start(bf16[11,2,16,512]{3,2,1,0:T(8,128)(2,1)S(1)} %get-tuple-element.7), channel_id=1, source_target_pairs={{0,2},{1,3},{2,0},{3,1},{4,6},{5,7},{6,4},{7,5},{8,10},{9,11},{10,... | collective-permute-start | bytes 1081352 | tf_op jit(solution)/shard_map/ppermute | solution.py:126
  14.1 23.0 %copy-start.2 = (bf16[11,2,16,512]{3,2,1,0:T(8,128)(2,1)}, bf16[11,2,16,512]{3,2,1,0:T(8,128)(2,1)S(1)}, u32[]{:S(2)}) copy-start(bf16[11,2,16,512]{3,2,1,0:T(8,128)(2,1)S(1)} %collective-permute-done.2.refs_4_) | copy-start | bytes 1081348
  22.7 14.4 %copy-start.3 = (bf16[11,2,16,512]{3,2,1,0:T(8,128)(2,1)}, bf16[11,2,16,512]{3,2,1,0:T(8,128)(2,1)S(1)}, u32[]{:S(2)}) copy-start(bf16[11,2,16,512]{3,2,1,0:T(8,128)(2,1)S(1)} %collective-permute-done.refs_2_) | copy-start | bytes 1081348
  37.1 0.7 %copy-start.4 = (bf16[11,2,16,512]{3,2,1,0:T(8,128)(2,1)}, bf16[11,2,16,512]{3,2,1,0:T(8,128)(2,1)S(1)}, u32[]{:S(2)}) copy-start(bf16[11,2,16,512]{3,2,1,0:T(8,128)(2,1)S(1)} %collective-permute-done.1.refs_3_) | copy-start | bytes 1081348
  41.2 8.8 %copy-start.5 = (bf16[3,3,3,4096]{3,2,1,0:T(4,128)(2,1)S(1)}, bf16[3,3,3,4096]{3,2,1,0:T(4,128)(2,1)}, u32[]{:S(2)}) copy-start(bf16[3,3,3,4096]{3,2,1,0:T(4,128)(2,1)} %param.4) | copy-start | bytes 663556
  41.2 20.9 %collective-permute-start.3 = (bf16[11,2,64,512]{3,2,1,0:T(8,128)(2,1)}, bf16[11,2,64,512]{3,2,1,0:T(8,128)(2,1)S(1)}, u32[]{:S(2)}, u32[]{:S(2)}) collective-permute-start(bf16[11,2,64,512]{3,2,1,0:T(8,128)(2,1)} %shard_map.37.own_ref), channel_id=1, source_target_pairs={{0,4},{4,8},{8,12},{1,5},{5,9},{9,13},{2,6},{6,10},{10,14},{3,7},{... | collective-permute-start | bytes 4325384 | tf_op jit(solution)/shard_map/ppermute | solution.py:106
  47.9 12.8 %collective-permute-start.4 = (bf16[11,1,64,512]{3,2,1,0:T(8,128)(2,1)}, bf16[11,1,64,512]{3,2,1,0:T(8,128)(2,1)S(1)}, u32[]{:S(2)}, u32[]{:S(2)}) collective-permute-start(bf16[11,1,64,512]{3,2,1,0:T(8,128)(2,1)} %slice.4), channel_id=1, source_target_pairs={{4,0},{8,4},{12,8},{5,1},{9,5},{13,9},{6,2},{10,6},{14,10},{7,3},{... | collective-permute-start | bytes 2162696 | tf_op jit(solution)/shard_map/ppermute | solution.py:106
  60.7 1.4 %copy-start.1 = (bf16[11,1,64,512]{3,2,1,0:T(8,128)(2,1)}, bf16[11,1,64,512]{3,2,1,0:T(8,128)(2,1)S(1)}, u32[]{:S(2)}) copy-start(bf16[11,1,64,512]{3,2,1,0:T(8,128)(2,1)S(1)} %collective-permute-done.4.high_ref) | copy-start | bytes 2162692
  62.1 1.1 %copy-start = (bf16[11,2,64,512]{3,2,1,0:T(8,128)(2,1)}, bf16[11,2,64,512]{3,2,1,0:T(8,128)(2,1)S(1)}, u32[]{:S(2)}) copy-start(bf16[11,2,64,512]{3,2,1,0:T(8,128)(2,1)S(1)} %collective-permute-done.3.low_ref) | copy-start | bytes 4325380

commit v2 on v1

--- a/solution.py
+++ b/solution.py
@@ -34,30 +34,30 @@
         )
 
 
-def conv_kernel(edge_ref, low_ref, own_ref, high_ref, first_ref, second_ref, out_ref, taps_ref, hid_ref):
-    rows = own_ref.shape[0]
-    half = own_ref.shape[3] // 2
-    hid_rows = rows - 2
+def conv_kernel(rows, *refs):
+    edge_ref, first_ref, second_ref = refs[:3]
+    blocks, (out_ref, taps_ref, hid_ref) = refs[3:-3], refs[-3:]
+    half = out_ref.shape[2]
     lane = lax.broadcasted_iota(jnp.int32, (C, half), 1)
-    for r in range(rows):
+    for r, (chunk, at) in enumerate(rows):
+        low_ref, own_ref, high_ref = blocks[3 * chunk : 3 * chunk + 3]
         for p in range(5):
             if p < 2:
-                cell = low_ref[r, p]
+                cell = low_ref[at, p]
             elif p < 4:
-                cell = own_ref[r, p - 2]
+                cell = own_ref[at, p - 2]
             else:
-                cell = high_ref[r, 0]
+                cell = high_ref[at, 0]
             even, odd = cell[:, :half], cell[:, half:]
-            zero = jnp.zeros((C, half), jnp.float32)
-            before = jnp.where(lane == 0, zero, pltpu.roll(odd.astype(jnp.float32), 1, 1))
-            after = jnp.where(lane == half - 1, zero, pltpu.roll(even.astype(jnp.float32), half - 1, 1))
+            before = jnp.where(lane == 0, 0.0, pltpu.roll(odd.astype(jnp.float32), 1, 1))
+            after = jnp.where(lane == half - 1, 0.0, pltpu.roll(even.astype(jnp.float32), half - 1, 1))
             base = r * 4 * C
             taps_ref[p, pl.ds(base, C), :] = before.astype(jnp.bfloat16)
             taps_ref[p, pl.ds(base + C, C), :] = even
             taps_ref[p, pl.ds(base + 2 * C, C), :] = odd
             taps_ref[p, pl.ds(base + 3 * C, C), :] = after.astype(jnp.bfloat16)
     size = 2 * C
-    for y in range(hid_rows):
+    for y in range(len(rows) - 2):
         total = [None] * 3
         for p in range(5):
             z_low, z_high = max(0, p - 2), min(2, p)
@@ -77,8 +77,7 @@
             if y == 0:
                 value = jnp.where(edge_ref[1] > 0, value, 0.0)
             value = value.astype(jnp.bfloat16)
-            odd = value[C:]
-            before = jnp.where(lane == 0, 0.0, pltpu.roll(odd.astype(jnp.float32), 1, 1))
+            before = jnp.where(lane == 0, 0.0, pltpu.roll(value[C:].astype(jnp.float32), 1, 1))
             base = (y * 3 + z) * 3 * C
             hid_ref[pl.ds(base, C), :] = before.astype(jnp.bfloat16)
             hid_ref[pl.ds(base + C, 2 * C), :] = value
@@ -106,52 +105,88 @@
     return lax.ppermute(block, axis, [(i, i + by) for i in range(count) if 0 <= i + by < count])
 
 
+def after(value, *others):
+    return lax.optimization_barrier((value, *others))[0]
+
+
+def chunks_of(band):
+    window = band + 3
+    if band < 8:
+        return [(0, window)]
+    return [(0, 5), (5, window - 2), (window - 2, window)]
+
+
 def local(volume, conv_weight, down_weight):
     bands = lax.axis_size("filt")
     me = lax.axis_index("filt")
     count, planes, all_rows, width = volume.shape
     band = all_rows // bands
-    window = band + 3
+    chunks = chunks_of(band)
     field = jnp.transpose(volume, (2, 1, 0, 3))
     field = jnp.pad(field, ((2, 1), (0, 0), (0, 0), (0, 0)))
     vmem = pl.BlockSpec(memory_space=pltpu.VMEM)
     smem = pl.BlockSpec(memory_space=pltpu.SMEM)
     params = pltpu.CompilerParams(vmem_limit_bytes=VMEM_LIMIT)
+    first, second = first_weights(conv_weight), second_weights(down_weight)
+    space = lax.axis_index("space")
+
+    travelled = []
+    for low, high in chunks:
+        pieces = []
+        if count % 16 == 0:
+            for d in range(bands):
+                target = lax.rem(me + d, bands)
+                piece = lax.dynamic_slice_in_dim(field, target * band + low, high - low, 0)
+                if d:
+                    if travelled:
+                        piece = after(piece, travelled[-1][d])
+                    piece = lax.ppermute(piece, "filt", [(i, (i + d) % bands) for i in range(bands)])
+                pieces.append(piece)
+        else:
+            sent = jnp.stack([field[t * band + low : t * band + high] for t in range(bands)])
+            got = lax.all_to_all(sent, "filt", split_axis=0, concat_axis=0, tiled=True)
+            pieces.append(jnp.transpose(got, (1, 2, 0, 3, 4)).reshape(high - low, planes, C, width))
+        travelled.append(pieces)
+
     if count % 16 == 0:
-        pieces = []
-        for d in range(bands):
-            target = lax.rem(me + d, bands)
-            piece = lax.dynamic_slice_in_dim(field, target * band, window, 0)
-            if d:
-                piece = lax.ppermute(piece, "filt", [(i, (i + d) % bands) for i in range(bands)])
-            pieces.append(piece)
         order = lax.rem(me - jnp.arange(bands, dtype=jnp.int32) + bands, bands)
     else:
-        sent = jnp.stack([field[t * band : t * band + window] for t in range(bands)])
-        got = lax.all_to_all(sent, "filt", split_axis=0, concat_axis=0, tiled=True)
-        pieces = [jnp.transpose(got, (1, 2, 0, 3, 4)).reshape(window, planes, C, width)]
         order = jnp.zeros((1,), jnp.int32)
-    own = pl.pallas_call(
-        gather_kernel,
-        out_shape=jax.ShapeDtypeStruct((window, planes, C, width), jnp.bfloat16),
-        in_specs=[smem] + [vmem] * len(pieces),
-        out_specs=vmem,
-        compiler_params=params,
-    )(order, *pieces)
-    low = shifted(own, "space", 1)
-    high = shifted(own[:, :1], "space", -1)
-    edge = jnp.stack([lax.axis_index("space"), me]).astype(jnp.int32)
-    coarse = pl.pallas_call(
-        conv_kernel,
-        out_shape=jax.ShapeDtypeStruct((band // 2, C2, width // 2), jnp.bfloat16),
-        in_specs=[smem] + [vmem] * 5,
-        out_specs=vmem,
-        scratch_shapes=[
-            pltpu.VMEM((5, window * 4 * C, width // 2), jnp.bfloat16),
-            pltpu.VMEM(((band + 1) * 9 * C, width // 2), jnp.bfloat16),
-        ],
-        compiler_params=params,
-    )(edge, low, own, high, first_weights(conv_weight), second_weights(down_weight))
+    order, first, second = lax.optimization_barrier((order, first, second))
+
+    blocks, outs, done_rows = [], [], 0
+    for (low, high), pieces in zip(chunks, travelled):
+        own = pl.pallas_call(
+            gather_kernel,
+            out_shape=jax.ShapeDtypeStruct((high - low, planes, C, width), jnp.bfloat16),
+            in_specs=[smem] + [vmem] * len(pieces),
+            out_specs=vmem,
+            compiler_params=params,
+        )(order, *pieces)
+        blocks.append((low, high, (shifted(own, "space", 1), own, shifted(own[:, :1], "space", -1))))
+        last = (high - 3) // 2
+        used = [block for block in blocks if block[1] > 2 * done_rows]
+        rows = []
+        for r in range(2 * done_rows, 2 * last + 3):
+            rows += [(i, r - block[0]) for i, block in enumerate(used) if block[0] <= r < block[1]]
+        top = (me > 0).astype(jnp.int32) if done_rows == 0 else jnp.ones((), jnp.int32)
+        edge = jnp.stack([space.astype(jnp.int32), top])
+        operands = [array for block in used for array in block[2]]
+        outs.append(
+            pl.pallas_call(
+                functools.partial(conv_kernel, rows),
+                out_shape=jax.ShapeDtypeStruct((last - done_rows, C2, width // 2), jnp.bfloat16),
+                in_specs=[smem] + [vmem] * (2 + len(operands)),
+                out_specs=vmem,
+                scratch_shapes=[
+                    pltpu.VMEM((5, len(rows) * 4 * C, width // 2), jnp.bfloat16),
+                    pltpu.VMEM(((len(rows) - 2) * 9 * C, width // 2), jnp.bfloat16),
+                ],
+                compiler_params=params,
+            )(edge, first, second, *operands)
+        )
+        done_rows = last
+    coarse = jnp.concatenate(outs)
     return jnp.transpose(coarse, (1, 0, 2))[:, None]
 
 

time: 73.5 us -> 87.4 us (1.19)
  starting transfers between devices: 11.4 us -> 35.2 us
  waiting for transfers between devices: 33.1 us -> 9.89 us
  Pallas kernels: 11.4 us -> 21.5 us
  local copies, waits for them, and re-layouts: 14.9 us -> 17 us
    ppermute x3 -> x9, waiting for transfers between devices: 29.1 us -> 9.88 us  [local(): lax.ppermute(piece, 'filt', [(i, (i + d) % bands) for i in range(bands)])]
    ppermute x3 -> x9, starting transfers between devices: 4.6 us -> 16.8 us  [local(): lax.ppermute(piece, 'filt', [(i, (i + d) % bands) for i in range(bands)])]
    ppermute x2 -> x6, starting transfers between devices: 6.76 us -> 18.4 us  [shifted(): lax.ppermute(block, axis, [(i, i + by) for i in range(count) if 0 <= i +...]
    pallas_call x2 -> x6, Pallas kernels: 11.4 us -> 21.5 us  [the longest x3 14.4 us: local(): pl.pallas_call(functools.partial(conv_kernel, rows), out_shape=jax.ShapeD...]
    ppermute x2 -> x6, waiting for transfers between devices: 3.99 us -> 0.02 us  [shifted(): lax.ppermute(block, axis, [(i, i + by) for i in range(count) if 0 <= i +...]
    unnamed x13 -> x45, local copies, waits for them, and re-layouts: 3.65 us -> 6.86 us
    dynamic_slice x1 -> x3, local copies, waits for them, and re-layouts: 0.97 us -> 2.27 us  [local(): piece = lax.dynamic_slice_in_dim(field, target * band + low, high - low, 0)]
    reshape x1, local copies, waits for them, and re-layouts: 1.87 us -> 0.71 us  [second_weights(): shaped = down_weight.reshape(3, 3, 3, C2, C)]
  transfers between devices with their start and end apart: 5 -> 15, of which waited for: 5 -> 4; matrix products, arithmetic and copies ran while one was open for 15% -> 12% of each run, Pallas kernels for 0% -> 20%
where the time goes in v2:
time: 87.4 us; the launch traced here: 86.9 us
  starting transfers between devices  35.2 us (40%)
  Pallas kernels  21.5 us (25%)
  local copies, waits for them, and re-layouts  17 us (19%)
  waiting for transfers between devices  9.89 us (11%)
  other arithmetic  3.01 us (3%)
    ppermute x6, starting transfers between devices, shifted(): lax.ppermute(block, axis, [(i, i + by) for i in range(count) if 0 <= i +...  18.4 us
    ppermute x9, starting transfers between devices, local(): lax.ppermute(piece, 'filt', [(i, (i + d) % bands) for i in range(bands)])  16.8 us
    pallas_call x3, Pallas kernels, local(): pl.pallas_call(functools.partial(conv_kernel, rows), out_shape=jax.ShapeD...  14.4 us
    ppermute x9, waiting for transfers between devices, local(): lax.ppermute(piece, 'filt', [(i, (i + d) % bands) for i in range(bands)])  9.88 us
    pallas_call x3, Pallas kernels, local(): pl.pallas_call(gather_kernel, out_shape=jax.ShapeDtypeStruct((high - low,...  7.05 us
    unnamed x45, local copies, waits for them, and re-layouts  6.86 us
    dynamic_slice x3, local copies, waits for them, and re-layouts, local(): piece = lax.dynamic_slice_in_dim(field, target * band + low, high - low, 0)  2.27 us
  transfers between devices with their start and end apart: 15, of which 4 were waited for; matrix products, arithmetic and copies ran while one was open for 12% of the time, Pallas kernels for 20%

profile of v2, /device:TPU:1, one launch (start us, length us, event | category | flops | bytes accessed | tf_op | source)
XLA Modules:
  0.0 86.9 jit_solution(4615695367760863312)
XLA Ops:
  0.0 1.8 %copy.19 = bf16[16,2,32,512]{3,0,1,2:T(8,128)(2,1)S(1)} copy(bf16[16,2,32,512]{3,2,1,0:T(8,128)(2,1)} %param.3) | data formatting | bytes 2097152 | tf_op args[0]
  1.8 0.8 pad_dynamic-slice_fusion.11
  2.7 2.1 %collective-permute-start = (bf16[5,2,16,512]{3,2,1,0:T(8,128)(2,1)}, bf16[5,2,16,512]{3,2,1,0:T(8,128)(2,1)S(1)}, u32[]{:S(2)}, u32[]{:S(2)}) collective-permute-start(bf16[5,2,16,512]{3,2,1,0:T(8,128)(2,1)} %get-tuple-element.24), channel_id=1, source_target_pairs={{0,1},{1,2},{2,3},{3,0},{4,5},{5,6},{6,7},{7,4},{8,9},{9,10},{10,1... | collective-permute-start | bytes 491528 | tf_op jit(solution)/shard_map/ppermute | solution.py:143
  4.8 2.3 %collective-permute-start.1 = (bf16[5,2,16,512]{3,2,1,0:T(8,128)(2,1)}, bf16[5,2,16,512]{3,2,1,0:T(8,128)(2,1)S(1)}, u32[]{:S(2)}, u32[]{:S(2)}) collective-permute-start(bf16[5,2,16,512]{3,2,1,0:T(8,128)(2,1)} %get-tuple-element.25), channel_id=1, source_target_pairs={{0,2},{1,3},{2,0},{3,1},{4,6},{5,7},{6,4},{7,5},{8,10},{9,11},{10,... | collective-permute-start | bytes 491528 | tf_op jit(solution)/shard_map/ppermute | solution.py:143
  7.1 1.1 %collective-permute-start.2 = (bf16[5,2,16,512]{3,2,1,0:T(8,128)(2,1)S(1)}, bf16[5,2,16,512]{3,2,1,0:T(8,128)(2,1)S(1)}, u32[]{:S(2)}, u32[]{:S(2)}) collective-permute-start(bf16[5,2,16,512]{3,2,1,0:T(8,128)(2,1)S(1)} %get-tuple-element.26), channel_id=1, source_target_pairs={{0,3},{1,0},{2,1},{3,2},{4,7},{5,4},{6,5},{7,6},{8,11},{9,8},{10,9... | collective-permute-start | bytes 491528 | tf_op jit(solution)/shard_map/ppermute | solution.py:143
  9.9 1.0 %pad_maximum_fusion = bf16[3,2,64,3,4,64]{5,4,3,2,1,0:T(4,128)(2,1)S(1)} fusion(bf16[3,1,64,3,4,64]{5,4,3,2,1,0:T(4,128)(2,1)S(1)} %get-tuple-element.36, bf16[3,1,64,3,4,64]{5,4,3,2,1,0:T(4,128)(2,1)S(1)} %get-tuple-element.35), kind=kLoop, calls=%fused_computation | loop fusion | flops 294912 | bytes 1179648 | tf_op jit(solution)/shard_map/stack | solution.py:95
  11.5 1.5 %reshape.13.refs_1_ = bf16[384,768]{1,0:T(8,128)(2,1)} reshape(bf16[3,2,64,3,4,64]{5,4,3,2,1,0:T(4,128)(2,1)S(1)} %pad_maximum_fusion) | data formatting | bytes 1179648 | tf_op jit(solution)/shard_map/reshape | solution.py:95
  13.7 1.1 %copy.11 = bf16[128,3,3,3,64]{0,4,3,2,1:T(8,128)(2,1)} copy(bf16[128,3,3,3,64]{4,0,3,1,2:T(8,128)(2,1)S(1)} %bitcast.23) | data formatting | bytes 884736 | tf_op jit(solution)/shard_map/transpose | solution.py:100
  15.9 2.8 %collective-permute-done.1.refs_3_ = bf16[5,2,16,512]{3,2,1,0:T(8,128)(2,1)S(1)} collective-permute-done((bf16[5,2,16,512]{3,2,1,0:T(8,128)(2,1)}, bf16[5,2,16,512]{3,2,1,0:T(8,128)(2,1)S(1)}, u32[]{:S(2)}, u32[]{:S(2)}) %collective-permute-start.1) | collective-permute-done | bytes 163872 | tf_op jit(solution)/shard_map/ppermute | solution.py:143
  19.4 2.5 %shard_map.37.refs_4_ = bf16[5,2,64,512]{3,2,1,0:T(8,128)(2,1)} custom-call(s32[4]{0:T(128)} %compare_select_fusion.refs_0_, bf16[5,2,16,512]{3,2,1,0:T(8,128)(2,1)} %get-tuple-element.23.refs_1_, bf16[5,2,16,512]{3,2,1,0:T(8,128)(2,1)} %copy-done.12, bf16[5,2,16,512]{3,2,1,0:T(8,128)(2,1)} %copy-done.13, bf16[5,2,16,512]{3,2,1,0:T(8,128)(2,1)} %copy-done.14), custom_call_target="tpu_custom_call" | custom-call | tf_op jit(solution)/shard_map/pallas_call | solution.py:159
  22.0 5.5 %collective-permute-start.3 = (bf16[5,2,64,512]{3,2,1,0:T(8,128)(2,1)}, bf16[5,2,64,512]{3,2,1,0:T(8,128)(2,1)S(1)}, u32[]{:S(2)}, u32[]{:S(2)}) collective-permute-start(bf16[5,2,64,512]{3,2,1,0:T(8,128)(2,1)} %shard_map.37.refs_4_), channel_id=1, source_target_pairs={{0,4},{4,8},{8,12},{1,5},{5,9},{9,13},{2,6},{6,10},{10,14},{3,7},{... | collective-permute-start | bytes 1966088 | tf_op jit(solution)/shard_map/ppermute | solution.py:105
  27.5 7.0 %collective-permute-start.7 = (bf16[4,2,16,512]{3,2,1,0:T(8,128)(2,1)S(1)}, bf16[4,2,16,512]{3,2,1,0:T(8,128)(2,1)S(1)}, u32[]{:S(2)}, u32[]{:S(2)}) collective-permute-start(bf16[4,2,16,512]{3,2,1,0:T(8,128)(2,1)S(1)} %get-tuple-element.19), channel_id=1, source_target_pairs={{0,3},{1,0},{2,1},{3,2},{4,7},{5,4},{6,5},{7,6},{8,11},{9,8},{10,9... | collective-permute-start | bytes 393224 | tf_op jit(solution)/shard_map/ppermute | solution.py:143
  34.5 2.8 %collective-permute-done.7.refs_4_ = bf16[4,2,16,512]{3,2,1,0:T(8,128)(2,1)S(1)} collective-permute-done((bf16[4,2,16,512]{3,2,1,0:T(8,128)(2,1)S(1)}, bf16[4,2,16,512]{3,2,1,0:T(8,128)(2,1)S(1)}, u32[]{:S(2)}, u32[]{:S(2)}) %collective-permute-start.7) | collective-permute-done | bytes 131104 | tf_op jit(solution)/shard_map/ppermute | solution.py:143
  38.0 2.4 %shard_map.39.refs_7_.refs_4_ = bf16[4,2,64,512]{3,2,1,0:T(8,128)(2,1)} custom-call(s32[4]{0:T(128)} %compare_select_fusion.refs_0_, bf16[4,2,16,512]{3,2,1,0:T(8,128)(2,1)} %get-tuple-element.32.refs_1_, bf16[4,2,16,512]{3,2,1,0:T(8,128)(2,1)} %copy-done.16, bf16[4,2,16,512]{3,2,1,0:T(8,128)(2,1)} %copy-done.17, bf16[4,2,16,512]{3,2,1,0:T(8,128)(2,1)} %copy-done.18), custom_call_target="tpu_custom_call" | custom-call | tf_op jit(solution)/shard_map/pallas_call | solution.py:159
  40.4 2.9 %collective-permute-start.8 = (bf16[4,2,64,512]{3,2,1,0:T(8,128)(2,1)}, bf16[4,2,64,512]{3,2,1,0:T(8,128)(2,1)S(1)}, u32[]{:S(2)}, u32[]{:S(2)}) collective-permute-start(bf16[4,2,64,512]{3,2,1,0:T(8,128)(2,1)} %shard_map.39.refs_7_.refs_4_), channel_id=1, source_target_pairs={{0,4},{4,8},{8,12},{1,5},{5,9},{9,13},{2,6},{6,10},{10,14},{3,7},{... | collective-permute-start | bytes 1572872 | tf_op jit(solution)/shard_map/ppermute | solution.py:105
  43.4 2.1 %collective-permute-start.4 = (bf16[5,1,64,512]{3,2,1,0:T(8,128)(2,1)S(1)}, bf16[5,1,64,512]{3,2,1,0:T(8,128)(2,1)S(1)}, u32[]{:S(2)}, u32[]{:S(2)}) collective-permute-start(bf16[5,1,64,512]{3,2,1,0:T(8,128)(2,1)S(1)} %slice.12), channel_id=1, source_target_pairs={{4,0},{8,4},{12,8},{5,1},{9,5},{13,9},{6,2},{10,6},{14,10},{7,3},{... | collective-permute-start | bytes 983048 | tf_op jit(solution)/shard_map/ppermute | solution.py:105
  46.2 1.7 %collective-permute-start.10 = (bf16[2,2,16,512]{3,2,1,0:T(8,128)(2,1)S(1)}, bf16[2,2,16,512]{3,2,1,0:T(8,128)(2,1)S(1)}, u32[]{:S(2)}, u32[]{:S(2)}) collective-permute-start(bf16[2,2,16,512]{3,2,1,0:T(8,128)(2,1)S(1)} %get-tuple-element.20), channel_id=1, source_target_pairs={{0,1},{1,2},{2,3},{3,0},{4,5},{5,6},{6,7},{7,4},{8,9},{9,10},{10,1... | collective-permute-start | bytes 196616 | tf_op jit(solution)/shard_map/ppermute | solution.py:143
  47.9 1.6 %collective-permute-start.11 = (bf16[2,2,16,512]{3,2,1,0:T(8,128)(2,1)S(1)}, bf16[2,2,16,512]{3,2,1,0:T(8,128)(2,1)S(1)}, u32[]{:S(2)}, u32[]{:S(2)}) collective-permute-start(bf16[2,2,16,512]{3,2,1,0:T(8,128)(2,1)S(1)} %get-tuple-element.21), channel_id=1, source_target_pairs={{0,2},{1,3},{2,0},{3,1},{4,6},{5,7},{6,4},{7,5},{8,10},{9,11},{10,... | collective-permute-start | bytes 196616 | tf_op jit(solution)/shard_map/ppermute | solution.py:143
  49.5 2.3 %collective-permute-done.10.refs_2_ = bf16[2,2,16,512]{3,2,1,0:T(8,128)(2,1)S(1)} collective-permute-done((bf16[2,2,16,512]{3,2,1,0:T(8,128)(2,1)S(1)}, bf16[2,2,16,512]{3,2,1,0:T(8,128)(2,1)S(1)}, u32[]{:S(2)}, u32[]{:S(2)}) %collective-permute-start.10) | collective-permute-done | bytes 65568 | tf_op jit(solution)/shard_map/ppermute | solution.py:143
  52.4 1.9 %collective-permute-done.11.refs_3_ = bf16[2,2,16,512]{3,2,1,0:T(8,128)(2,1)S(1)} collective-permute-done((bf16[2,2,16,512]{3,2,1,0:T(8,128)(2,1)S(1)}, bf16[2,2,16,512]{3,2,1,0:T(8,128)(2,1)S(1)}, u32[]{:S(2)}, u32[]{:S(2)}) %collective-permute-start.11) | collective-permute-done | bytes 65568 | tf_op jit(solution)/shard_map/ppermute | solution.py:143
  54.3 2.3 %collective-permute-start.9 = (bf16[4,1,64,512]{3,2,1,0:T(8,128)(2,1)S(1)}, bf16[4,1,64,512]{3,2,1,0:T(8,128)(2,1)S(1)}, u32[]{:S(2)}, u32[]{:S(2)}) collective-permute-start(bf16[4,1,64,512]{3,2,1,0:T(8,128)(2,1)S(1)} %slice.13), channel_id=1, source_target_pairs={{4,0},{8,4},{12,8},{5,1},{9,5},{13,9},{6,2},{10,6},{14,10},{7,3},{... | collective-permute-start | bytes 786440 | tf_op jit(solution)/shard_map/ppermute | solution.py:105
  57.3 2.1 %shard_map.41.refs_7_ = bf16[2,2,64,512]{3,2,1,0:T(8,128)(2,1)} custom-call(s32[4]{0:T(128)} %compare_select_fusion.refs_0_, bf16[2,2,16,512]{3,2,1,0:T(8,128)(2,1)} %get-tuple-element.28.refs_1_, bf16[2,2,16,512]{3,2,1,0:T(8,128)(2,1)} %copy-done.19, bf16[2,2,16,512]{3,2,1,0:T(8,128)(2,1)} %copy-done.20, bf16[2,2,16,512]{3,2,1,0:T(8,128)(2,1)} %copy-done.21), custom_call_target="tpu_custom_call" | custom-call | tf_op jit(solution)/shard_map/pallas_call | solution.py:159
  59.4 3.5 %collective-permute-start.13 = (bf16[2,2,64,512]{3,2,1,0:T(8,128)(2,1)}, bf16[2,2,64,512]{3,2,1,0:T(8,128)(2,1)S(1)}, u32[]{:S(2)}, u32[]{:S(2)}) collective-permute-start(bf16[2,2,64,512]{3,2,1,0:T(8,128)(2,1)} %shard_map.41.refs_7_), channel_id=1, source_target_pairs={{0,4},{4,8},{8,12},{1,5},{5,9},{9,13},{2,6},{6,10},{10,14},{3,7},{... | collective-permute-start | bytes 786440 | tf_op jit(solution)/shard_map/ppermute | solution.py:105
  62.9 0.9 %slice.14 = bf16[2,1,64,512]{3,2,1,0:T(8,128)(2,1)S(1)} slice(bf16[2,2,64,512]{3,2,1,0:T(8,128)(2,1)} %shard_map.41.refs_7_), slice={[0:2], [0:1], [0:64], [0:512]} | slice | bytes 262144 | tf_op jit(solution)/shard_map/slice | solution.py:166
  63.9 2.1 %collective-permute-start.14 = (bf16[2,1,64,512]{3,2,1,0:T(8,128)(2,1)S(1)}, bf16[2,1,64,512]{3,2,1,0:T(8,128)(2,1)S(1)}, u32[]{:S(2)}, u32[]{:S(2)}) collective-permute-start(bf16[2,1,64,512]{3,2,1,0:T(8,128)(2,1)S(1)} %slice.14), channel_id=1, source_target_pairs={{4,0},{8,4},{12,8},{5,1},{9,5},{13,9},{6,2},{10,6},{14,10},{7,3},{... | collective-permute-start | bytes 393224 | tf_op jit(solution)/shard_map/ppermute | solution.py:105
  66.0 1.0 %copy.13.refs_2_ = bf16[128,1728]{1,0:T(8,128)(2,1)} copy(bf16[128,1728]{0,1:T(8,128)(2,1)S(1)} %bitcast.25) | data formatting | bytes 884736 | tf_op jit(solution)/shard_map/optimization_barrier | solution.py:155
  67.6 0.9 copy-done.2
  68.4 4.3 %shard_map.38 = bf16[1,128,256]{2,1,0:T(8,128)(2,1)} custom-call(s32[2]{0:T(128)} %get-tuple-element.37.refs_0_, bf16[384,768]{1,0:T(8,128)(2,1)} %reshape.13.refs_1_, bf16[128,1728]{1,0:T(8,128)(2,1)} %copy.13.refs_2_, bf16[5,2,64,512]{3,2,1,0:T(8,128)(2,1)} %copy-done.2, bf16[5,2,64,512]{3,2,1,0:T(8,128)(2,1)} %shard_map.37.refs_4_, ...), custom_call_target="tpu_custom_call" | custom-call | tf_op jit(solution)/shard_map/pallas_call | solution.py:176
  73.6 5.8 %shard_map.40 = bf16[2,128,256]{2,1,0:T(8,128)(2,1)} custom-call(s32[2]{0:T(128)} %get-tuple-element.38.refs_0_, bf16[384,768]{1,0:T(8,128)(2,1)} %reshape.13.refs_1_, bf16[128,1728]{1,0:T(8,128)(2,1)} %copy.13.refs_2_, bf16[5,2,64,512]{3,2,1,0:T(8,128)(2,1)} %copy-done.2, bf16[5,2,64,512]{3,2,1,0:T(8,128)(2,1)} %shard_map.37.refs_4_, ...), custom_call_target="tpu_custom_call" | custom-call | tf_op jit(solution)/shard_map/pallas_call | solution.py:176
  80.7 4.4 %shard_map.42 = bf16[1,128,256]{2,1,0:T(8,128)(2,1)} custom-call(s32[2]{0:T(128)} %get-tuple-element.38.refs_0_, bf16[384,768]{1,0:T(8,128)(2,1)} %reshape.13.refs_1_, bf16[128,1728]{1,0:T(8,128)(2,1)} %copy.13.refs_2_, bf16[4,2,64,512]{3,2,1,0:T(8,128)(2,1)} %copy-done.3, bf16[4,2,64,512]{3,2,1,0:T(8,128)(2,1)} %shard_map.39.refs_7_.refs_4_, ...), custom_call_target="tpu_custom_call" | custom-call | tf_op jit(solution)/shard_map/pallas_call | solution.py:176
  85.1 0.9 %maximum_bitcast_fusion = bf16[128,1,4,256]{3,0,2,1:T(8,128)(2,1)S(1)} fusion(bf16[1,128,256]{2,1,0:T(8,128)(2,1)} %shard_map.42, bf16[2,128,256]{2,1,0:T(8,128)(2,1)S(1)} %copy-done.8, bf16[1,128,256]{2,1,0:T(8,128)(2,1)S(1)} %copy-done.11), kind=kLoop, calls=%fused_computation.5 | loop fusion | flops 262144 | bytes 524288 | tf_op jit(solution)/shard_map/broadcast_in_dim | solution.py:190
  86.0 0.9 %copy.16 = bf16[128,1,4,256]{3,2,1,0:T(4,128)(2,1)} copy(bf16[128,1,4,256]{3,0,2,1:T(8,128)(2,1)S(1)} %maximum_bitcast_fusion) | data formatting | bytes 524288 | tf_op jit(solution)/shard_map/broadcast_in_dim | solution.py:190
  (68 shorter events, 10.3 us)
Async XLA Ops:
  1.8 6.4 %copy-start.9 = (bf16[3,3,3,4096]{3,2,1,0:T(4,128)(2,1)S(1)}, bf16[3,3,3,4096]{3,2,1,0:T(4,128)(2,1)}, u32[]{:S(2)}) copy-start(bf16[3,3,3,4096]{3,2,1,0:T(4,128)(2,1)} %param.4) | copy-start | bytes 663556
  2.7 12.9 %collective-permute-start = (bf16[5,2,16,512]{3,2,1,0:T(8,128)(2,1)}, bf16[5,2,16,512]{3,2,1,0:T(8,128)(2,1)S(1)}, u32[]{:S(2)}, u32[]{:S(2)}) collective-permute-start(bf16[5,2,16,512]{3,2,1,0:T(8,128)(2,1)} %get-tuple-element.24), channel_id=1, source_target_pairs={{0,1},{1,2},{2,3},{3,0},{4,5},{5,6},{6,7},{7,4},{8,9},{9,10},{10,1... | collective-permute-start | bytes 491528 | tf_op jit(solution)/shard_map/ppermute | solution.py:143
  4.8 13.9 %collective-permute-start.1 = (bf16[5,2,16,512]{3,2,1,0:T(8,128)(2,1)}, bf16[5,2,16,512]{3,2,1,0:T(8,128)(2,1)S(1)}, u32[]{:S(2)}, u32[]{:S(2)}) collective-permute-start(bf16[5,2,16,512]{3,2,1,0:T(8,128)(2,1)} %get-tuple-element.25), channel_id=1, source_target_pairs={{0,2},{1,3},{2,0},{3,1},{4,6},{5,7},{6,4},{7,5},{8,10},{9,11},{10,... | collective-permute-start | bytes 491528 | tf_op jit(solution)/shard_map/ppermute | solution.py:143
  7.1 11.6 %collective-permute-start.2 = (bf16[5,2,16,512]{3,2,1,0:T(8,128)(2,1)S(1)}, bf16[5,2,16,512]{3,2,1,0:T(8,128)(2,1)S(1)}, u32[]{:S(2)}, u32[]{:S(2)}) collective-permute-start(bf16[5,2,16,512]{3,2,1,0:T(8,128)(2,1)S(1)} %get-tuple-element.26), channel_id=1, source_target_pairs={{0,3},{1,0},{2,1},{3,2},{4,7},{5,4},{6,5},{7,6},{8,11},{9,8},{10,9... | collective-permute-start | bytes 491528 | tf_op jit(solution)/shard_map/ppermute | solution.py:143
  10.9 2.1 %copy-start.7 = (bf16[3,3,3,8192]{3,2,1,0:T(4,128)(2,1)S(1)}, bf16[3,3,3,8192]{3,2,1,0:T(4,128)(2,1)}, u32[]{:S(2)}) copy-start(bf16[3,3,3,8192]{3,2,1,0:T(4,128)(2,1)} %param.5) | copy-start | bytes 1327108
  15.5 3.2 %copy-start.12 = (bf16[5,2,16,512]{3,2,1,0:T(8,128)(2,1)}, bf16[5,2,16,512]{3,2,1,0:T(8,128)(2,1)S(1)}, u32[]{:S(2)}) copy-start(bf16[5,2,16,512]{3,2,1,0:T(8,128)(2,1)S(1)} %collective-permute-done.refs_2_) | copy-start | bytes 491524
  15.5 19.0 %collective-permute-start.5 = (bf16[4,2,16,512]{3,2,1,0:T(8,128)(2,1)S(1)}, bf16[4,2,16,512]{3,2,1,0:T(8,128)(2,1)S(1)}, u32[]{:S(2)}, u32[]{:S(2)}) collective-permute-start(bf16[4,2,16,512]{3,2,1,0:T(8,128)(2,1)S(1)} %get-tuple-element.17), channel_id=1, source_target_pairs={{0,1},{1,2},{2,3},{3,0},{4,5},{5,6},{6,7},{7,4},{8,9},{9,10},{10,1... | collective-permute-start | bytes 393224 | tf_op jit(solution)/shard_map/ppermute | solution.py:143
  18.7 15.8 %collective-permute-start.6 = (bf16[4,2,16,512]{3,2,1,0:T(8,128)(2,1)S(1)}, bf16[4,2,16,512]{3,2,1,0:T(8,128)(2,1)S(1)}, u32[]{:S(2)}, u32[]{:S(2)}) collective-permute-start(bf16[4,2,16,512]{3,2,1,0:T(8,128)(2,1)S(1)} %get-tuple-element.18), channel_id=1, source_target_pairs={{0,2},{1,3},{2,0},{3,1},{4,6},{5,7},{6,4},{7,5},{8,10},{9,11},{10,... | collective-permute-start | bytes 393224 | tf_op jit(solution)/shard_map/ppermute | solution.py:143
  18.7 0.7 copy-start.14
  22.0 21.4 %copy-start = (bf16[5,2,64,512]{3,2,1,0:T(8,128)(2,1)S(1)}, bf16[5,2,64,512]{3,2,1,0:T(8,128)(2,1)}, u32[]{:S(2)}) copy-start(bf16[5,2,64,512]{3,2,1,0:T(8,128)(2,1)} %shard_map.37.refs_4_) | copy-start | bytes 1966084
  22.0 45.6 %collective-permute-start.3 = (bf16[5,2,64,512]{3,2,1,0:T(8,128)(2,1)}, bf16[5,2,64,512]{3,2,1,0:T(8,128)(2,1)S(1)}, u32[]{:S(2)}, u32[]{:S(2)}) collective-permute-start(bf16[5,2,64,512]{3,2,1,0:T(8,128)(2,1)} %shard_map.37.refs_4_), channel_id=1, source_target_pairs={{0,4},{4,8},{8,12},{1,5},{5,9},{9,13},{2,6},{6,10},{10,14},{3,7},{... | collective-permute-start | bytes 1966088 | tf_op jit(solution)/shard_map/ppermute | solution.py:105
  27.5 9.8 %collective-permute-start.7 = (bf16[4,2,16,512]{3,2,1,0:T(8,128)(2,1)S(1)}, bf16[4,2,16,512]{3,2,1,0:T(8,128)(2,1)S(1)}, u32[]{:S(2)}, u32[]{:S(2)}) collective-permute-start(bf16[4,2,16,512]{3,2,1,0:T(8,128)(2,1)S(1)} %get-tuple-element.19), channel_id=1, source_target_pairs={{0,3},{1,0},{2,1},{3,2},{4,7},{5,4},{6,5},{7,6},{8,11},{9,8},{10,9... | collective-permute-start | bytes 393224 | tf_op jit(solution)/shard_map/ppermute | solution.py:143
  34.5 2.9 %copy-start.16 = (bf16[4,2,16,512]{3,2,1,0:T(8,128)(2,1)}, bf16[4,2,16,512]{3,2,1,0:T(8,128)(2,1)S(1)}, u32[]{:S(2)}) copy-start(bf16[4,2,16,512]{3,2,1,0:T(8,128)(2,1)S(1)} %collective-permute-done.5.refs_2_) | copy-start | bytes 393220
  34.5 2.9 %copy-start.17 = (bf16[4,2,16,512]{3,2,1,0:T(8,128)(2,1)}, bf16[4,2,16,512]{3,2,1,0:T(8,128)(2,1)S(1)}, u32[]{:S(2)}) copy-start(bf16[4,2,16,512]{3,2,1,0:T(8,128)(2,1)S(1)} %collective-permute-done.6.refs_3_) | copy-start | bytes 393220
  40.4 12.0 %copy-start.1 = (bf16[4,2,64,512]{3,2,1,0:T(8,128)(2,1)S(1)}, bf16[4,2,64,512]{3,2,1,0:T(8,128)(2,1)}, u32[]{:S(2)}) copy-start(bf16[4,2,64,512]{3,2,1,0:T(8,128)(2,1)} %shard_map.39.refs_7_.refs_4_) | copy-start | bytes 1572868
  40.4 32.3 %collective-permute-start.8 = (bf16[4,2,64,512]{3,2,1,0:T(8,128)(2,1)}, bf16[4,2,64,512]{3,2,1,0:T(8,128)(2,1)S(1)}, u32[]{:S(2)}, u32[]{:S(2)}) collective-permute-start(bf16[4,2,64,512]{3,2,1,0:T(8,128)(2,1)} %shard_map.39.refs_7_.refs_4_), channel_id=1, source_target_pairs={{0,4},{4,8},{8,12},{1,5},{5,9},{9,13},{2,6},{6,10},{10,14},{3,7},{... | collective-permute-start | bytes 1572872 | tf_op jit(solution)/shard_map/ppermute | solution.py:105
  43.4 22.6 %copy-start.4 = (bf16[128,3,3,3,64]{0,4,3,2,1:T(8,128)(2,1)S(1)}, bf16[128,3,3,3,64]{0,4,3,2,1:T(8,128)(2,1)}, u32[]{:S(2)}) copy-start(bf16[128,3,3,3,64]{0,4,3,2,1:T(8,128)(2,1)} %copy.11) | copy-start | bytes 1327108
  43.4 20.4 %collective-permute-start.4 = (bf16[5,1,64,512]{3,2,1,0:T(8,128)(2,1)S(1)}, bf16[5,1,64,512]{3,2,1,0:T(8,128)(2,1)S(1)}, u32[]{:S(2)}, u32[]{:S(2)}) collective-permute-start(bf16[5,1,64,512]{3,2,1,0:T(8,128)(2,1)S(1)} %slice.12), channel_id=1, source_target_pairs={{4,0},{8,4},{12,8},{5,1},{9,5},{13,9},{6,2},{10,6},{14,10},{7,3},{... | collective-permute-start | bytes 983048 | tf_op jit(solution)/shard_map/ppermute | solution.py:105
  46.2 5.6 %collective-permute-start.10 = (bf16[2,2,16,512]{3,2,1,0:T(8,128)(2,1)S(1)}, bf16[2,2,16,512]{3,2,1,0:T(8,128)(2,1)S(1)}, u32[]{:S(2)}, u32[]{:S(2)}) collective-permute-start(bf16[2,2,16,512]{3,2,1,0:T(8,128)(2,1)S(1)} %get-tuple-element.20), channel_id=1, source_target_pairs={{0,1},{1,2},{2,3},{3,0},{4,5},{5,6},{6,7},{7,4},{8,9},{9,10},{10,1... | collective-permute-start | bytes 196616 | tf_op jit(solution)/shard_map/ppermute | solution.py:143
  47.9 6.4 %collective-permute-start.11 = (bf16[2,2,16,512]{3,2,1,0:T(8,128)(2,1)S(1)}, bf16[2,2,16,512]{3,2,1,0:T(8,128)(2,1)S(1)}, u32[]{:S(2)}, u32[]{:S(2)}) collective-permute-start(bf16[2,2,16,512]{3,2,1,0:T(8,128)(2,1)S(1)} %get-tuple-element.21), channel_id=1, source_target_pairs={{0,2},{1,3},{2,0},{3,1},{4,6},{5,7},{6,4},{7,5},{8,10},{9,11},{10,... | collective-permute-start | bytes 196616 | tf_op jit(solution)/shard_map/ppermute | solution.py:143
  51.8 4.9 %copy-start.19 = (bf16[2,2,16,512]{3,2,1,0:T(8,128)(2,1)}, bf16[2,2,16,512]{3,2,1,0:T(8,128)(2,1)S(1)}, u32[]{:S(2)}) copy-start(bf16[2,2,16,512]{3,2,1,0:T(8,128)(2,1)S(1)} %collective-permute-done.10.refs_2_) | copy-start | bytes 196612
  51.8 4.8 %collective-permute-start.12 = (bf16[2,2,16,512]{3,2,1,0:T(8,128)(2,1)S(1)}, bf16[2,2,16,512]{3,2,1,0:T(8,128)(2,1)S(1)}, u32[]{:S(2)}, u32[]{:S(2)}) collective-permute-start(bf16[2,2,16,512]{3,2,1,0:T(8,128)(2,1)S(1)} %get-tuple-element.22), channel_id=1, source_target_pairs={{0,3},{1,0},{2,1},{3,2},{4,7},{5,4},{6,5},{7,6},{8,11},{9,8},{10,9... | collective-permute-start | bytes 196616 | tf_op jit(solution)/shard_map/ppermute | solution.py:143
  54.3 2.3 %copy-start.20 = (bf16[2,2,16,512]{3,2,1,0:T(8,128)(2,1)}, bf16[2,2,16,512]{3,2,1,0:T(8,128)(2,1)S(1)}, u32[]{:S(2)}) copy-start(bf16[2,2,16,512]{3,2,1,0:T(8,128)(2,1)S(1)} %collective-permute-done.11.refs_3_) | copy-start | bytes 196612
  54.3 18.4 %collective-permute-start.9 = (bf16[4,1,64,512]{3,2,1,0:T(8,128)(2,1)S(1)}, bf16[4,1,64,512]{3,2,1,0:T(8,128)(2,1)S(1)}, u32[]{:S(2)}, u32[]{:S(2)}) collective-permute-start(bf16[4,1,64,512]{3,2,1,0:T(8,128)(2,1)S(1)} %slice.13), channel_id=1, source_target_pairs={{4,0},{8,4},{12,8},{5,1},{9,5},{13,9},{6,2},{10,6},{14,10},{7,3},{... | collective-permute-start | bytes 786440 | tf_op jit(solution)/shard_map/ppermute | solution.py:105
  59.4 20.0 %collective-permute-start.13 = (bf16[2,2,64,512]{3,2,1,0:T(8,128)(2,1)}, bf16[2,2,64,512]{3,2,1,0:T(8,128)(2,1)S(1)}, u32[]{:S(2)}, u32[]{:S(2)}) collective-permute-start(bf16[2,2,64,512]{3,2,1,0:T(8,128)(2,1)} %shard_map.41.refs_7_), channel_id=1, source_target_pairs={{0,4},{4,8},{8,12},{1,5},{5,9},{9,13},{2,6},{6,10},{10,14},{3,7},{... | collective-permute-start | bytes 786440 | tf_op jit(solution)/shard_map/ppermute | solution.py:105
  63.8 3.7 %copy-start.5 = (bf16[5,1,64,512]{3,2,1,0:T(8,128)(2,1)}, bf16[5,1,64,512]{3,2,1,0:T(8,128)(2,1)S(1)}, u32[]{:S(2)}) copy-start(bf16[5,1,64,512]{3,2,1,0:T(8,128)(2,1)S(1)} %collective-permute-done.4.refs_5_) | copy-start | bytes 983044
  63.9 15.5 %collective-permute-start.14 = (bf16[2,1,64,512]{3,2,1,0:T(8,128)(2,1)S(1)}, bf16[2,1,64,512]{3,2,1,0:T(8,128)(2,1)S(1)}, u32[]{:S(2)}, u32[]{:S(2)}) collective-permute-start(bf16[2,1,64,512]{3,2,1,0:T(8,128)(2,1)S(1)} %slice.14), channel_id=1, source_target_pairs={{4,0},{8,4},{12,8},{5,1},{9,5},{13,9},{6,2},{10,6},{14,10},{7,3},{... | collective-permute-start | bytes 393224 | tf_op jit(solution)/shard_map/ppermute | solution.py:105
  67.6 0.9 %copy-start.2 = (bf16[5,2,64,512]{3,2,1,0:T(8,128)(2,1)}, bf16[5,2,64,512]{3,2,1,0:T(8,128)(2,1)S(1)}, u32[]{:S(2)}) copy-start(bf16[5,2,64,512]{3,2,1,0:T(8,128)(2,1)S(1)} %collective-permute-done.3.refs_3_) | copy-start | bytes 1966084
  72.7 0.7 copy-start.6
  72.7 0.9 %copy-start.3 = (bf16[4,2,64,512]{3,2,1,0:T(8,128)(2,1)}, bf16[4,2,64,512]{3,2,1,0:T(8,128)(2,1)S(1)}, u32[]{:S(2)}) copy-start(bf16[4,2,64,512]{3,2,1,0:T(8,128)(2,1)S(1)} %collective-permute-done.8.refs_6_.refs_3_) | copy-start | bytes 1572868
  79.4 5.7 %copy-start.8 = (bf16[2,128,256]{2,1,0:T(8,128)(2,1)S(1)}, bf16[2,128,256]{2,1,0:T(8,128)(2,1)}, u32[]{:S(2)}) copy-start(bf16[2,128,256]{2,1,0:T(8,128)(2,1)} %shard_map.40) | copy-start | bytes 393220
  79.4 5.7 %copy-start.11 = (bf16[1,128,256]{2,1,0:T(8,128)(2,1)S(1)}, bf16[1,128,256]{2,1,0:T(8,128)(2,1)}, u32[]{:S(2)}) copy-start(bf16[1,128,256]{2,1,0:T(8,128)(2,1)} %shard_map.38) | copy-start | bytes 196612
  (5 other events, 3.3 us)

commit v3 on v1

v3 whole, which is shorter than its diff:
```python
import functools

import jax
import jax.numpy as jnp
from jax import lax
from jax.experimental import pallas as pl
from jax.experimental.pallas import tpu as pltpu
from jax.sharding import PartitionSpec as P

C = 64
C2 = 128
BELOW, ABOVE = 2, 1
negative_slope = 0.01
VMEM_LIMIT = 56 * 1024 * 1024


def split_matrix(width):
    half = width // 2
    source = lax.broadcasted_iota(jnp.int32, (width, width), 0)
    column = lax.broadcasted_iota(jnp.int32, (width, width), 1)
    wanted = jnp.where(column < half, 2 * column, 2 * (column - half) + 1)
    return jnp.where(source == wanted, 1.0, 0.0).astype(jnp.bfloat16)


def turn_matrix(count, rows):
    size = count * rows
    target = lax.broadcasted_iota(jnp.int32, (size, size), 0)
    source = lax.broadcasted_iota(jnp.int32, (size, size), 1)
    wanted = lax.rem(target, count) * rows + lax.div(target, count)
    return jnp.where(source == wanted, 1.0, 0.0).astype(jnp.bfloat16)


def send_kernel(band, parts, start_ref, volume_ref, *refs):
    out_refs, field_ref = refs[:-1], refs[-1]
    count, planes, all_rows, width = volume_ref.shape
    step = 16
    split, turn = split_matrix(width), turn_matrix(count, step)
    field_ref[pl.ds(0, BELOW)] = jnp.zeros((BELOW, planes, count, width), jnp.bfloat16)
    field_ref[pl.ds(BELOW + all_rows, ABOVE)] = jnp.zeros((ABOVE, planes, count, width), jnp.bfloat16)
    for p in range(planes):
        for at in range(0, all_rows, step):
            block = volume_ref[:, p, at : at + step, :].reshape(count * step, width)
            block = jnp.dot(block, split, preferred_element_type=jnp.float32).astype(jnp.bfloat16)
            block = jnp.dot(turn, block, preferred_element_type=jnp.float32).astype(jnp.bfloat16)
            field_ref[pl.ds(BELOW + at, step), p] = block.reshape(step, count, width)
    for (which, low, high), out_ref in zip(parts, out_refs):
        out_ref[...] = field_ref[pl.ds(start_ref[which] + low, high - low)]


def conv_kernel(parts, window, edge_ref, order_ref, first_ref, second_ref, *refs):
    blocks, (out_ref, taps_ref, hid_ref) = refs[:-3], refs[-3:]
    half = out_ref.shape[2]
    for i, (which, low, high) in enumerate(parts):
        below_ref, own_ref, above_ref = blocks[3 * i : 3 * i + 3]
        count = own_ref.shape[2]
        lane = lax.broadcasted_iota(jnp.int32, (count, half), 1)
        at = pl.multiple_of(order_ref[which] * count, count)
        for r in range(low, high):
            for p in range(5):
                cell = (below_ref, own_ref, above_ref)[p // 2][r - low, p % 2]
                even, odd = cell[:, :half], cell[:, half:]
                before = jnp.where(lane == 0, 0.0, pltpu.roll(odd.astype(jnp.float32), 1, 1))
                after = jnp.where(lane == half - 1, 0.0, pltpu.roll(even.astype(jnp.float32), half - 1, 1))
                shifts = (before.astype(jnp.bfloat16), even, odd, after.astype(jnp.bfloat16))
                for k, value in enumerate(shifts):
                    taps_ref[p, pl.ds((4 * r + k) * C + at, count), :] = value
    size = 2 * C
    lane = lax.broadcasted_iota(jnp.int32, (C, half), 1)
    for y in range(window - 2):
        total = [None] * 3
        for p in range(5):
            z_low, z_high = max(0, p - 2), min(2, p)
            first = 2 - (p - z_low)
            weight = first_ref[pl.ds(first * size, (z_high - z_low + 1) * size), :]
            part = jnp.dot(
                weight, taps_ref[p, pl.ds(y * 4 * C, 12 * C), :], preferred_element_type=jnp.float32
            )
            for z in range(z_low, z_high + 1):
                piece = part[(z - z_low) * size : (z - z_low + 1) * size]
                total[z] = piece if total[z] is None else total[z] + piece
        for z in range(3):
            value = total[z]
            value = jnp.where(value > 0, value, negative_slope * value)
            if z == 0:
                value = jnp.where(edge_ref[0] > 0, value, 0.0)
            if y == 0:
                value = jnp.where(edge_ref[1] > 0, value, 0.0)
            value = value.astype(jnp.bfloat16)
            before = jnp.where(lane == 0, 0.0, pltpu.roll(value[C:].astype(jnp.float32), 1, 1))
            base = (y * 3 + z) * 3 * C
            hid_ref[pl.ds(base, C), :] = before.astype(jnp.bfloat16)
            hid_ref[pl.ds(base + C, 2 * C), :] = value
    for y in range(out_ref.shape[0]):
        out_ref[y] = jnp.dot(
            second_ref[...], hid_ref[pl.ds(2 * y * 9 * C, 27 * C), :], preferred_element_type=jnp.float32
        ).astype(jnp.bfloat16)


def first_weights(conv_weight):
    shaped = jnp.transpose(conv_weight.reshape(3, 3, 3, C, C), (0, 3, 1, 2, 4))
    shaped = shaped[::-1]
    even = jnp.pad(shaped, ((0, 0), (0, 0), (0, 0), (0, 1), (0, 0)))
    odd = jnp.pad(shaped, ((0, 0), (0, 0), (0, 0), (1, 0), (0, 0)))
    return jnp.stack([even, odd], axis=1).reshape(3 * 2 * C, 12 * C)


def second_weights(down_weight):
    shaped = down_weight.reshape(3, 3, 3, C2, C)
    return jnp.transpose(shaped, (3, 1, 0, 2, 4)).reshape(C2, 27 * C)


def shifted(block, axis, by):
    count = lax.axis_size(axis)
    return lax.ppermute(block, axis, [(i, i + by) for i in range(count) if 0 <= i + by < count])


def after(value, *others):
    return lax.optimization_barrier((value, *others))[0]


def local(volume, conv_weight, down_weight):
    bands = lax.axis_size("filt")
    me = lax.axis_index("filt").astype(jnp.int32)
    space = lax.axis_index("space").astype(jnp.int32)
    count, planes, all_rows, width = volume.shape
    band = all_rows // bands
    window = BELOW + band + ABOVE
    vmem = pl.BlockSpec(memory_space=pltpu.VMEM)
    smem = pl.BlockSpec(memory_space=pltpu.SMEM)
    params = pltpu.CompilerParams(vmem_limit_bytes=VMEM_LIMIT)
    distance = jnp.arange(bands, dtype=jnp.int32)
    own = []
    first, second = first_weights(conv_weight), second_weights(down_weight)
    if count == 16 and bands == 4:
        parts = [(d, 0, window) for d in (0, 3, 1, 2)]
        sent = pl.pallas_call(
            functools.partial(send_kernel, band, parts),
            out_shape=[
                jax.ShapeDtypeStruct((high - low, planes, count, width), jnp.bfloat16)
                for _, low, high in parts
            ],
            in_specs=[smem, vmem],
            out_specs=[vmem] * len(parts),
            scratch_shapes=[
                pltpu.VMEM((BELOW + all_rows + ABOVE, planes, count, width), jnp.bfloat16)
            ],
            compiler_params=params,
        )(lax.rem(me + distance, bands) * band, volume)
        for (d, _, _), piece in zip(parts, sent):
            if d:
                piece = lax.ppermute(piece, "filt", [(i, (i + d) % bands) for i in range(bands)])
            own.append(piece)
        order = lax.rem(me - distance + bands, bands)
        own[0], own[1], first, second, order = lax.optimization_barrier((own[0], own[1], first, second, order))
    else:
        parts = [(0, 0, window)]
        field = jnp.transpose(volume, (2, 1, 0, 3))
        field = jnp.concatenate([field[..., ::2], field[..., 1::2]], axis=-1)
        field = jnp.pad(field, ((BELOW, ABOVE), (0, 0), (0, 0), (0, 0)))
        sent = jnp.stack([field[t * band : t * band + window] for t in range(bands)])
        got = lax.all_to_all(sent, "filt", split_axis=0, concat_axis=0, tiled=True)
        own.append(jnp.transpose(got, (1, 2, 0, 3, 4)).reshape(window, planes, C, width))
        order = jnp.zeros((1,), jnp.int32)
    triples = []
    for i, piece in enumerate(own):
        if i > 1:
            piece = after(piece, *triples[i - 2])
        triples.append((shifted(piece, "space", 1), piece, shifted(piece, "space", -1)))
    operands = [array for triple in triples for array in triple]
    coarse = pl.pallas_call(
        functools.partial(conv_kernel, parts, window),
        out_shape=jax.ShapeDtypeStruct((band // 2, C2, width // 2), jnp.bfloat16),
        in_specs=[smem] * 2 + [vmem] * (2 + len(operands)),
        out_specs=vmem,
        scratch_shapes=[
            pltpu.VMEM((5, window * 4 * C, width // 2), jnp.bfloat16),
            pltpu.VMEM(((band + 1) * 9 * C, width // 2), jnp.bfloat16),
        ],
        compiler_params=params,
    )(jnp.stack([space, me]), order, first, second, *operands)
    return jnp.transpose(coarse, (1, 0, 2))[:, None]


def solution(mesh):
    return jax.shard_map(
        local,
        mesh=mesh,
        in_specs=(P("filt", ("groups", "space"), None, None), P(), P()),
        out_specs=P(None, ("groups", "space"), "filt", None),
        check_vma=False,
    )
```

time: 73.5 us -> 66.5 us (0.905)
  waiting for transfers between devices: 33.1 us -> 11.4 us
  starting transfers between devices: 11.4 us -> 30.7 us
  local copies, waits for them, and re-layouts: 14.9 us -> 7.91 us
  Pallas kernels: 11.4 us -> 13.2 us
    ppermute x3, waiting for transfers between devices: 29.1 us -> 6.21 us  [local(): lax.ppermute(piece, 'filt', [(i, (i + d) % bands) for i in range(bands)])]
    ppermute x2 -> x8, starting transfers between devices: 6.76 us -> 25.4 us  [shifted(): lax.ppermute(block, axis, [(i, i + by) for i in range(count) if 0 <= i +...]
    unnamed x13 -> x22, local copies, waits for them, and re-layouts: 3.65 us -> 0.81 us
    slice x1 -> x0, local copies, waits for them, and re-layouts: 2.05 us -> none  [local(): high = shifted(own[:, :1], 'space', -1)]
    pallas_call x2, Pallas kernels: 11.4 us -> 13.2 us  [the longest x1 9.29 us: local(): pl.pallas_call(functools.partial(conv_kernel, parts, window), out_shape=j...]
    ppermute x2 -> x8, waiting for transfers between devices: 3.99 us -> 5.21 us  [shifted(): lax.ppermute(block, axis, [(i, i + by) for i in range(count) if 0 <= i +...]
    reshape x1, local copies, waits for them, and re-layouts: 1.87 us -> 0.71 us  [second_weights(): shaped = down_weight.reshape(3, 3, 3, C2, C)]
    reshape x1 -> x0, local copies, waits for them, and re-layouts: 1.01 us -> none  [second_weights(): return jnp.transpose(shaped, (3, 1, 0, 2, 4)).reshape(C2, 27 * C)]
  transfers between devices with their start and end apart: 5 -> 11, of which waited for: 5 -> 5; matrix products, arithmetic and copies ran while one was open for 15% -> 11% of each run, Pallas kernels for 0% -> 0%
where the time goes in v3:
time: 66.5 us; the launch traced here: 66.2 us
  starting transfers between devices  30.7 us (46%)
  Pallas kernels  13.2 us (20%)
  waiting for transfers between devices  11.4 us (17%)
  local copies, waits for them, and re-layouts  7.91 us (12%)
  other arithmetic  2.7 us (4%)
    ppermute x8, starting transfers between devices, shifted(): lax.ppermute(block, axis, [(i, i + by) for i in range(count) if 0 <= i +...  25.4 us
    pallas_call x1, Pallas kernels, local(): pl.pallas_call(functools.partial(conv_kernel, parts, window), out_shape=j...  9.29 us
    ppermute x3, waiting for transfers between devices, local(): lax.ppermute(piece, 'filt', [(i, (i + d) % bands) for i in range(bands)])  6.21 us
    ppermute x3, starting transfers between devices, local(): lax.ppermute(piece, 'filt', [(i, (i + d) % bands) for i in range(bands)])  5.34 us
    ppermute x8, waiting for transfers between devices, shifted(): lax.ppermute(block, axis, [(i, i + by) for i in range(count) if 0 <= i +...  5.21 us
    pallas_call x1, Pallas kernels, local(): pl.pallas_call(functools.partial(send_kernel, band, parts), out_shape=[ja...  3.9 us
    broadcast_in_dim x1, local copies, waits for them, and re-layouts, local(): return jnp.transpose(coarse, (1, 0, 2))[:, None]  1.86 us
    reshape x1, local copies, waits for them, and re-layouts, first_weights(): return jnp.stack([even, odd], axis=1).reshape(3 * 2 * C, 12 * C)  1.52 us
  transfers between devices with their start and end apart: 11, of which 5 were waited for; matrix products, arithmetic and copies ran while one was open for 11% of the time, Pallas kernels for 0%

profile of v3, /device:TPU:1, one launch (start us, length us, event | category | flops | bytes accessed | tf_op | source)
XLA Modules:
  0.0 66.2 jit_solution(643857151333103911)
XLA Ops:
  0.0 0.6 fusion.1.start_ref
  0.6 3.9 %shard_map.37 = (bf16[11,2,16,512]{3,2,1,0:T(8,128)(2,1)}, bf16[11,2,16,512]{3,2,1,0:T(8,128)(2,1)}, bf16[11,2,16,512]{3,2,1,0:T(8,128)(2,1)}, bf16[11,2,16,512]{3,2,1,0:T(8,128)(2,1)}) custom-call(s32[4]{0:T(128)} %fusion.1.start_ref, bf16[16,2,32,512]{3,2,1,0:T(8,128)(2,1)} %volume_ref.1), custom_call_target="tpu_custom_call" | custom-call | tf_op jit(solution)/shard_map/pallas_call | solution.py:136
  4.5 4.2 %collective-permute-start = (bf16[11,2,16,512]{3,2,1,0:T(8,128)(2,1)}, bf16[11,2,16,512]{3,2,1,0:T(8,128)(2,1)S(1)}, u32[]{:S(2)}, u32[]{:S(2)}) collective-permute-start(bf16[11,2,16,512]{3,2,1,0:T(8,128)(2,1)} %get-tuple-element.17), channel_id=1, source_target_pairs={{0,3},{1,0},{2,1},{3,2},{4,7},{5,4},{6,5},{7,6},{8,11},{9,8},{10,9... | collective-permute-start | bytes 1081352 | tf_op jit(solution)/shard_map/ppermute | solution.py:151
  8.7 0.4 reshape.12
  9.1 0.4 copy.14
  9.5 0.2 rev.3
  9.7 0.7 %pad_bitcast_fusion.1 = (bf16[3,1,64,3,4,64]{5,4,3,2,1,0:T(4,128)(2,1)S(1)}, bf16[3,1,64,3,4,64]{5,4,3,2,1,0:T(4,128)(2,1)S(1)}) fusion(bf16[3,64,3,3,64]{4,3,2,1,0:T(4,128)(2,1)S(1)} %rev.3), kind=kLoop, calls=%fused_computation.3 | loop fusion | bytes 811008 | tf_op jit(solution)/shard_map/stack | solution.py:104
  10.4 1.0 %pad_maximum_fusion = bf16[3,2,64,3,4,64]{5,4,3,2,1,0:T(4,128)(2,1)S(1)} fusion(bf16[3,1,64,3,4,64]{5,4,3,2,1,0:T(4,128)(2,1)S(1)} %get-tuple-element.28, bf16[3,1,64,3,4,64]{5,4,3,2,1,0:T(4,128)(2,1)S(1)} %get-tuple-element.27), kind=kLoop, calls=%fused_computation | loop fusion | flops 294912 | bytes 1179648 | tf_op jit(solution)/shard_map/stack | solution.py:104
  11.4 0.0 copy-start
  11.4 1.5 %reshape.13.first_ref = bf16[384,768]{1,0:T(8,128)(2,1)} reshape(bf16[3,2,64,3,4,64]{5,4,3,2,1,0:T(4,128)(2,1)S(1)} %pad_maximum_fusion) | data formatting | bytes 1179648 | tf_op jit(solution)/shard_map/reshape | solution.py:104
  12.9 0.7 %reshape.14 = bf16[3,3,3,128,64]{4,3,2,1,0:T(8,128)(2,1)S(1)} reshape(bf16[3,3,3,8192]{3,2,1,0:T(4,128)(2,1)S(1)} %copy-done) | data formatting | bytes 884736 | tf_op jit(solution)/shard_map/reshape | solution.py:108
  13.6 0.3 copy.10
  14.0 0.5 compare_select_fusion.order_ref
  14.5 1.6 %collective-permute-done.refs_4_ = bf16[11,2,16,512]{3,2,1,0:T(8,128)(2,1)S(1)} collective-permute-done((bf16[11,2,16,512]{3,2,1,0:T(8,128)(2,1)}, bf16[11,2,16,512]{3,2,1,0:T(8,128)(2,1)S(1)}, u32[]{:S(2)}, u32[]{:S(2)}) %collective-permute-start) | collective-permute-done | bytes 360480 | tf_op jit(solution)/shard_map/ppermute | solution.py:151
  16.2 5.6 %collective-permute-start.1 = (bf16[11,2,16,512]{3,2,1,0:T(8,128)(2,1)S(1)}, bf16[11,2,16,512]{3,2,1,0:T(8,128)(2,1)S(1)}, u32[]{:S(2)}, u32[]{:S(2)}) collective-permute-start(bf16[11,2,16,512]{3,2,1,0:T(8,128)(2,1)S(1)} %copy-done.1), channel_id=1, source_target_pairs={{0,4},{4,8},{8,12},{1,5},{5,9},{9,13},{2,6},{6,10},{10,14},{3,7},{... | collective-permute-start | bytes 1081352 | tf_op jit(solution)/shard_map/ppermute | solution.py:114
  21.7 1.9 %collective-permute-start.2 = (bf16[11,2,16,512]{3,2,1,0:T(8,128)(2,1)S(1)}, bf16[11,2,16,512]{3,2,1,0:T(8,128)(2,1)S(1)}, u32[]{:S(2)}, u32[]{:S(2)}) collective-permute-start(bf16[11,2,16,512]{3,2,1,0:T(8,128)(2,1)S(1)} %copy-done.1), channel_id=1, source_target_pairs={{4,0},{8,4},{12,8},{5,1},{9,5},{13,9},{6,2},{10,6},{14,10},{7,3},{... | collective-permute-start | bytes 1081352 | tf_op jit(solution)/shard_map/ppermute | solution.py:114
  23.7 1.2 %collective-permute-start.8 = (bf16[11,2,16,512]{3,2,1,0:T(8,128)(2,1)}, bf16[11,2,16,512]{3,2,1,0:T(8,128)(2,1)S(1)}, u32[]{:S(2)}, u32[]{:S(2)}) collective-permute-start(bf16[11,2,16,512]{3,2,1,0:T(8,128)(2,1)} %get-tuple-element.25), channel_id=1, source_target_pairs={{0,2},{1,3},{2,0},{3,1},{4,6},{5,7},{6,4},{7,5},{8,10},{9,11},{10,... | collective-permute-start | bytes 1081352 | tf_op jit(solution)/shard_map/ppermute | solution.py:151
  24.8 3.9 %collective-permute-start.3 = (bf16[11,2,16,512]{3,2,1,0:T(8,128)(2,1)S(1)}, bf16[11,2,16,512]{3,2,1,0:T(8,128)(2,1)S(1)}, u32[]{:S(2)}, u32[]{:S(2)}) collective-permute-start(bf16[11,2,16,512]{3,2,1,0:T(8,128)(2,1)S(1)} %collective-permute-done.refs_4_), channel_id=1, source_target_pairs={{0,4},{4,8},{8,12},{1,5},{5,9},{9,13},{2,6},{6,10},{10,14},{3,7},{... | collective-permute-start | bytes 1081352 | tf_op jit(solution)/shard_map/ppermute | solution.py:114
  28.8 1.9 %collective-permute-start.4 = (bf16[11,2,16,512]{3,2,1,0:T(8,128)(2,1)S(1)}, bf16[11,2,16,512]{3,2,1,0:T(8,128)(2,1)S(1)}, u32[]{:S(2)}, u32[]{:S(2)}) collective-permute-start(bf16[11,2,16,512]{3,2,1,0:T(8,128)(2,1)S(1)} %collective-permute-done.refs_4_), channel_id=1, source_target_pairs={{4,0},{8,4},{12,8},{5,1},{9,5},{13,9},{6,2},{10,6},{14,10},{7,3},{... | collective-permute-start | bytes 1081352 | tf_op jit(solution)/shard_map/ppermute | solution.py:114
  30.7 0.1 collective-permute-done.2.refs_2_
  30.8 3.6 %collective-permute-start.6 = (bf16[11,2,16,512]{3,2,1,0:T(8,128)(2,1)S(1)}, bf16[11,2,16,512]{3,2,1,0:T(8,128)(2,1)S(1)}, u32[]{:S(2)}, u32[]{:S(2)}) collective-permute-start(bf16[11,2,16,512]{3,2,1,0:T(8,128)(2,1)S(1)} %collective-permute-done.5.refs_7_), channel_id=1, source_target_pairs={{0,4},{4,8},{8,12},{1,5},{5,9},{9,13},{2,6},{6,10},{10,14},{3,7},{... | collective-permute-start | bytes 1081352 | tf_op jit(solution)/shard_map/ppermute | solution.py:114
  34.4 1.9 %collective-permute-start.7 = (bf16[11,2,16,512]{3,2,1,0:T(8,128)(2,1)S(1)}, bf16[11,2,16,512]{3,2,1,0:T(8,128)(2,1)}, u32[]{:S(2)}, u32[]{:S(2)}) collective-permute-start(bf16[11,2,16,512]{3,2,1,0:T(8,128)(2,1)S(1)} %collective-permute-done.5.refs_7_), channel_id=1, source_target_pairs={{4,0},{8,4},{12,8},{5,1},{9,5},{13,9},{6,2},{10,6},{14,10},{7,3},{... | collective-permute-start | bytes 1081352 | tf_op jit(solution)/shard_map/ppermute | solution.py:114
  36.3 4.6 %collective-permute-done.8.refs_10_ = bf16[11,2,16,512]{3,2,1,0:T(8,128)(2,1)S(1)} collective-permute-done((bf16[11,2,16,512]{3,2,1,0:T(8,128)(2,1)}, bf16[11,2,16,512]{3,2,1,0:T(8,128)(2,1)S(1)}, u32[]{:S(2)}, u32[]{:S(2)}) %collective-permute-start.8) | collective-permute-done | bytes 360480 | tf_op jit(solution)/shard_map/ppermute | solution.py:151
  40.9 0.8 %copy-done.8 = bf16[11,2,16,512]{3,2,1,0:T(8,128)(2,1)} copy-done((bf16[11,2,16,512]{3,2,1,0:T(8,128)(2,1)}, bf16[11,2,16,512]{3,2,1,0:T(8,128)(2,1)S(1)}, u32[]{:S(2)}) %copy-start.8) | copy-done | bytes 360472
  41.7 4.4 %collective-permute-start.9 = (bf16[11,2,16,512]{3,2,1,0:T(8,128)(2,1)S(1)}, bf16[11,2,16,512]{3,2,1,0:T(8,128)(2,1)}, u32[]{:S(2)}, u32[]{:S(2)}) collective-permute-start(bf16[11,2,16,512]{3,2,1,0:T(8,128)(2,1)S(1)} %collective-permute-done.8.refs_10_), channel_id=1, source_target_pairs={{0,4},{4,8},{8,12},{1,5},{5,9},{9,13},{2,6},{6,10},{10,14},{3,7},{... | collective-permute-start | bytes 1081352 | tf_op jit(solution)/shard_map/ppermute | solution.py:114
  46.1 2.1 %collective-permute-start.10 = (bf16[11,2,16,512]{3,2,1,0:T(8,128)(2,1)S(1)}, bf16[11,2,16,512]{3,2,1,0:T(8,128)(2,1)}, u32[]{:S(2)}, u32[]{:S(2)}) collective-permute-start(bf16[11,2,16,512]{3,2,1,0:T(8,128)(2,1)S(1)} %collective-permute-done.8.refs_10_), channel_id=1, source_target_pairs={{4,0},{8,4},{12,8},{5,1},{9,5},{13,9},{6,2},{10,6},{14,10},{7,3},{... | collective-permute-start | bytes 1081352 | tf_op jit(solution)/shard_map/ppermute | solution.py:114
  48.2 0.6 pad_add_fusion.edge_ref
  48.8 1.0 %copy.11.second_ref = bf16[128,1728]{1,0:T(8,128)(2,1)} copy(bf16[128,1728]{0,1:T(8,128)(2,1)S(1)} %bitcast.18) | data formatting | bytes 884736 | tf_op jit(solution)/shard_map/optimization_barrier | solution.py:154
  49.8 0.6 collective-permute-done.9.refs_9_
  50.5 4.5 %collective-permute-done.10.refs_11_ = bf16[11,2,16,512]{3,2,1,0:T(8,128)(2,1)} collective-permute-done((bf16[11,2,16,512]{3,2,1,0:T(8,128)(2,1)S(1)}, bf16[11,2,16,512]{3,2,1,0:T(8,128)(2,1)}, u32[]{:S(2)}, u32[]{:S(2)}) %collective-permute-start.10) | collective-permute-done | bytes 360480 | tf_op jit(solution)/shard_map/ppermute | solution.py:114
  55.0 9.3 %shard_map.38 = bf16[4,128,256]{2,1,0:T(8,128)(2,1)} custom-call(s32[2]{0:T(128)} %pad_add_fusion.edge_ref, s32[4]{0:T(128)} %compare_select_fusion.order_ref, bf16[384,768]{1,0:T(8,128)(2,1)} %reshape.13.first_ref, bf16[128,1728]{1,0:T(8,128)(2,1)} %copy.11.second_ref, bf16[11,2,16,512]{3,2,1,0:T(8,128)(2,1)} %copy-done.4, ...), custom_call_target="tpu_custom_call" | custom-call | tf_op jit(solution)/shard_map/pallas_call | solution.py:170
  64.3 1.9 %copy.12 = bf16[128,1,4,256]{3,2,1,0:T(4,128)(2,1)} copy(bf16[128,1,4,256]{3,0,2,1:T(8,128)(2,1)} %bitcast.19) | data formatting | bytes 524288 | tf_op jit(solution)/shard_map/broadcast_in_dim | solution.py:181
  (27 shorter events, 0.1 us)
Async XLA Ops:
  0.0 8.7 %copy-start.10 = (bf16[3,3,3,4096]{3,2,1,0:T(4,128)(2,1)S(1)}, bf16[3,3,3,4096]{3,2,1,0:T(4,128)(2,1)}, u32[]{:S(2)}) copy-start(bf16[3,3,3,4096]{3,2,1,0:T(4,128)(2,1)} %param.4) | copy-start | bytes 663556
  4.5 11.7 %collective-permute-start = (bf16[11,2,16,512]{3,2,1,0:T(8,128)(2,1)}, bf16[11,2,16,512]{3,2,1,0:T(8,128)(2,1)S(1)}, u32[]{:S(2)}, u32[]{:S(2)}) collective-permute-start(bf16[11,2,16,512]{3,2,1,0:T(8,128)(2,1)} %get-tuple-element.17), channel_id=1, source_target_pairs={{0,3},{1,0},{2,1},{3,2},{4,7},{5,4},{6,5},{7,6},{8,11},{9,8},{10,9... | collective-permute-start | bytes 1081352 | tf_op jit(solution)/shard_map/ppermute | solution.py:151
  8.7 20.1 %collective-permute-start.5 = (bf16[11,2,16,512]{3,2,1,0:T(8,128)(2,1)}, bf16[11,2,16,512]{3,2,1,0:T(8,128)(2,1)S(1)}, u32[]{:S(2)}, u32[]{:S(2)}) collective-permute-start(bf16[11,2,16,512]{3,2,1,0:T(8,128)(2,1)} %get-tuple-element.23), channel_id=1, source_target_pairs={{0,1},{1,2},{2,3},{3,0},{4,5},{5,6},{6,7},{7,4},{8,9},{9,10},{10,1... | collective-permute-start | bytes 1081352 | tf_op jit(solution)/shard_map/ppermute | solution.py:151
  11.4 1.5 %copy-start = (bf16[3,3,3,8192]{3,2,1,0:T(4,128)(2,1)S(1)}, bf16[3,3,3,8192]{3,2,1,0:T(4,128)(2,1)}, u32[]{:S(2)}) copy-start(bf16[3,3,3,8192]{3,2,1,0:T(4,128)(2,1)} %param.5) | copy-start | bytes 1327108
  12.9 3.3 %copy-start.1 = (bf16[11,2,16,512]{3,2,1,0:T(8,128)(2,1)S(1)}, bf16[11,2,16,512]{3,2,1,0:T(8,128)(2,1)}, u32[]{:S(2)}) copy-start(bf16[11,2,16,512]{3,2,1,0:T(8,128)(2,1)} %get-tuple-element.21.refs_1_) | copy-start | bytes 1081348
  16.1 38.8 %copy-start.2 = (bf16[11,2,16,512]{3,2,1,0:T(8,128)(2,1)}, bf16[11,2,16,512]{3,2,1,0:T(8,128)(2,1)S(1)}, u32[]{:S(2)}) copy-start(bf16[11,2,16,512]{3,2,1,0:T(8,128)(2,1)S(1)} %collective-permute-done.refs_4_) | copy-start | bytes 1081348
  16.2 14.5 %collective-permute-start.1 = (bf16[11,2,16,512]{3,2,1,0:T(8,128)(2,1)S(1)}, bf16[11,2,16,512]{3,2,1,0:T(8,128)(2,1)S(1)}, u32[]{:S(2)}, u32[]{:S(2)}) collective-permute-start(bf16[11,2,16,512]{3,2,1,0:T(8,128)(2,1)S(1)} %copy-done.1), channel_id=1, source_target_pairs={{0,4},{4,8},{8,12},{1,5},{5,9},{9,13},{2,6},{6,10},{10,14},{3,7},{... | collective-permute-start | bytes 1081352 | tf_op jit(solution)/shard_map/ppermute | solution.py:114
  21.7 9.0 %collective-permute-start.2 = (bf16[11,2,16,512]{3,2,1,0:T(8,128)(2,1)S(1)}, bf16[11,2,16,512]{3,2,1,0:T(8,128)(2,1)S(1)}, u32[]{:S(2)}, u32[]{:S(2)}) collective-permute-start(bf16[11,2,16,512]{3,2,1,0:T(8,128)(2,1)S(1)} %copy-done.1), channel_id=1, source_target_pairs={{4,0},{8,4},{12,8},{5,1},{9,5},{13,9},{6,2},{10,6},{14,10},{7,3},{... | collective-permute-start | bytes 1081352 | tf_op jit(solution)/shard_map/ppermute | solution.py:114
  23.7 17.2 %collective-permute-start.8 = (bf16[11,2,16,512]{3,2,1,0:T(8,128)(2,1)}, bf16[11,2,16,512]{3,2,1,0:T(8,128)(2,1)S(1)}, u32[]{:S(2)}, u32[]{:S(2)}) collective-permute-start(bf16[11,2,16,512]{3,2,1,0:T(8,128)(2,1)} %get-tuple-element.25), channel_id=1, source_target_pairs={{0,2},{1,3},{2,0},{3,1},{4,6},{5,7},{6,4},{7,5},{8,10},{9,11},{10,... | collective-permute-start | bytes 1081352 | tf_op jit(solution)/shard_map/ppermute | solution.py:151
  24.8 16.1 %collective-permute-start.3 = (bf16[11,2,16,512]{3,2,1,0:T(8,128)(2,1)S(1)}, bf16[11,2,16,512]{3,2,1,0:T(8,128)(2,1)S(1)}, u32[]{:S(2)}, u32[]{:S(2)}) collective-permute-start(bf16[11,2,16,512]{3,2,1,0:T(8,128)(2,1)S(1)} %collective-permute-done.refs_4_), channel_id=1, source_target_pairs={{0,4},{4,8},{8,12},{1,5},{5,9},{9,13},{2,6},{6,10},{10,14},{3,7},{... | collective-permute-start | bytes 1081352 | tf_op jit(solution)/shard_map/ppermute | solution.py:114
  28.8 26.2 %copy-start.3 = (bf16[11,2,16,512]{3,2,1,0:T(8,128)(2,1)}, bf16[11,2,16,512]{3,2,1,0:T(8,128)(2,1)S(1)}, u32[]{:S(2)}) copy-start(bf16[11,2,16,512]{3,2,1,0:T(8,128)(2,1)S(1)} %collective-permute-done.5.refs_7_) | copy-start | bytes 1081348
  28.8 12.1 %collective-permute-start.4 = (bf16[11,2,16,512]{3,2,1,0:T(8,128)(2,1)S(1)}, bf16[11,2,16,512]{3,2,1,0:T(8,128)(2,1)S(1)}, u32[]{:S(2)}, u32[]{:S(2)}) collective-permute-start(bf16[11,2,16,512]{3,2,1,0:T(8,128)(2,1)S(1)} %collective-permute-done.refs_4_), channel_id=1, source_target_pairs={{4,0},{8,4},{12,8},{5,1},{9,5},{13,9},{6,2},{10,6},{14,10},{7,3},{... | collective-permute-start | bytes 1081352 | tf_op jit(solution)/shard_map/ppermute | solution.py:114
  30.7 24.3 %copy-start.4 = (bf16[11,2,16,512]{3,2,1,0:T(8,128)(2,1)}, bf16[11,2,16,512]{3,2,1,0:T(8,128)(2,1)S(1)}, u32[]{:S(2)}) copy-start(bf16[11,2,16,512]{3,2,1,0:T(8,128)(2,1)S(1)} %collective-permute-done.1.refs_0_) | copy-start | bytes 1081348
  30.8 24.2 %copy-start.5 = (bf16[11,2,16,512]{3,2,1,0:T(8,128)(2,1)}, bf16[11,2,16,512]{3,2,1,0:T(8,128)(2,1)S(1)}, u32[]{:S(2)}) copy-start(bf16[11,2,16,512]{3,2,1,0:T(8,128)(2,1)S(1)} %collective-permute-done.2.refs_2_) | copy-start | bytes 1081348
  30.8 19.0 %collective-permute-start.6 = (bf16[11,2,16,512]{3,2,1,0:T(8,128)(2,1)S(1)}, bf16[11,2,16,512]{3,2,1,0:T(8,128)(2,1)S(1)}, u32[]{:S(2)}, u32[]{:S(2)}) collective-permute-start(bf16[11,2,16,512]{3,2,1,0:T(8,128)(2,1)S(1)} %collective-permute-done.5.refs_7_), channel_id=1, source_target_pairs={{0,4},{4,8},{8,12},{1,5},{5,9},{9,13},{2,6},{6,10},{10,14},{3,7},{... | collective-permute-start | bytes 1081352 | tf_op jit(solution)/shard_map/ppermute | solution.py:114
  34.4 15.4 %collective-permute-start.7 = (bf16[11,2,16,512]{3,2,1,0:T(8,128)(2,1)S(1)}, bf16[11,2,16,512]{3,2,1,0:T(8,128)(2,1)}, u32[]{:S(2)}, u32[]{:S(2)}) collective-permute-start(bf16[11,2,16,512]{3,2,1,0:T(8,128)(2,1)S(1)} %collective-permute-done.5.refs_7_), channel_id=1, source_target_pairs={{4,0},{8,4},{12,8},{5,1},{9,5},{13,9},{6,2},{10,6},{14,10},{7,3},{... | collective-permute-start | bytes 1081352 | tf_op jit(solution)/shard_map/ppermute | solution.py:114
  40.9 14.1 %copy-start.6 = (bf16[11,2,16,512]{3,2,1,0:T(8,128)(2,1)}, bf16[11,2,16,512]{3,2,1,0:T(8,128)(2,1)S(1)}, u32[]{:S(2)}) copy-start(bf16[11,2,16,512]{3,2,1,0:T(8,128)(2,1)S(1)} %collective-permute-done.8.refs_10_) | copy-start | bytes 1081348
  40.9 14.1 %copy-start.7 = (bf16[11,2,16,512]{3,2,1,0:T(8,128)(2,1)}, bf16[11,2,16,512]{3,2,1,0:T(8,128)(2,1)S(1)}, u32[]{:S(2)}) copy-start(bf16[11,2,16,512]{3,2,1,0:T(8,128)(2,1)S(1)} %collective-permute-done.3.refs_3_) | copy-start | bytes 1081348
  40.9 0.8 %copy-start.8 = (bf16[11,2,16,512]{3,2,1,0:T(8,128)(2,1)}, bf16[11,2,16,512]{3,2,1,0:T(8,128)(2,1)S(1)}, u32[]{:S(2)}) copy-start(bf16[11,2,16,512]{3,2,1,0:T(8,128)(2,1)S(1)} %collective-permute-done.4.refs_5_) | copy-start | bytes 1081348
  41.7 8.8 %collective-permute-start.9 = (bf16[11,2,16,512]{3,2,1,0:T(8,128)(2,1)S(1)}, bf16[11,2,16,512]{3,2,1,0:T(8,128)(2,1)}, u32[]{:S(2)}, u32[]{:S(2)}) collective-permute-start(bf16[11,2,16,512]{3,2,1,0:T(8,128)(2,1)S(1)} %collective-permute-done.8.refs_10_), channel_id=1, source_target_pairs={{0,4},{4,8},{8,12},{1,5},{5,9},{9,13},{2,6},{6,10},{10,14},{3,7},{... | collective-permute-start | bytes 1081352 | tf_op jit(solution)/shard_map/ppermute | solution.py:114
  46.1 8.9 %collective-permute-start.10 = (bf16[11,2,16,512]{3,2,1,0:T(8,128)(2,1)S(1)}, bf16[11,2,16,512]{3,2,1,0:T(8,128)(2,1)}, u32[]{:S(2)}, u32[]{:S(2)}) collective-permute-start(bf16[11,2,16,512]{3,2,1,0:T(8,128)(2,1)S(1)} %collective-permute-done.8.refs_10_), channel_id=1, source_target_pairs={{4,0},{8,4},{12,8},{5,1},{9,5},{13,9},{6,2},{10,6},{14,10},{7,3},{... | collective-permute-start | bytes 1081352 | tf_op jit(solution)/shard_map/ppermute | solution.py:114
  49.8 5.2 %copy-start.9 = (bf16[11,2,16,512]{3,2,1,0:T(8,128)(2,1)}, bf16[11,2,16,512]{3,2,1,0:T(8,128)(2,1)S(1)}, u32[]{:S(2)}) copy-start(bf16[11,2,16,512]{3,2,1,0:T(8,128)(2,1)S(1)} %collective-permute-done.6.refs_6_) | copy-start | bytes 1081348

commit v4 on v3

v4 whole, which is shorter than its diff:
```python
import functools

import jax
import jax.numpy as jnp
from jax import lax
from jax.experimental import pallas as pl
from jax.experimental.pallas import tpu as pltpu
from jax.sharding import PartitionSpec as P

C = 64
C2 = 128
BELOW, ABOVE = 2, 1
negative_slope = 0.01
VMEM_LIMIT = 20 * 1024 * 1024


def split_matrix(width):
    half = width // 2
    source = lax.broadcasted_iota(jnp.int32, (width, width), 0)
    column = lax.broadcasted_iota(jnp.int32, (width, width), 1)
    wanted = jnp.where(column < half, 2 * column, 2 * (column - half) + 1)
    return jnp.where(source == wanted, 1.0, 0.0).astype(jnp.bfloat16)


def turn_matrix(count, rows):
    size = count * rows
    target = lax.broadcasted_iota(jnp.int32, (size, size), 0)
    source = lax.broadcasted_iota(jnp.int32, (size, size), 1)
    wanted = lax.rem(target, count) * rows + lax.div(target, count)
    return jnp.where(source == wanted, 1.0, 0.0).astype(jnp.bfloat16)


def send_kernel(band, distances, volume_ref, *refs):
    out_refs, field_ref = refs[:-1], refs[-1]
    count, planes, all_rows, width = volume_ref.shape
    step = 16
    split, turn = split_matrix(width), turn_matrix(count, step)
    field_ref[pl.ds(0, BELOW)] = jnp.zeros((BELOW, planes, count, width), jnp.bfloat16)
    field_ref[pl.ds(BELOW + all_rows, ABOVE)] = jnp.zeros((ABOVE, planes, count, width), jnp.bfloat16)
    for p in range(planes):
        for at in range(0, all_rows, step):
            block = volume_ref[:, p, at : at + step, :].reshape(count * step, width)
            block = jnp.dot(block, split, preferred_element_type=jnp.float32).astype(jnp.bfloat16)
            block = jnp.dot(turn, block, preferred_element_type=jnp.float32).astype(jnp.bfloat16)
            field_ref[pl.ds(BELOW + at, step), p] = block.reshape(step, count, width)
    me, bands = lax.axis_index("filt"), lax.axis_size("filt")
    for d, out_ref in zip(distances, out_refs):
        start = lax.rem(me + d, bands) * band
        out_ref[...] = field_ref[pl.ds(start, out_ref.shape[0])]


def store_taps(taps_ref, row, at, channels, cell):
    count, half = cell.shape[0], cell.shape[1] // 2
    lane = lax.broadcasted_iota(jnp.int32, (count, half), 1)
    even, odd = cell[:, :half], cell[:, half:]
    before = jnp.where(lane == 0, 0.0, pltpu.roll(odd.astype(jnp.float32), 1, 1))
    after_it = jnp.where(lane == half - 1, 0.0, pltpu.roll(even.astype(jnp.float32), half - 1, 1))
    for k, value in enumerate((before.astype(jnp.bfloat16), even, odd, after_it.astype(jnp.bfloat16))):
        taps_ref[pl.ds((4 * row + k) * channels + at, count), :] = value


def plane_parts(total, weight_ref, taps, y, p, depth):
    size = 2 * C
    z_low, z_high = max(0, p - 2), min(2, p)
    first = 2 - (p - z_low)
    weight = weight_ref[pl.ds(first * size, (z_high - z_low + 1) * size), :]
    part = jnp.dot(weight, taps[pl.ds(y * depth, 3 * depth), :], preferred_element_type=jnp.float32)
    for z in range(z_low, z_high + 1):
        piece = part[(z - z_low) * size : (z - z_low + 1) * size]
        total[z] = piece if total[z] is None else total[z] + piece


def early_kernel(parts, late, window, first_ref, *refs):
    blocks, (out_ref, taps_ref) = refs[:-2], refs[-2:]
    half = out_ref.shape[1]
    for i, row, at, planes in parts:
        for r in range(window):
            for k, p in enumerate(planes):
                if p is not None:
                    store_taps(taps_ref.at[p], r, at, C, blocks[i][row + r, k])
    if late:
        empty = jnp.zeros((late, half), jnp.bfloat16)
        for p in (0, 1, 4):
            for r in range(4 * window):
                taps_ref[p, pl.ds(r * C + C - late, late), :] = empty
    for y in range(window - 2):
        total = [None] * 3
        for p in range(5):
            plane_parts(total, first_ref, taps_ref.at[p], y, p, 4 * C)
        for z in range(3):
            out_ref[pl.ds((y * 3 + z) * 2 * C, 2 * C), :] = total[z]


def late_kernel(late, window, edge_ref, feature_ref, second_ref, *refs):
    out_ref, hid_ref = refs[-2:] if not late else refs[-3:-1]
    half = out_ref.shape[2]
    if late:
        weight_ref, below_ref, above_ref, taps_ref = refs[0], refs[1], refs[2], refs[-1]
        for r in range(window):
            store_taps(taps_ref.at[0], r, 0, late, below_ref[r, 0])
            store_taps(taps_ref.at[1], r, 0, late, below_ref[r, 1])
            store_taps(taps_ref.at[2], r, 0, late, above_ref[r, 0])
    size = 2 * C
    lane = lax.broadcasted_iota(jnp.int32, (C, half), 1)
    for y in range(window - 2):
        total = [feature_ref[pl.ds((y * 3 + z) * size, size), :] for z in range(3)]
        if late:
            for k, p in enumerate((0, 1, 4)):
                plane_parts(total, weight_ref, taps_ref.at[k], y, p, 4 * late)
        for z in range(3):
            value = total[z]
            value = jnp.where(value > 0, value, negative_slope * value)
            if z == 0:
                value = jnp.where(edge_ref[0] > 0, value, 0.0)
            if y == 0:
                value = jnp.where(edge_ref[1] > 0, value, 0.0)
            value = value.astype(jnp.bfloat16)
            before = jnp.where(lane == 0, 0.0, pltpu.roll(value[C:].astype(jnp.float32), 1, 1))
            base = (y * 3 + z) * 3 * C
            hid_ref[pl.ds(base, C), :] = before.astype(jnp.bfloat16)
            hid_ref[pl.ds(base + C, 2 * C), :] = value
    for y in range(out_ref.shape[0]):
        out_ref[y] = jnp.dot(
            second_ref[...], hid_ref[pl.ds(2 * y * 9 * C, 27 * C), :], preferred_element_type=jnp.float32
        ).astype(jnp.bfloat16)


def first_weights(conv_weight, turn):
    shaped = conv_weight.reshape(3, 3, 3, C, C)
    if turn is not None:
        shaped = jnp.dot(shaped, turn, preferred_element_type=jnp.float32).astype(jnp.bfloat16)
    shaped = jnp.transpose(shaped, (0, 3, 1, 2, 4))[::-1]
    even = jnp.pad(shaped, ((0, 0), (0, 0), (0, 0), (0, 1), (0, 0)))
    odd = jnp.pad(shaped, ((0, 0), (0, 0), (0, 0), (1, 0), (0, 0)))
    return jnp.stack([even, odd], axis=1).reshape(3 * 2 * C, 12 * C)


def second_weights(down_weight):
    shaped = down_weight.reshape(3, 3, 3, C2, C)
    return jnp.transpose(shaped, (3, 1, 0, 2, 4)).reshape(C2, 27 * C)


def shifted(block, axis, by):
    count = lax.axis_size(axis)
    return lax.ppermute(block, axis, [(i, i + by) for i in range(count) if 0 <= i + by < count])


def after(value, *others):
    return lax.optimization_barrier((value, *others))[0]


def in_vmem(value):
    return pltpu.with_memory_space_constraint(value, pltpu.VMEM)


def block_order(me, distances, bands, count):
    row = lax.broadcasted_iota(jnp.int32, (C, C), 0)
    column = lax.broadcasted_iota(jnp.int32, (C, C), 1)
    piece = column // count
    source = sum(jnp.where(piece == i, lax.rem(me - d + bands, bands), 0) for i, d in enumerate(distances))
    return (row == source * count + column % count).astype(jnp.bfloat16)


def local(volume, conv_weight, down_weight):
    bands = lax.axis_size("filt")
    me = lax.axis_index("filt").astype(jnp.int32)
    space = lax.axis_index("space").astype(jnp.int32)
    count, planes, all_rows, width = volume.shape
    band = all_rows // bands
    window = BELOW + band + ABOVE
    half = width // 2
    vmem = pl.BlockSpec(memory_space=pltpu.VMEM)
    smem = pl.BlockSpec(memory_space=pltpu.SMEM)
    params = pltpu.CompilerParams(vmem_limit_bytes=VMEM_LIMIT)
    second = second_weights(down_weight)
    below, inside, above = (0, 1), (2, 3), (4, None)
    if count == 16 and bands == 4:
        distances = (0, 3, 1, 2)
        sent = pl.pallas_call(
            functools.partial(send_kernel, band, distances),
            out_shape=[pltpu.VMEM((window, planes, count, width), jnp.bfloat16)] * bands,
            in_specs=[vmem],
            out_specs=[vmem] * bands,
            scratch_shapes=[
                pltpu.VMEM((BELOW + all_rows + ABOVE, planes, count, width), jnp.bfloat16)
            ],
            compiler_params=params,
        )(volume)
        own = [
            lax.ppermute(piece, "filt", [(i, (i + d) % bands) for i in range(bands)]) if d else piece
            for d, piece in zip(distances, sent)
        ]
        first = first_weights(conv_weight, block_order(me, distances, bands, count))
        late = count
        last = first.reshape(6 * C, 12, C)[:, :, C - late :].reshape(6 * C, 12 * late)
        mine = after(own[0], own[1])
        middle = jnp.concatenate(own[1:3])
        middle = after(middle, own[1])
        blocks = [own[0], shifted(mine, "space", 1), shifted(mine, "space", -1)]
        blocks += [middle, shifted(middle, "space", 1), shifted(middle, "space", -1), own[3]]
        parts = []
        for i, held in enumerate((inside, below, above)):
            parts += [(i, 0, 0, held), (3 + i, 0, count, held), (3 + i, window, 2 * count, held)]
        parts.append((6, 0, 3 * count, inside))
        tail, first, second, last = lax.optimization_barrier((own[3], first, second, last, *blocks[1:3]))[:4]
        tails = [last, shifted(tail, "space", 1), shifted(tail, "space", -1)]
    else:
        field = jnp.transpose(volume, (2, 1, 0, 3))
        field = jnp.concatenate([field[..., ::2], field[..., 1::2]], axis=-1)
        field = jnp.pad(field, ((BELOW, ABOVE), (0, 0), (0, 0), (0, 0)))
        sent = jnp.stack([field[t * band : t * band + window] for t in range(bands)])
        got = lax.all_to_all(sent, "filt", split_axis=0, concat_axis=0, tiled=True)
        own = jnp.transpose(got, (1, 2, 0, 3, 4)).reshape(window, planes, C, width)
        first = first_weights(conv_weight, None)
        blocks = [own, shifted(own, "space", 1), shifted(own, "space", -1)]
        parts = [(i, 0, 0, held) for i, held in enumerate((inside, below, above))]
        late, tails = 0, []
    hid_rows = band + 1
    feature = pl.pallas_call(
        functools.partial(early_kernel, parts, late, window),
        out_shape=pltpu.VMEM((hid_rows * 6 * C, half), jnp.float32),
        in_specs=[vmem] * (1 + len(blocks)),
        out_specs=vmem,
        scratch_shapes=[pltpu.VMEM((5, window * 4 * C, half), jnp.bfloat16)],
        compiler_params=params,
    )(in_vmem(first), *map(in_vmem, blocks))
    coarse = pl.pallas_call(
        functools.partial(late_kernel, late, window),
        out_shape=pltpu.VMEM((band // 2, C2, half), jnp.bfloat16),
        in_specs=[smem] + [vmem] * (2 + len(tails)),
        out_specs=vmem,
        scratch_shapes=[pltpu.VMEM((hid_rows * 9 * C, half), jnp.bfloat16)]
        + [pltpu.VMEM((3, window * 4 * late, half), jnp.bfloat16)] * (late > 0),
        compiler_params=params,
    )(jnp.stack([space, me]), in_vmem(feature), in_vmem(second), *map(in_vmem, tails))
    return jnp.transpose(coarse, (1, 0, 2))[:, None]


def solution(mesh):
    return jax.shard_map(
        local,
        mesh=mesh,
        in_specs=(P("filt", ("groups", "space"), None, None), P(), P()),
        out_specs=P(None, ("groups", "space"), "filt", None),
        check_vma=False,
    )
```

time: 66.5 us -> 83.9 us (1.26)
  the two profiles are of different devices: /device:TPU:1 before, /device:TPU:13 now
where the time goes in v4:
time: 83.9 us; the launch traced here: 83.3 us
  starting transfers between devices  39.9 us (48%)
  local copies, waits for them, and re-layouts  27.8 us (33%)
  Pallas kernels  10.8 us (13%)
  waiting for transfers between devices  2.53 us (3%)
  other arithmetic  1.44 us (2%)
    ppermute x6, starting transfers between devices, shifted(): lax.ppermute(block, axis, [(i, i + by) for i in range(count) if 0 <= i +...  34.4 us
    another operation x3, local copies, waits for them, and re-layouts, first_weights(): return jnp.stack([even, odd], axis=1).reshape(3 * 2 * C, 12 * C)  8.32 us
    ppermute x3, starting transfers between devices, local(): lax.ppermute(piece, 'filt', [(i, (i + d) % bands) for i in range(bands)])  5.57 us
    pallas_call x1, Pallas kernels, local(): pl.pallas_call(functools.partial(early_kernel, parts, late, window), out_...  5.56 us
    another operation x1, local copies, waits for them, and re-layouts, local(): first.reshape(6 * C, 12, C)[:, :, C - late:].reshape(6 * C, 12 * late)  3.46 us
    pallas_call x1, Pallas kernels, local(): pl.pallas_call(functools.partial(late_kernel, late, window), out_shape=pl...  2.81 us
    reshape x1, local copies, waits for them, and re-layouts, second_weights(): shaped = down_weight.reshape(3, 3, 3, C2, C)  2.66 us
    ppermute x3, waiting for transfers between devices, local(): lax.ppermute(piece, 'filt', [(i, (i + d) % bands) for i in range(bands)])  2.52 us
  transfers between devices with their start and end apart: 9, of which 1 were waited for; matrix products, arithmetic and copies ran while one was open for 32% of the time, Pallas kernels for 7%

profile of v4, /device:TPU:13, one launch (start us, length us, event | category | flops | bytes accessed | tf_op | source)
XLA Modules:
  0.0 83.3 jit_solution(7528337348284254051)
XLA Ops:
  0.0 1.2 %copy-done = bf16[16,2,32,512]{3,2,1,0:T(8,128)(2,1)S(1)} copy-done((bf16[16,2,32,512]{3,2,1,0:T(8,128)(2,1)S(1)}, bf16[16,2,32,512]{3,2,1,0:T(8,128)(2,1)}, u32[]{:S(2)}) %copy-start) | copy-done | bytes 1048600
  1.2 2.4 %shard_map.37 = (bf16[11,2,16,512]{3,2,1,0:T(8,128)(2,1)S(1)}, bf16[11,2,16,512]{3,2,1,0:T(8,128)(2,1)S(1)}, bf16[11,2,16,512]{3,2,1,0:T(8,128)(2,1)S(1)}, bf16[11,2,16,512]{3,2,1,0:T(8,128)(2,1)}) custom-call(bf16[16,2,32,512]{3,2,1,0:T(8,128)(2,1)S(1)} %copy-done), custom_call_target="tpu_custom_call" | custom-call | tf_op jit(solution)/shard_map/pallas_call | solution.py:179
  3.7 0.2 collective-permute-start.1
  3.8 1.3 %collective-permute-start.4 = (bf16[11,2,16,512]{3,2,1,0:T(8,128)(2,1)S(1)}, bf16[11,2,16,512]{3,2,1,0:T(8,128)(2,1)S(1)}, u32[]{:S(2)}, u32[]{:S(2)}) collective-permute-start(bf16[11,2,16,512]{3,2,1,0:T(8,128)(2,1)S(1)} %get-tuple-element.20), channel_id=1, source_target_pairs={{0,1},{1,2},{2,3},{3,0},{4,5},{5,6},{6,7},{7,4},{8,9},{9,10},{10,1... | collective-permute-start | bytes 1081352 | tf_op jit(solution)/shard_map/ppermute | solution.py:190
  5.1 4.1 %collective-permute-start = (bf16[11,2,16,512]{3,2,1,0:T(8,128)(2,1)}, bf16[11,2,16,512]{3,2,1,0:T(8,128)(2,1)}, u32[]{:S(2)}, u32[]{:S(2)}) collective-permute-start(bf16[11,2,16,512]{3,2,1,0:T(8,128)(2,1)} %get-tuple-element.15), channel_id=1, source_target_pairs={{0,2},{1,3},{2,0},{3,1},{4,6},{5,7},{6,4},{7,5},{8,10},{9,11},{10,... | collective-permute-start | bytes 1081352 | tf_op jit(solution)/shard_map/ppermute | solution.py:190
  9.2 1.2 %reshape.15 = bf16[3,3,3,64,64]{4,3,2,1,0:T(8,128)(2,1)} reshape(bf16[3,3,3,4096]{3,2,1,0:T(4,128)(2,1)S(1)} %copy-done.4) | data formatting | bytes 442368 | tf_op jit(solution)/shard_map/reshape | solution.py:129
  10.4 2.5 %collective-permute-done.1 = bf16[11,2,16,512]{3,2,1,0:T(8,128)(2,1)S(1)} collective-permute-done((bf16[11,2,16,512]{3,2,1,0:T(8,128)(2,1)S(1)}, bf16[11,2,16,512]{3,2,1,0:T(8,128)(2,1)S(1)}, u32[]{:S(2)}, u32[]{:S(2)}) %collective-permute-start.1) | collective-permute-done | bytes 360480 | tf_op jit(solution)/shard_map/ppermute | solution.py:190
  12.9 21.1 %collective-permute-start.2 = (bf16[11,2,16,512]{3,2,1,0:T(8,128)(2,1)S(1)}, bf16[11,2,16,512]{3,2,1,0:T(8,128)(2,1)}, u32[]{:S(2)}, u32[]{:S(2)}) collective-permute-start(bf16[11,2,16,512]{3,2,1,0:T(8,128)(2,1)S(1)} %get-tuple-element.18.refs_0_), channel_id=1, source_target_pairs={{0,4},{4,8},{8,12},{1,5},{5,9},{9,13},{2,6},{6,10},{10,14},{3,7},{... | collective-permute-start | bytes 1081352 | tf_op jit(solution)/shard_map/ppermute | solution.py:145
  34.1 1.9 %collective-permute-start.3 = (bf16[11,2,16,512]{3,2,1,0:T(8,128)(2,1)S(1)}, bf16[11,2,16,512]{3,2,1,0:T(8,128)(2,1)}, u32[]{:S(2)}, u32[]{:S(2)}) collective-permute-start(bf16[11,2,16,512]{3,2,1,0:T(8,128)(2,1)S(1)} %get-tuple-element.18.refs_0_), channel_id=1, source_target_pairs={{4,0},{8,4},{12,8},{5,1},{9,5},{13,9},{6,2},{10,6},{14,10},{7,3},{... | collective-permute-start | bytes 1081352 | tf_op jit(solution)/shard_map/ppermute | solution.py:145
  36.0 0.1 pad_maximum_fusion.1.refs_3_
  36.1 3.6 %collective-permute-start.5 = (bf16[22,2,16,512]{3,2,1,0:T(8,128)(2,1)S(1)}, bf16[22,2,16,512]{3,2,1,0:T(8,128)(2,1)S(1)}, u32[]{:S(2)}, u32[]{:S(2)}) collective-permute-start(bf16[22,2,16,512]{3,2,1,0:T(8,128)(2,1)S(1)} %pad_maximum_fusion.1.refs_3_), channel_id=1, source_target_pairs={{0,4},{4,8},{8,12},{1,5},{5,9},{9,13},{2,6},{6,10},{10,14},{3,7},{... | collective-permute-start | bytes 2162696 | tf_op jit(solution)/shard_map/ppermute | solution.py:145
  39.7 1.9 %collective-permute-start.6 = (bf16[22,2,16,512]{3,2,1,0:T(8,128)(2,1)S(1)}, bf16[22,2,16,512]{3,2,1,0:T(8,128)(2,1)S(1)}, u32[]{:S(2)}, u32[]{:S(2)}) collective-permute-start(bf16[22,2,16,512]{3,2,1,0:T(8,128)(2,1)S(1)} %pad_maximum_fusion.1.refs_3_), channel_id=1, source_target_pairs={{4,0},{8,4},{12,8},{5,1},{9,5},{13,9},{6,2},{10,6},{14,10},{7,3},{... | collective-permute-start | bytes 2162696 | tf_op jit(solution)/shard_map/ppermute | solution.py:145
  41.7 0.6 fusion
  42.3 0.8 rev.3
  43.1 1.4 %pad_bitcast_fusion.1 = (bf16[3,1,64,3,4,64]{2,5,4,3,0,1:T(8,128)(2,1)S(1)}, bf16[3,1,64,3,4,64]{2,5,4,3,0,1:T(8,128)(2,1)S(1)}) fusion(bf16[3,64,3,3,64]{1,4,3,2,0:T(8,128)(2,1)} %rev.3), kind=kLoop, calls=%fused_computation.5 | loop fusion | bytes 811008 | tf_op jit(solution)/shard_map/stack | solution.py:135
  44.4 1.3 %pad_maximum_fusion = bf16[3,2,64,3,4,64]{2,5,4,3,0,1:T(8,128)(2,1)} fusion(bf16[3,1,64,3,4,64]{2,5,4,3,0,1:T(8,128)(2,1)S(1)} %get-tuple-element.26, bf16[3,1,64,3,4,64]{2,5,4,3,0,1:T(8,128)(2,1)S(1)} %get-tuple-element.25), kind=kLoop, calls=%fused_computation.2 | loop fusion | flops 294912 | bytes 1179648 | tf_op jit(solution)/shard_map/stack | solution.py:135
  45.7 3.4 %copy.7 = bf16[3,2,64,3,4,64]{5,4,3,2,1,0:T(4,128)(2,1)} copy(bf16[3,2,64,3,4,64]{2,5,4,3,0,1:T(8,128)(2,1)} %pad_maximum_fusion) | data formatting | bytes 1179648 | tf_op jit(solution)/shard_map/stack | solution.py:135
  49.1 3.5 %copy.9 = bf16[3,2,64,3,4,64]{2,1,0,5,4,3:T(2,128)(2,1)} copy(bf16[3,2,64,3,4,64]{2,5,4,3,0,1:T(8,128)(2,1)} %pad_maximum_fusion) | data formatting | bytes 1179648 | tf_op jit(solution)/shard_map/stack | solution.py:135
  52.7 2.2 %reshape.16.first_ref = bf16[384,768]{1,0:T(8,128)(2,1)S(1)} reshape(bf16[3,2,64,3,4,64]{5,4,3,2,1,0:T(4,128)(2,1)} %copy.7) | data formatting | bytes 1179648 | tf_op jit(solution)/shard_map/reshape | solution.py:135
  54.9 2.7 %reshape.17 = bf16[3,3,3,128,64]{4,3,2,1,0:T(8,128)(2,1)} reshape(bf16[3,3,3,8192]{3,2,1,0:T(4,128)(2,1)} %param.5) | data formatting | bytes 884736 | tf_op jit(solution)/shard_map/reshape | solution.py:139
  57.6 2.2 %copy.8 = bf16[128,3,3,3,64]{0,4,3,2,1:T(8,128)(2,1)} copy(bf16[128,3,3,3,64]{4,0,3,1,2:T(8,128)(2,1)} %bitcast.23) | data formatting | bytes 884736 | tf_op jit(solution)/shard_map/transpose | solution.py:140
  59.8 3.5 %reshape_reshape.3 = bf16[384,12,64]{0,2,1:T(8,128)(2,1)} reshape(bf16[3,2,64,3,4,64]{2,1,0,5,4,3:T(2,128)(2,1)} %copy.9) | data formatting | bytes 1179648 | tf_op jit(solution)/shard_map/reshape;reshape | solution.py:195
  63.2 1.6 %slice.4 = bf16[384,12,16]{0,2,1:T(8,128)(2,1)} slice(bf16[384,12,64]{0,2,1:T(8,128)(2,1)} %reshape_reshape.3), slice={[0:384], [0:12], [48:64]} | slice | bytes 294912 | tf_op jit(solution)/shard_map/slice | solution.py:195
  64.8 3.6 %collective-permute-start.7 = (bf16[11,2,16,512]{3,2,1,0:T(8,128)(2,1)}, bf16[11,2,16,512]{3,2,1,0:T(8,128)(2,1)}, u32[]{:S(2)}, u32[]{:S(2)}) collective-permute-start(bf16[11,2,16,512]{3,2,1,0:T(8,128)(2,1)} %collective-permute-done.refs_6_), channel_id=1, source_target_pairs={{0,4},{4,8},{8,12},{1,5},{5,9},{9,13},{2,6},{6,10},{10,14},{3,7},{... | collective-permute-start | bytes 1081352 | tf_op jit(solution)/shard_map/ppermute | solution.py:145
  68.5 2.1 %collective-permute-start.8 = (bf16[11,2,16,512]{3,2,1,0:T(8,128)(2,1)}, bf16[11,2,16,512]{3,2,1,0:T(8,128)(2,1)}, u32[]{:S(2)}, u32[]{:S(2)}) collective-permute-start(bf16[11,2,16,512]{3,2,1,0:T(8,128)(2,1)} %collective-permute-done.refs_6_), channel_id=1, source_target_pairs={{4,0},{8,4},{12,8},{5,1},{9,5},{13,9},{6,2},{10,6},{14,10},{7,3},{... | collective-permute-start | bytes 1081352 | tf_op jit(solution)/shard_map/ppermute | solution.py:145
  70.6 0.1 pad_add_fusion.edge_ref
  70.7 1.2 %copy.10.second_ref = bf16[128,1728]{1,0:T(8,128)(2,1)S(1)} copy(bf16[128,1728]{0,1:T(8,128)(2,1)} %bitcast.24) | data formatting | bytes 884736 | tf_op jit(solution)/shard_map/optimization_barrier | solution.py:205
  71.9 1.0 %copy.11.refs_0_ = bf16[384,192]{1,0:T(8,128)(2,1)S(1)} copy(bf16[384,192]{0,1:T(8,128)(2,1)} %bitcast.25) | data formatting | bytes 294912 | tf_op jit(solution)/shard_map/optimization_barrier | solution.py:205
  73.0 1.0 %copy-done.2 = bf16[11,2,16,512]{3,2,1,0:T(8,128)(2,1)S(1)} copy-done((bf16[11,2,16,512]{3,2,1,0:T(8,128)(2,1)S(1)}, bf16[11,2,16,512]{3,2,1,0:T(8,128)(2,1)}, u32[]{:S(2)}) %copy-start.2) | copy-done | bytes 360472
  74.0 5.6 %shard_map.38.feature_ref = f32[3456,256]{1,0:T(8,128)S(1)} custom-call(bf16[384,768]{1,0:T(8,128)(2,1)S(1)} %reshape.16.first_ref, bf16[11,2,16,512]{3,2,1,0:T(8,128)(2,1)S(1)} %copy-done.2, bf16[11,2,16,512]{3,2,1,0:T(8,128)(2,1)} %collective-permute-done.2.refs_1_, bf16[11,2,16,512]{3,2,1,0:T(8,128)(2,1)} %collective-permute-done.3.refs_2_, ...), custom_call_target="tpu_custom_call" | custom-call | tf_op jit(solution)/shard_map/pallas_call | solution.py:219
  79.5 2.8 %shard_map.39 = bf16[4,128,256]{2,1,0:T(8,128)(2,1)S(1)} custom-call(s32[2]{0:T(128)S(1)} %pad_add_fusion.edge_ref, f32[3456,256]{1,0:T(8,128)S(1)} %shard_map.38.feature_ref, bf16[128,1728]{1,0:T(8,128)(2,1)S(1)} %copy.10.second_ref, bf16[384,192]{1,0:T(8,128)(2,1)S(1)} %copy.11.refs_0_, bf16[11,2,16,512]{3,2,1,0:T(8,128)(2,1)} %collective-permute-done.7.refs_1_, ...), custom_call_target="tpu_custom_call" | custom-call | tf_op jit(solution)/shard_map/pallas_call | solution.py:227
  82.4 0.9 %copy.12 = bf16[128,1,4,256]{3,2,1,0:T(4,128)(2,1)} copy(bf16[128,1,4,256]{3,0,2,1:T(8,128)(2,1)S(1)} %bitcast.22) | data formatting | bytes 524288 | tf_op jit(solution)/shard_map/broadcast_in_dim | solution.py:236
  (19 shorter events, 0.1 us)
Async XLA Ops:
  0.0 1.2 %copy-start = (bf16[16,2,32,512]{3,2,1,0:T(8,128)(2,1)S(1)}, bf16[16,2,32,512]{3,2,1,0:T(8,128)(2,1)}, u32[]{:S(2)}) copy-start(bf16[16,2,32,512]{3,2,1,0:T(8,128)(2,1)} %volume_ref.1) | copy-start | bytes 3145732
  1.2 8.0 %copy-start.4 = (bf16[3,3,3,4096]{3,2,1,0:T(4,128)(2,1)S(1)}, bf16[3,3,3,4096]{3,2,1,0:T(4,128)(2,1)}, u32[]{:S(2)}) copy-start(bf16[3,3,3,4096]{3,2,1,0:T(4,128)(2,1)} %param.4) | copy-start | bytes 663556
  3.7 38.6 %copy-start.1 = (bf16[11,2,16,512]{3,2,1,0:T(8,128)(2,1)}, bf16[11,2,16,512]{3,2,1,0:T(8,128)(2,1)S(1)}, u32[]{:S(2)}) copy-start(bf16[11,2,16,512]{3,2,1,0:T(8,128)(2,1)S(1)} %get-tuple-element.18.refs_0_) | copy-start | bytes 1081348
  3.7 9.3 %collective-permute-start.1 = (bf16[11,2,16,512]{3,2,1,0:T(8,128)(2,1)S(1)}, bf16[11,2,16,512]{3,2,1,0:T(8,128)(2,1)S(1)}, u32[]{:S(2)}, u32[]{:S(2)}) collective-permute-start(bf16[11,2,16,512]{3,2,1,0:T(8,128)(2,1)S(1)} %get-tuple-element.17), channel_id=1, source_target_pairs={{0,3},{1,0},{2,1},{3,2},{4,7},{5,4},{6,5},{7,6},{8,11},{9,8},{10,9... | collective-permute-start | bytes 1081352 | tf_op jit(solution)/shard_map/ppermute | solution.py:190
  3.8 32.2 %collective-permute-start.4 = (bf16[11,2,16,512]{3,2,1,0:T(8,128)(2,1)S(1)}, bf16[11,2,16,512]{3,2,1,0:T(8,128)(2,1)S(1)}, u32[]{:S(2)}, u32[]{:S(2)}) collective-permute-start(bf16[11,2,16,512]{3,2,1,0:T(8,128)(2,1)S(1)} %get-tuple-element.20), channel_id=1, source_target_pairs={{0,1},{1,2},{2,3},{3,0},{4,5},{5,6},{6,7},{7,4},{8,9},{9,10},{10,1... | collective-permute-start | bytes 1081352 | tf_op jit(solution)/shard_map/ppermute | solution.py:190
  5.1 59.7 %collective-permute-start = (bf16[11,2,16,512]{3,2,1,0:T(8,128)(2,1)}, bf16[11,2,16,512]{3,2,1,0:T(8,128)(2,1)}, u32[]{:S(2)}, u32[]{:S(2)}) collective-permute-start(bf16[11,2,16,512]{3,2,1,0:T(8,128)(2,1)} %get-tuple-element.15), channel_id=1, source_target_pairs={{0,2},{1,3},{2,0},{3,1},{4,6},{5,7},{6,4},{7,5},{8,10},{9,11},{10,... | collective-permute-start | bytes 1081352 | tf_op jit(solution)/shard_map/ppermute | solution.py:190
  10.4 31.3 %copy-start.3 = (bf16[3,3,3,64,64]{4,3,2,1,0:T(8,128)(2,1)S(1)}, bf16[3,3,3,64,64]{4,3,2,1,0:T(8,128)(2,1)}, u32[]{:S(2)}) copy-start(bf16[3,3,3,64,64]{4,3,2,1,0:T(8,128)(2,1)} %reshape.15) | copy-start | bytes 663556
  12.9 51.9 %collective-permute-start.2 = (bf16[11,2,16,512]{3,2,1,0:T(8,128)(2,1)S(1)}, bf16[11,2,16,512]{3,2,1,0:T(8,128)(2,1)}, u32[]{:S(2)}, u32[]{:S(2)}) collective-permute-start(bf16[11,2,16,512]{3,2,1,0:T(8,128)(2,1)S(1)} %get-tuple-element.18.refs_0_), channel_id=1, source_target_pairs={{0,4},{4,8},{8,12},{1,5},{5,9},{9,13},{2,6},{6,10},{10,14},{3,7},{... | collective-permute-start | bytes 1081352 | tf_op jit(solution)/shard_map/ppermute | solution.py:145
  34.1 30.8 %collective-permute-start.3 = (bf16[11,2,16,512]{3,2,1,0:T(8,128)(2,1)S(1)}, bf16[11,2,16,512]{3,2,1,0:T(8,128)(2,1)}, u32[]{:S(2)}, u32[]{:S(2)}) collective-permute-start(bf16[11,2,16,512]{3,2,1,0:T(8,128)(2,1)S(1)} %get-tuple-element.18.refs_0_), channel_id=1, source_target_pairs={{4,0},{8,4},{12,8},{5,1},{9,5},{13,9},{6,2},{10,6},{14,10},{7,3},{... | collective-permute-start | bytes 1081352 | tf_op jit(solution)/shard_map/ppermute | solution.py:145
  36.1 36.9 %collective-permute-start.5 = (bf16[22,2,16,512]{3,2,1,0:T(8,128)(2,1)S(1)}, bf16[22,2,16,512]{3,2,1,0:T(8,128)(2,1)S(1)}, u32[]{:S(2)}, u32[]{:S(2)}) collective-permute-start(bf16[22,2,16,512]{3,2,1,0:T(8,128)(2,1)S(1)} %pad_maximum_fusion.1.refs_3_), channel_id=1, source_target_pairs={{0,4},{4,8},{8,12},{1,5},{5,9},{9,13},{2,6},{6,10},{10,14},{3,7},{... | collective-permute-start | bytes 2162696 | tf_op jit(solution)/shard_map/ppermute | solution.py:145
  39.7 33.2 %collective-permute-start.6 = (bf16[22,2,16,512]{3,2,1,0:T(8,128)(2,1)S(1)}, bf16[22,2,16,512]{3,2,1,0:T(8,128)(2,1)S(1)}, u32[]{:S(2)}, u32[]{:S(2)}) collective-permute-start(bf16[22,2,16,512]{3,2,1,0:T(8,128)(2,1)S(1)} %pad_maximum_fusion.1.refs_3_), channel_id=1, source_target_pairs={{4,0},{8,4},{12,8},{5,1},{9,5},{13,9},{6,2},{10,6},{14,10},{7,3},{... | collective-permute-start | bytes 2162696 | tf_op jit(solution)/shard_map/ppermute | solution.py:145
  64.8 14.7 %collective-permute-start.7 = (bf16[11,2,16,512]{3,2,1,0:T(8,128)(2,1)}, bf16[11,2,16,512]{3,2,1,0:T(8,128)(2,1)}, u32[]{:S(2)}, u32[]{:S(2)}) collective-permute-start(bf16[11,2,16,512]{3,2,1,0:T(8,128)(2,1)} %collective-permute-done.refs_6_), channel_id=1, source_target_pairs={{0,4},{4,8},{8,12},{1,5},{5,9},{9,13},{2,6},{6,10},{10,14},{3,7},{... | collective-permute-start | bytes 1081352 | tf_op jit(solution)/shard_map/ppermute | solution.py:145
  68.5 11.1 %collective-permute-start.8 = (bf16[11,2,16,512]{3,2,1,0:T(8,128)(2,1)}, bf16[11,2,16,512]{3,2,1,0:T(8,128)(2,1)}, u32[]{:S(2)}, u32[]{:S(2)}) collective-permute-start(bf16[11,2,16,512]{3,2,1,0:T(8,128)(2,1)} %collective-permute-done.refs_6_), channel_id=1, source_target_pairs={{4,0},{8,4},{12,8},{5,1},{9,5},{13,9},{6,2},{10,6},{14,10},{7,3},{... | collective-permute-start | bytes 1081352 | tf_op jit(solution)/shard_map/ppermute | solution.py:145
  73.0 1.0 %copy-start.2 = (bf16[11,2,16,512]{3,2,1,0:T(8,128)(2,1)S(1)}, bf16[11,2,16,512]{3,2,1,0:T(8,128)(2,1)}, u32[]{:S(2)}) copy-start(bf16[11,2,16,512]{3,2,1,0:T(8,128)(2,1)} %copy-done.1) | copy-start | bytes 1081348

commit v5 on v4

--- a/solution.py
+++ b/solution.py
@@ -70,14 +70,13 @@
         total[z] = piece if total[z] is None else total[z] + piece
 
 
-def early_kernel(parts, late, window, first_ref, *refs):
+def early_kernel(parts, late, window, places_ref, first_ref, *refs):
     blocks, (out_ref, taps_ref) = refs[:-2], refs[-2:]
     half = out_ref.shape[1]
-    for i, row, at, planes in parts:
+    for i, row, at, held in parts:
         for r in range(window):
-            for k, p in enumerate(planes):
-                if p is not None:
-                    store_taps(taps_ref.at[p], r, at, C, blocks[i][row + r, k])
+            for k in range(2):
+                store_taps(taps_ref.at[places_ref[2 * held + k]], r, at, C, blocks[i][row + r, k])
     if late:
         empty = jnp.zeros((late, half), jnp.bfloat16)
         for p in (0, 1, 4):
@@ -95,11 +94,12 @@
     out_ref, hid_ref = refs[-2:] if not late else refs[-3:-1]
     half = out_ref.shape[2]
     if late:
-        weight_ref, below_ref, above_ref, taps_ref = refs[0], refs[1], refs[2], refs[-1]
-        for r in range(window):
-            store_taps(taps_ref.at[0], r, 0, late, below_ref[r, 0])
-            store_taps(taps_ref.at[1], r, 0, late, below_ref[r, 1])
-            store_taps(taps_ref.at[2], r, 0, late, above_ref[r, 0])
+        weight_ref, taps_ref = refs[0], refs[-1]
+        for i in range(2):
+            for r in range(window):
+                for k in range(2):
+                    place = edge_ref[2 + 2 * i + k]
+                    store_taps(taps_ref.at[place], r, 0, late, refs[1 + i][r, k])
     size = 2 * C
     lane = lax.broadcasted_iota(jnp.int32, (C, half), 1)
     for y in range(window - 2):
@@ -121,28 +121,71 @@
             hid_ref[pl.ds(base + C, 2 * C), :] = value
     for y in range(out_ref.shape[0]):
         out_ref[y] = jnp.dot(
-            second_ref[...], hid_ref[pl.ds(2 * y * 9 * C, 27 * C), :], preferred_element_type=jnp.float32
+            second_ref[:, : 27 * C], hid_ref[pl.ds(2 * y * 9 * C, 27 * C), :], preferred_element_type=jnp.float32
         ).astype(jnp.bfloat16)
 
 
-def first_weights(conv_weight, turn):
-    shaped = conv_weight.reshape(3, 3, 3, C, C)
-    if turn is not None:
-        shaped = jnp.dot(shaped, turn, preferred_element_type=jnp.float32).astype(jnp.bfloat16)
-    shaped = jnp.transpose(shaped, (0, 3, 1, 2, 4))[::-1]
-    even = jnp.pad(shaped, ((0, 0), (0, 0), (0, 0), (0, 1), (0, 0)))
-    odd = jnp.pad(shaped, ((0, 0), (0, 0), (0, 0), (1, 0), (0, 0)))
-    return jnp.stack([even, odd], axis=1).reshape(3 * 2 * C, 12 * C)
-
-
-def second_weights(down_weight):
-    shaped = down_weight.reshape(3, 3, 3, C2, C)
-    return jnp.transpose(shaped, (3, 1, 0, 2, 4)).reshape(C2, 27 * C)
-
-
-def shifted(block, axis, by):
+def exact(left, right):
+    return jnp.dot(left, right, preferred_element_type=jnp.float32)
+
+
+def weight_kernel(distances, conv_ref, down_ref, first_ref, second_ref, *refs):
+    row = lax.broadcasted_iota(jnp.int32, (C, 2 * C), 0)
+    lane = lax.broadcasted_iota(jnp.int32, (C, 2 * C), 1)
+    low, high = (row == lane).astype(jnp.bfloat16), (row == lane - C).astype(jnp.bfloat16)
+    for j in range(14):
+        total = None
+        for t, place in ((2 * j, low), (2 * j + 1, high)):
+            if t < 27:
+                tap = down_ref[t // 3 % 3 * 9 + t // 9 * 3 + t % 3]
+                part = exact(tap, place)
+                total = part if total is None else total + part
+        second_ref[:, pl.ds(2 * C * j, 2 * C)] = total.astype(jnp.bfloat16)
+    if distances:
+        me, bands = lax.axis_index("filt"), len(distances)
+        count = C // bands
+        block, inside = lane % C // count, lane % count
+        source = jnp.zeros_like(lane)
+        for i, d in enumerate(distances):
+            source = jnp.where(block == i, lax.rem(me - d + bands, bands), source)
+        wanted = row == source * count + inside
+        low, high = [(wanted & (lane // C == k)).astype(jnp.bfloat16) for k in range(2)]
+    for a in range(3):
+        taps = [jnp.concatenate([conv_ref[9 * a + 3 * b + c] for b in range(3)]) for c in range(3)]
+        lows, highs = [[exact(tap, place) for tap in taps] for place in (low, high)]
+        tiles = ((lows[0] + highs[1], lows[2]), (highs[0], lows[1] + highs[2]))
+        for parity in range(2):
+            for k in range(2):
+                tile = tiles[parity][k].astype(jnp.bfloat16)
+                for b in range(3):
+                    at = (2 - a) * 2 * C + parity * C
+                    first_ref[pl.ds(at, C), pl.ds((2 * b + k) * 2 * C, 2 * C)] = tile[b * C : (b + 1) * C]
+    if distances:
+        last_ref = refs[0]
+        row = lax.broadcasted_iota(jnp.int32, (C, 12 * count), 0)
+        lane = lax.broadcasted_iota(jnp.int32, (C, 12 * count), 1)
+        source = lax.rem(me - distances[-1] + bands, bands) * count
+        for parity in range(2):
+            total = None
+            for b in range(3):
+                for c in range(3):
+                    taps = jnp.concatenate([conv_ref[9 * a + 3 * b + c] for a in range(3)])
+                    at = (4 * b + c + parity) * count
+                    place = (lane >= at) & (lane < at + count) & (row == source + lane - at)
+                    part = exact(taps, place.astype(jnp.bfloat16))
+                    total = part if total is None else total + part
+            total = total.astype(jnp.bfloat16)
+            for a in range(3):
+                last_ref[pl.ds((2 - a) * 2 * C + parity * C, C), :] = total[a * C : (a + 1) * C]
+
+
+def swapped(block, axis):
     count = lax.axis_size(axis)
-    return lax.ppermute(block, axis, [(i, i + by) for i in range(count) if 0 <= i + by < count])
+    results = []
+    for start in (0, 1):
+        pairs = [(i, i + 1) for i in range(start, count - 1, 2)]
+        results.append(lax.ppermute(block, axis, pairs + [(j, i) for i, j in pairs]))
+    return results
 
 
 def after(value, *others):
@@ -151,14 +194,6 @@
 
 def in_vmem(value):
     return pltpu.with_memory_space_constraint(value, pltpu.VMEM)
-
-
-def block_order(me, distances, bands, count):
-    row = lax.broadcasted_iota(jnp.int32, (C, C), 0)
-    column = lax.broadcasted_iota(jnp.int32, (C, C), 1)
-    piece = column // count
-    source = sum(jnp.where(piece == i, lax.rem(me - d + bands, bands), 0) for i, d in enumerate(distances))
-    return (row == source * count + column % count).astype(jnp.bfloat16)
 
 
 def local(volume, conv_weight, down_weight):
@@ -169,13 +204,26 @@
     band = all_rows // bands
     window = BELOW + band + ABOVE
     half = width // 2
+    hid_rows = band + 1
     vmem = pl.BlockSpec(memory_space=pltpu.VMEM)
     smem = pl.BlockSpec(memory_space=pltpu.SMEM)
     params = pltpu.CompilerParams(vmem_limit_bytes=VMEM_LIMIT)
-    second = second_weights(down_weight)
-    below, inside, above = (0, 1), (2, 3), (4, None)
-    if count == 16 and bands == 4:
-        distances = (0, 3, 1, 2)
+    direct = count == 16 and bands == 4
+    distances = (0, 3, 1, 2) if direct else ()
+    late = count if direct else 0
+    lay = pl.pallas_call(
+        functools.partial(weight_kernel, distances),
+        out_shape=[
+            pltpu.VMEM((6 * C, 12 * C), jnp.bfloat16),
+            pltpu.VMEM((C2, 28 * C), jnp.bfloat16),
+        ]
+        + [pltpu.VMEM((6 * C, 12 * late), jnp.bfloat16)] * direct,
+        in_specs=[vmem] * 2,
+        out_specs=[vmem] * (3 if direct else 2),
+        compiler_params=params,
+    )
+    first, second, *last = lay(conv_weight.reshape(27, C, C), down_weight.reshape(27, C2, C))
+    if direct:
         sent = pl.pallas_call(
             functools.partial(send_kernel, band, distances),
             out_shape=[pltpu.VMEM((window, planes, count, width), jnp.bfloat16)] * bands,
@@ -186,24 +234,22 @@
             ],
             compiler_params=params,
         )(volume)
-        own = [
-            lax.ppermute(piece, "filt", [(i, (i + d) % bands) for i in range(bands)]) if d else piece
-            for d, piece in zip(distances, sent)
-        ]
-        first = first_weights(conv_weight, block_order(me, distances, bands, count))
-        late = count
-        last = first.reshape(6 * C, 12, C)[:, :, C - late :].reshape(6 * C, 12 * late)
-        mine = after(own[0], own[1])
+        own = []
+        for d, piece in zip(distances, sent):
+            if d == 2:
+                piece = after(piece, own[1])
+            if d:
+                piece = lax.ppermute(piece, "filt", [(i, (i + d) % bands) for i in range(bands)])
+            own.append(piece)
+        mine = swapped(after(own[0], first), "space")
         middle = jnp.concatenate(own[1:3])
-        middle = after(middle, own[1])
-        blocks = [own[0], shifted(mine, "space", 1), shifted(mine, "space", -1)]
-        blocks += [middle, shifted(middle, "space", 1), shifted(middle, "space", -1), own[3]]
+        middles = swapped(middle, "space")
+        tails = last + swapped(after(own[3], *mine), "space")
+        blocks = [own[0], *mine, middle, *middles, own[3]]
         parts = []
-        for i, held in enumerate((inside, below, above)):
-            parts += [(i, 0, 0, held), (3 + i, 0, count, held), (3 + i, window, 2 * count, held)]
-        parts.append((6, 0, 3 * count, inside))
-        tail, first, second, last = lax.optimization_barrier((own[3], first, second, last, *blocks[1:3]))[:4]
-        tails = [last, shifted(tail, "space", 1), shifted(tail, "space", -1)]
+        for held in range(3):
+            parts += [(held, 0, 0, held), (3 + held, 0, count, held), (3 + held, window, 2 * count, held)]
+        parts.append((6, 0, 3 * count, 0))
     else:
         field = jnp.transpose(volume, (2, 1, 0, 3))
         field = jnp.concatenate([field[..., ::2], field[..., 1::2]], axis=-1)
@@ -211,28 +257,34 @@
         sent = jnp.stack([field[t * band : t * band + window] for t in range(bands)])
         got = lax.all_to_all(sent, "filt", split_axis=0, concat_axis=0, tiled=True)
         own = jnp.transpose(got, (1, 2, 0, 3, 4)).reshape(window, planes, C, width)
-        first = first_weights(conv_weight, None)
-        blocks = [own, shifted(own, "space", 1), shifted(own, "space", -1)]
-        parts = [(i, 0, 0, held) for i, held in enumerate((inside, below, above))]
-        late, tails = 0, []
-    hid_rows = band + 1
+        blocks = [own, *swapped(own, "space")]
+        parts = [(held, 0, 0, held) for held in range(3)]
+        tails = []
+    even = space % 2 == 0
+    places = [jnp.where(even, p, q) for p, q in ((4, 0), (5, 1), (0, 4), (1, 5))]
+    slots = [jnp.where(even, p, q) for p, q in ((2, 0), (3, 1), (0, 2), (1, 3))]
     feature = pl.pallas_call(
         functools.partial(early_kernel, parts, late, window),
         out_shape=pltpu.VMEM((hid_rows * 6 * C, half), jnp.float32),
-        in_specs=[vmem] * (1 + len(blocks)),
+        in_specs=[smem] + [vmem] * (1 + len(blocks)),
         out_specs=vmem,
-        scratch_shapes=[pltpu.VMEM((5, window * 4 * C, half), jnp.bfloat16)],
+        scratch_shapes=[pltpu.VMEM((6, window * 4 * C, half), jnp.bfloat16)],
         compiler_params=params,
-    )(in_vmem(first), *map(in_vmem, blocks))
+    )(jnp.stack([2, 3, *places]).astype(jnp.int32), in_vmem(first), *map(in_vmem, blocks))
     coarse = pl.pallas_call(
         functools.partial(late_kernel, late, window),
         out_shape=pltpu.VMEM((band // 2, C2, half), jnp.bfloat16),
         in_specs=[smem] + [vmem] * (2 + len(tails)),
         out_specs=vmem,
         scratch_shapes=[pltpu.VMEM((hid_rows * 9 * C, half), jnp.bfloat16)]
-        + [pltpu.VMEM((3, window * 4 * late, half), jnp.bfloat16)] * (late > 0),
+        + [pltpu.VMEM((4, window * 4 * late, half), jnp.bfloat16)] * direct,
         compiler_params=params,
-    )(jnp.stack([space, me]), in_vmem(feature), in_vmem(second), *map(in_vmem, tails))
+    )(
+        jnp.stack([space, me, *slots]).astype(jnp.int32),
+        in_vmem(feature),
+        in_vmem(second),
+        *map(in_vmem, tails),
+    )
     return jnp.transpose(coarse, (1, 0, 2))[:, None]
 
 

time: 83.9 us -> 56.7 us (0.68)
  the two profiles are of different devices: /device:TPU:13 before, /device:TPU:1 now
where the time goes in v5:
time: 56.7 us; the launch traced here: 56.3 us
  starting transfers between devices  18.3 us (32%)
  waiting for transfers between devices  13.9 us (25%)
  Pallas kernels  12.9 us (23%)
  local copies, waits for them, and re-layouts  11 us (19%)
    ppermute x3, waiting for transfers between devices, local(): lax.ppermute(piece, 'filt', [(i, (i + d) % bands) for i in range(bands)])  13.9 us
    ppermute x6, starting transfers between devices, swapped(): lax.ppermute(block, axis, pairs + [(j, i) for i, j in pairs])  13.4 us
    pallas_call x1, Pallas kernels, local(): pl.pallas_call(functools.partial(early_kernel, parts, late, window), out_...  6.47 us
    unnamed x11, local copies, waits for them, and re-layouts  5.71 us
    ppermute x3, starting transfers between devices, local(): lax.ppermute(piece, 'filt', [(i, (i + d) % bands) for i in range(bands)])  4.95 us
    pallas_call x1, Pallas kernels, local(): pl.pallas_call(functools.partial(late_kernel, late, window), out_shape=pl...  2.97 us
    pallas_call x1, Pallas kernels, local(): pl.pallas_call(functools.partial(send_kernel, band, distances), out_shape...  2.54 us
    reshape x1, local copies, waits for them, and re-layouts, local(): down_weight.reshape(27, C2, C)  1.88 us
  transfers between devices with their start and end apart: 9, of which 2 were waited for; matrix products, arithmetic and copies ran while one was open for 10% of the time, Pallas kernels for 13%

profile of v5, /device:TPU:1, one launch (start us, length us, event | category | flops | bytes accessed | tf_op | source)
XLA Modules:
  0.0 56.3 jit_solution(14232820844373837613)
XLA Ops:
  0.0 1.2 %copy-done = bf16[16,2,32,512]{3,2,1,0:T(8,128)(2,1)S(1)} copy-done((bf16[16,2,32,512]{3,2,1,0:T(8,128)(2,1)S(1)}, bf16[16,2,32,512]{3,2,1,0:T(8,128)(2,1)}, u32[]{:S(2)}) %copy-start) | copy-done | bytes 1048600
  1.2 2.5 %shard_map.38 = (bf16[11,2,16,512]{3,2,1,0:T(8,128)(2,1)}, bf16[11,2,16,512]{3,2,1,0:T(8,128)(2,1)S(1)}, bf16[11,2,16,512]{3,2,1,0:T(8,128)(2,1)S(1)}, bf16[11,2,16,512]{3,2,1,0:T(8,128)(2,1)}) custom-call(bf16[16,2,32,512]{3,2,1,0:T(8,128)(2,1)S(1)} %copy-done), custom_call_target="tpu_custom_call" | custom-call | tf_op jit(solution)/shard_map/pallas_call | solution.py:227
  3.8 4.2 %collective-permute-start.2 = (bf16[11,2,16,512]{3,2,1,0:T(8,128)(2,1)S(1)}, bf16[11,2,16,512]{3,2,1,0:T(8,128)(2,1)}, u32[]{:S(2)}, u32[]{:S(2)}) collective-permute-start(bf16[11,2,16,512]{3,2,1,0:T(8,128)(2,1)S(1)} %get-tuple-element.18), channel_id=1, source_target_pairs={{0,3},{1,0},{2,1},{3,2},{4,7},{5,4},{6,5},{7,6},{8,11},{9,8},{10,9... | collective-permute-start | bytes 1081352 | tf_op jit(solution)/shard_map/ppermute | solution.py:242
  7.9 0.0 collective-permute-start.3
  7.9 1.4 %reshape.6.conv_ref = bf16[27,64,64]{2,1,0:T(8,128)(2,1)S(1)} reshape(bf16[3,3,3,4096]{3,2,1,0:T(4,128)(2,1)} %param.4) | data formatting | bytes 442368 | tf_op jit(solution)/shard_map/reshape | solution.py:225
  9.3 1.9 %reshape.7.down_ref = bf16[27,128,64]{2,1,0:T(8,128)(2,1)S(1)} reshape(bf16[3,3,3,8192]{3,2,1,0:T(4,128)(2,1)} %param.5) | data formatting | bytes 884736 | tf_op jit(solution)/shard_map/reshape | solution.py:225
  11.2 0.9 %shard_map.37 = (bf16[384,768]{1,0:T(8,128)(2,1)S(1)}, bf16[128,1792]{1,0:T(8,128)(2,1)S(1)}, bf16[384,192]{1,0:T(8,128)(2,1)S(1)}) custom-call(bf16[27,64,64]{2,1,0:T(8,128)(2,1)S(1)} %reshape.6.conv_ref, bf16[27,128,64]{2,1,0:T(8,128)(2,1)S(1)} %reshape.7.down_ref), custom_call_target="tpu_custom_call" | custom-call | tf_op jit(solution)/shard_map/pallas_call | solution.py:225
  12.1 1.0 %collective-permute-start = (bf16[11,2,16,512]{3,2,1,0:T(8,128)(2,1)}, bf16[11,2,16,512]{3,2,1,0:T(8,128)(2,1)S(1)}, u32[]{:S(2)}, u32[]{:S(2)}) collective-permute-start(bf16[11,2,16,512]{3,2,1,0:T(8,128)(2,1)} %get-tuple-element.17.refs_0_), channel_id=1, source_target_pairs={{0,4},{8,12},{4,0},{12,8},{1,5},{9,13},{5,1},{13,9},{2,6},{10,14},... | collective-permute-start | bytes 1081352 | tf_op jit(solution)/shard_map/ppermute | solution.py:187
  13.1 3.0 %collective-permute-start.1 = (bf16[11,2,16,512]{3,2,1,0:T(8,128)(2,1)}, bf16[11,2,16,512]{3,2,1,0:T(8,128)(2,1)S(1)}, u32[]{:S(2)}, u32[]{:S(2)}) collective-permute-start(bf16[11,2,16,512]{3,2,1,0:T(8,128)(2,1)} %get-tuple-element.17.refs_0_), channel_id=1, source_target_pairs={{4,8},{8,4},{5,9},{9,5},{6,10},{10,6},{7,11},{11,7},{20,24},{24,20... | collective-permute-start | bytes 1081352 | tf_op jit(solution)/shard_map/ppermute | solution.py:187
  16.2 0.0 collective-permute-done.2
  16.2 0.8 %collective-permute-start.6 = (bf16[11,2,16,512]{3,2,1,0:T(8,128)(2,1)}, bf16[11,2,16,512]{3,2,1,0:T(8,128)(2,1)}, u32[]{:S(2)}, u32[]{:S(2)}) collective-permute-start(bf16[11,2,16,512]{3,2,1,0:T(8,128)(2,1)} %get-tuple-element.21), channel_id=1, source_target_pairs={{0,2},{1,3},{2,0},{3,1},{4,6},{5,7},{6,4},{7,5},{8,10},{9,11},{10,... | collective-permute-start | bytes 1081352 | tf_op jit(solution)/shard_map/ppermute | solution.py:242
  17.0 1.0 %constant_dynamic-update-slice_fusion.1 = bf16[22,2,16,512]{3,2,1,0:T(8,128)(2,1)S(1)} fusion(bf16[11,2,16,512]{3,2,1,0:T(8,128)(2,1)} %collective-permute-done.2), kind=kLoop, calls=%fused_computation.1 | loop fusion | bytes 720896
  18.0 5.8 %collective-permute-done.3 = bf16[11,2,16,512]{3,2,1,0:T(8,128)(2,1)} collective-permute-done((bf16[11,2,16,512]{3,2,1,0:T(8,128)(2,1)S(1)}, bf16[11,2,16,512]{3,2,1,0:T(8,128)(2,1)}, u32[]{:S(2)}, u32[]{:S(2)}) %collective-permute-start.3) | collective-permute-done | bytes 360480 | tf_op jit(solution)/shard_map/ppermute | solution.py:242
  23.8 1.0 %constant_dynamic-update-slice_fusion.refs_3_ = bf16[22,2,16,512]{3,2,1,0:T(8,128)(2,1)S(1)} fusion(bf16[22,2,16,512]{3,2,1,0:T(8,128)(2,1)S(1)} %constant_dynamic-update-slice_fusion.1, bf16[11,2,16,512]{3,2,1,0:T(8,128)(2,1)} %collective-permute-done.3), kind=kLoop, calls=%fused_computation | loop fusion | bytes 720896 | tf_op jit(solution)/shard_map/concatenate | solution.py:245
  24.8 2.8 %collective-permute-start.4 = (bf16[22,2,16,512]{3,2,1,0:T(8,128)(2,1)S(1)}, bf16[22,2,16,512]{3,2,1,0:T(8,128)(2,1)S(1)}, u32[]{:S(2)}, u32[]{:S(2)}) collective-permute-start(bf16[22,2,16,512]{3,2,1,0:T(8,128)(2,1)S(1)} %constant_dynamic-update-slice_fusion.refs_3_), channel_id=1, source_target_pairs={{0,4},{8,12},{4,0},{12,8},{1,5},{9,13},{5,1},{13,9},{2,6},{10,14},... | collective-permute-start | bytes 2162696 | tf_op jit(solution)/shard_map/ppermute | solution.py:187
  27.6 3.0 %collective-permute-start.5 = (bf16[22,2,16,512]{3,2,1,0:T(8,128)(2,1)S(1)}, bf16[22,2,16,512]{3,2,1,0:T(8,128)(2,1)S(1)}, u32[]{:S(2)}, u32[]{:S(2)}) collective-permute-start(bf16[22,2,16,512]{3,2,1,0:T(8,128)(2,1)S(1)} %constant_dynamic-update-slice_fusion.refs_3_), channel_id=1, source_target_pairs={{4,8},{8,4},{5,9},{9,5},{6,10},{10,6},{7,11},{11,7},{20,24},{24,20... | collective-permute-start | bytes 2162696 | tf_op jit(solution)/shard_map/ppermute | solution.py:187
  30.6 0.0 collective-permute-done.refs_1_
  30.7 0.7 %copy-done.1 = bf16[11,2,16,512]{3,2,1,0:T(8,128)(2,1)} copy-done((bf16[11,2,16,512]{3,2,1,0:T(8,128)(2,1)}, bf16[11,2,16,512]{3,2,1,0:T(8,128)(2,1)S(1)}, u32[]{:S(2)}) %copy-start.1) | copy-done | bytes 360472
  31.4 0.8 %copy-done.3 = bf16[11,2,16,512]{3,2,1,0:T(8,128)(2,1)} copy-done((bf16[11,2,16,512]{3,2,1,0:T(8,128)(2,1)}, bf16[11,2,16,512]{3,2,1,0:T(8,128)(2,1)S(1)}, u32[]{:S(2)}) %copy-start.3) | copy-done | bytes 360472
  32.2 8.1 %collective-permute-done.6.refs_6_ = bf16[11,2,16,512]{3,2,1,0:T(8,128)(2,1)} collective-permute-done((bf16[11,2,16,512]{3,2,1,0:T(8,128)(2,1)}, bf16[11,2,16,512]{3,2,1,0:T(8,128)(2,1)}, u32[]{:S(2)}, u32[]{:S(2)}) %collective-permute-start.6) | collective-permute-done | bytes 360480 | tf_op jit(solution)/shard_map/ppermute | solution.py:242
  40.2 0.5 collective-permute-start.7
  40.7 3.0 %collective-permute-start.8 = (bf16[11,2,16,512]{3,2,1,0:T(8,128)(2,1)}, bf16[11,2,16,512]{3,2,1,0:T(8,128)(2,1)}, u32[]{:S(2)}, u32[]{:S(2)}) collective-permute-start(bf16[11,2,16,512]{3,2,1,0:T(8,128)(2,1)} %collective-permute-done.6.refs_6_), channel_id=1, source_target_pairs={{4,8},{8,4},{5,9},{9,5},{6,10},{10,6},{7,11},{11,7},{20,24},{24,20... | collective-permute-start | bytes 1081352 | tf_op jit(solution)/shard_map/ppermute | solution.py:187
  43.8 0.1 stack.42.edge_ref
  43.9 0.1 stack.47.places_ref
  43.9 0.0 collective-permute-done.4.refs_4_
  43.9 0.0 collective-permute-done.5.refs_5_
  44.0 1.0 %copy-done.2 = bf16[11,2,16,512]{3,2,1,0:T(8,128)(2,1)S(1)} copy-done((bf16[11,2,16,512]{3,2,1,0:T(8,128)(2,1)S(1)}, bf16[11,2,16,512]{3,2,1,0:T(8,128)(2,1)}, u32[]{:S(2)}) %copy-start.2) | copy-done | bytes 360472
  44.9 1.0 %copy-done.4 = bf16[11,2,16,512]{3,2,1,0:T(8,128)(2,1)S(1)} copy-done((bf16[11,2,16,512]{3,2,1,0:T(8,128)(2,1)S(1)}, bf16[11,2,16,512]{3,2,1,0:T(8,128)(2,1)}, u32[]{:S(2)}) %copy-start.4) | copy-done | bytes 360472
  45.9 6.5 %shard_map.39.feature_ref = f32[3456,256]{1,0:T(8,128)S(1)} custom-call(s32[6]{0:T(128)S(1)} %stack.47.places_ref, bf16[384,768]{1,0:T(8,128)(2,1)S(1)} %get-tuple-element.15.first_ref, bf16[11,2,16,512]{3,2,1,0:T(8,128)(2,1)} %get-tuple-element.17.refs_0_, bf16[11,2,16,512]{3,2,1,0:T(8,128)(2,1)S(1)} %copy-done.2, bf16[11,2,16,512]{3,2,1,0:T(8,128)(2,1)S(1)} %copy-done.4, ...), custom_call_target="tpu_custom_call" | custom-call | tf_op jit(solution)/shard_map/pallas_call | solution.py:266
  52.4 0.0 collective-permute-done.8.refs_2_
  52.4 3.0 %shard_map.40 = bf16[4,128,256]{2,1,0:T(8,128)(2,1)S(1)} custom-call(s32[6]{0:T(128)S(1)} %stack.42.edge_ref, f32[3456,256]{1,0:T(8,128)S(1)} %shard_map.39.feature_ref, bf16[128,1792]{1,0:T(8,128)(2,1)S(1)} %get-tuple-element.22.second_ref, bf16[384,192]{1,0:T(8,128)(2,1)S(1)} %get-tuple-element.23.refs_0_, ...), custom_call_target="tpu_custom_call" | custom-call | tf_op jit(solution)/shard_map/pallas_call | solution.py:274
  55.4 0.9 %copy.5 = bf16[128,1,4,256]{3,2,1,0:T(4,128)(2,1)} copy(bf16[128,1,4,256]{3,0,2,1:T(8,128)(2,1)S(1)} %bitcast.13) | data formatting | bytes 524288 | tf_op jit(solution)/shard_map/broadcast_in_dim | solution.py:288
  (7 shorter events, 0.0 us)
Async XLA Ops:
  0.0 1.2 %copy-start = (bf16[16,2,32,512]{3,2,1,0:T(8,128)(2,1)S(1)}, bf16[16,2,32,512]{3,2,1,0:T(8,128)(2,1)}, u32[]{:S(2)}) copy-start(bf16[16,2,32,512]{3,2,1,0:T(8,128)(2,1)} %volume_ref.1) | copy-start | bytes 3145732
  3.8 12.4 %collective-permute-start.2 = (bf16[11,2,16,512]{3,2,1,0:T(8,128)(2,1)S(1)}, bf16[11,2,16,512]{3,2,1,0:T(8,128)(2,1)}, u32[]{:S(2)}, u32[]{:S(2)}) collective-permute-start(bf16[11,2,16,512]{3,2,1,0:T(8,128)(2,1)S(1)} %get-tuple-element.18), channel_id=1, source_target_pairs={{0,3},{1,0},{2,1},{3,2},{4,7},{5,4},{6,5},{7,6},{8,11},{9,8},{10,9... | collective-permute-start | bytes 1081352 | tf_op jit(solution)/shard_map/ppermute | solution.py:242
  7.9 15.9 %collective-permute-start.3 = (bf16[11,2,16,512]{3,2,1,0:T(8,128)(2,1)S(1)}, bf16[11,2,16,512]{3,2,1,0:T(8,128)(2,1)}, u32[]{:S(2)}, u32[]{:S(2)}) collective-permute-start(bf16[11,2,16,512]{3,2,1,0:T(8,128)(2,1)S(1)} %get-tuple-element.19), channel_id=1, source_target_pairs={{0,1},{1,2},{2,3},{3,0},{4,5},{5,6},{6,7},{7,4},{8,9},{9,10},{10,1... | collective-permute-start | bytes 1081352 | tf_op jit(solution)/shard_map/ppermute | solution.py:242
  12.1 18.5 %collective-permute-start = (bf16[11,2,16,512]{3,2,1,0:T(8,128)(2,1)}, bf16[11,2,16,512]{3,2,1,0:T(8,128)(2,1)S(1)}, u32[]{:S(2)}, u32[]{:S(2)}) collective-permute-start(bf16[11,2,16,512]{3,2,1,0:T(8,128)(2,1)} %get-tuple-element.17.refs_0_), channel_id=1, source_target_pairs={{0,4},{8,12},{4,0},{12,8},{1,5},{9,13},{5,1},{13,9},{2,6},{10,14},... | collective-permute-start | bytes 1081352 | tf_op jit(solution)/shard_map/ppermute | solution.py:187
  13.1 18.3 %collective-permute-start.1 = (bf16[11,2,16,512]{3,2,1,0:T(8,128)(2,1)}, bf16[11,2,16,512]{3,2,1,0:T(8,128)(2,1)S(1)}, u32[]{:S(2)}, u32[]{:S(2)}) collective-permute-start(bf16[11,2,16,512]{3,2,1,0:T(8,128)(2,1)} %get-tuple-element.17.refs_0_), channel_id=1, source_target_pairs={{4,8},{8,4},{5,9},{9,5},{6,10},{10,6},{7,11},{11,7},{20,24},{24,20... | collective-permute-start | bytes 1081352 | tf_op jit(solution)/shard_map/ppermute | solution.py:187
  16.2 24.1 %collective-permute-start.6 = (bf16[11,2,16,512]{3,2,1,0:T(8,128)(2,1)}, bf16[11,2,16,512]{3,2,1,0:T(8,128)(2,1)}, u32[]{:S(2)}, u32[]{:S(2)}) collective-permute-start(bf16[11,2,16,512]{3,2,1,0:T(8,128)(2,1)} %get-tuple-element.21), channel_id=1, source_target_pairs={{0,2},{1,3},{2,0},{3,1},{4,6},{5,7},{6,4},{7,5},{8,10},{9,11},{10,... | collective-permute-start | bytes 1081352 | tf_op jit(solution)/shard_map/ppermute | solution.py:242
  24.8 19.2 %collective-permute-start.4 = (bf16[22,2,16,512]{3,2,1,0:T(8,128)(2,1)S(1)}, bf16[22,2,16,512]{3,2,1,0:T(8,128)(2,1)S(1)}, u32[]{:S(2)}, u32[]{:S(2)}) collective-permute-start(bf16[22,2,16,512]{3,2,1,0:T(8,128)(2,1)S(1)} %constant_dynamic-update-slice_fusion.refs_3_), channel_id=1, source_target_pairs={{0,4},{8,12},{4,0},{12,8},{1,5},{9,13},{5,1},{13,9},{2,6},{10,14},... | collective-permute-start | bytes 2162696 | tf_op jit(solution)/shard_map/ppermute | solution.py:187
  27.6 16.3 %collective-permute-start.5 = (bf16[22,2,16,512]{3,2,1,0:T(8,128)(2,1)S(1)}, bf16[22,2,16,512]{3,2,1,0:T(8,128)(2,1)S(1)}, u32[]{:S(2)}, u32[]{:S(2)}) collective-permute-start(bf16[22,2,16,512]{3,2,1,0:T(8,128)(2,1)S(1)} %constant_dynamic-update-slice_fusion.refs_3_), channel_id=1, source_target_pairs={{4,8},{8,4},{5,9},{9,5},{6,10},{10,6},{7,11},{11,7},{20,24},{24,20... | collective-permute-start | bytes 2162696 | tf_op jit(solution)/shard_map/ppermute | solution.py:187
  30.6 0.7 %copy-start.1 = (bf16[11,2,16,512]{3,2,1,0:T(8,128)(2,1)}, bf16[11,2,16,512]{3,2,1,0:T(8,128)(2,1)S(1)}, u32[]{:S(2)}) copy-start(bf16[11,2,16,512]{3,2,1,0:T(8,128)(2,1)S(1)} %collective-permute-done.refs_1_) | copy-start | bytes 1081348
  31.4 0.8 %copy-start.3 = (bf16[11,2,16,512]{3,2,1,0:T(8,128)(2,1)}, bf16[11,2,16,512]{3,2,1,0:T(8,128)(2,1)S(1)}, u32[]{:S(2)}) copy-start(bf16[11,2,16,512]{3,2,1,0:T(8,128)(2,1)S(1)} %collective-permute-done.1.refs_2_) | copy-start | bytes 1081348
  40.2 12.2 %collective-permute-start.7 = (bf16[11,2,16,512]{3,2,1,0:T(8,128)(2,1)}, bf16[11,2,16,512]{3,2,1,0:T(8,128)(2,1)}, u32[]{:S(2)}, u32[]{:S(2)}) collective-permute-start(bf16[11,2,16,512]{3,2,1,0:T(8,128)(2,1)} %collective-permute-done.6.refs_6_), channel_id=1, source_target_pairs={{0,4},{8,12},{4,0},{12,8},{1,5},{9,13},{5,1},{13,9},{2,6},{10,14},... | collective-permute-start | bytes 1081352 | tf_op jit(solution)/shard_map/ppermute | solution.py:187
  40.7 11.7 %collective-permute-start.8 = (bf16[11,2,16,512]{3,2,1,0:T(8,128)(2,1)}, bf16[11,2,16,512]{3,2,1,0:T(8,128)(2,1)}, u32[]{:S(2)}, u32[]{:S(2)}) collective-permute-start(bf16[11,2,16,512]{3,2,1,0:T(8,128)(2,1)} %collective-permute-done.6.refs_6_), channel_id=1, source_target_pairs={{4,8},{8,4},{5,9},{9,5},{6,10},{10,6},{7,11},{11,7},{20,24},{24,20... | collective-permute-start | bytes 1081352 | tf_op jit(solution)/shard_map/ppermute | solution.py:187
  44.0 1.0 %copy-start.2 = (bf16[11,2,16,512]{3,2,1,0:T(8,128)(2,1)S(1)}, bf16[11,2,16,512]{3,2,1,0:T(8,128)(2,1)}, u32[]{:S(2)}) copy-start(bf16[11,2,16,512]{3,2,1,0:T(8,128)(2,1)} %copy-done.1) | copy-start | bytes 1081348
  44.9 1.0 %copy-start.4 = (bf16[11,2,16,512]{3,2,1,0:T(8,128)(2,1)S(1)}, bf16[11,2,16,512]{3,2,1,0:T(8,128)(2,1)}, u32[]{:S(2)}) copy-start(bf16[11,2,16,512]{3,2,1,0:T(8,128)(2,1)} %copy-done.3) | copy-start | bytes 1081348

commit v6 on v4

v6 whole, which is shorter than its diff:
```python
import functools

import jax
import jax.numpy as jnp
from jax import lax
from jax.experimental import pallas as pl
from jax.experimental.pallas import tpu as pltpu
from jax.sharding import PartitionSpec as P

C = 64
C2 = 128
BELOW, ABOVE = 2, 1
negative_slope = 0.01
VMEM_LIMIT = 20 * 1024 * 1024


def split_matrix(width):
    half = width // 2
    source = lax.broadcasted_iota(jnp.int32, (width, width), 0)
    column = lax.broadcasted_iota(jnp.int32, (width, width), 1)
    wanted = jnp.where(column < half, 2 * column, 2 * (column - half) + 1)
    return jnp.where(source == wanted, 1.0, 0.0).astype(jnp.bfloat16)


def turn_matrix(count, rows):
    size = count * rows
    target = lax.broadcasted_iota(jnp.int32, (size, size), 0)
    source = lax.broadcasted_iota(jnp.int32, (size, size), 1)
    wanted = lax.rem(target, count) * rows + lax.div(target, count)
    return jnp.where(source == wanted, 1.0, 0.0).astype(jnp.bfloat16)


def send_kernel(band, distances, volume_ref, *refs):
    out_refs, (block_ref, field_ref, sems) = refs[:-3], refs[-3:]
    count, planes, all_rows, width = volume_ref.shape
    step = block_ref.shape[2]
    places = [(p, at) for at in range(0, all_rows, step) for p in range(planes)]
    copies = [
        pltpu.make_async_copy(volume_ref.at[:, p, pl.ds(at, step), :], block_ref.at[i], sems.at[i])
        for i, (p, at) in enumerate(places)
    ]
    for copy in copies:
        copy.start()
    split, turn = split_matrix(width), turn_matrix(count, step)
    field_ref[pl.ds(0, BELOW)] = jnp.zeros((BELOW, planes, count, width), jnp.bfloat16)
    field_ref[pl.ds(BELOW + all_rows, ABOVE)] = jnp.zeros((ABOVE, planes, count, width), jnp.bfloat16)
    for i, (p, at) in enumerate(places):
        copies[i].wait()
        block = block_ref[i].reshape(count * step, width)
        block = jnp.dot(block, split, preferred_element_type=jnp.float32).astype(jnp.bfloat16)
        block = jnp.dot(turn, block, preferred_element_type=jnp.float32).astype(jnp.bfloat16)
        field_ref[pl.ds(BELOW + at, step), p] = block.reshape(step, count, width)
    me = lax.axis_index("filt")
    for d, out_ref in zip(distances, out_refs):
        start = lax.bitwise_xor(me, d) * band
        out_ref[...] = field_ref[pl.ds(start, out_ref.shape[0])]


def store_taps(taps_ref, row, at, channels, cell):
    count, half = cell.shape[0], cell.shape[1] // 2
    lane = lax.broadcasted_iota(jnp.int32, (count, half), 1)
    even, odd = cell[:, :half], cell[:, half:]
    before = jnp.where(lane == 0, 0.0, pltpu.roll(odd.astype(jnp.float32), 1, 1))
    after_it = jnp.where(lane == half - 1, 0.0, pltpu.roll(even.astype(jnp.float32), half - 1, 1))
    for k, value in enumerate((before.astype(jnp.bfloat16), even, odd, after_it.astype(jnp.bfloat16))):
        taps_ref[pl.ds((4 * row + k) * channels + at, count), :] = value


def plane_parts(total, weight_ref, taps, y, p, depth):
    size = 2 * C
    z_low, z_high = max(0, p - 2), min(2, p)
    first = 2 - (p - z_low)
    weight = weight_ref[pl.ds(first * size, (z_high - z_low + 1) * size), :]
    part = jnp.dot(weight, taps[pl.ds(y * depth, 3 * depth), :], preferred_element_type=jnp.float32)
    for z in range(z_low, z_high + 1):
        piece = part[(z - z_low) * size : (z - z_low + 1) * size]
        total[z] = piece if total[z] is None else total[z] + piece


def join_kernel(one_ref, two_ref, out_ref):
    rows = one_ref.shape[0]
    out_ref[:rows] = one_ref[...]
    out_ref[rows:] = two_ref[...]


class Group:
    def __init__(self, inside, channels, blocks):
        self.inside, self.channels, self.blocks = inside, channels, blocks
        self.planes = (2, 3) if inside else (0, 1, 4)
        self.arrays = 1 + max(i for i, _, _ in blocks)


def conv_kernel(groups, window, first, last, *refs):
    space, band = lax.axis_index("space"), lax.axis_index("filt")
    odd = lax.rem(space, 2)
    places = ((2 - 2 * odd, 3 - 2 * odd), (2 * odd, 1 + 2 * odd))
    refs = list(refs)
    feature_ref = None if first else refs.pop(0)
    second_ref = refs.pop(0) if last else None
    inputs = [[refs.pop(0) for _ in range(1 + group.arrays)] for group in groups]
    out_ref = refs.pop(0)
    hid_ref = refs.pop(0) if last else None
    half = out_ref.shape[-1]
    for group, (_, *blocks), taps_ref in zip(groups, inputs, refs):
        for i, row, at in group.blocks:
            for r in range(window):
                for k in range(2):
                    place = k if group.inside else places[i % 2][k]
                    store_taps(taps_ref.at[place], r, at, group.channels, blocks[i][row + r, k])
    size = 2 * C
    lane = lax.broadcasted_iota(jnp.int32, (C, half), 1)
    for y in range(window - 2):
        total = [None if first else feature_ref[pl.ds((y * 3 + z) * size, size), :] for z in range(3)]
        for group, (weight_ref, *_), taps_ref in zip(groups, inputs, refs):
            for k, p in enumerate(group.planes):
                plane_parts(total, weight_ref, taps_ref.at[k], y, p, 4 * group.channels)
        for z in range(3):
            if not last:
                out_ref[pl.ds((y * 3 + z) * size, size), :] = total[z]
                continue
            value = total[z]
            value = jnp.where(value > 0, value, negative_slope * value)
            if z == 0:
                value = jnp.where(space > 0, value, 0.0)
            if y == 0:
                value = jnp.where(band > 0, value, 0.0)
            value = value.astype(jnp.bfloat16)
            before = jnp.where(lane == 0, 0.0, pltpu.roll(value[C:].astype(jnp.float32), 1, 1))
            base = (y * 3 + z) * 3 * C
            hid_ref[pl.ds(base, C), :] = before.astype(jnp.bfloat16)
            hid_ref[pl.ds(base + C, 2 * C), :] = value
    if last:
        for y in range(out_ref.shape[0]):
            out_ref[y] = jnp.dot(
                second_ref[:, : 27 * C],
                hid_ref[pl.ds(2 * y * 9 * C, 27 * C), :],
                preferred_element_type=jnp.float32,
            ).astype(jnp.bfloat16)


def exact(left, right):
    return jnp.dot(left, right, preferred_element_type=jnp.float32)


def weight_kernel(distances, ranges, conv_ref, down_ref, second_ref, *first_refs):
    row = lax.broadcasted_iota(jnp.int32, (2 * C, 2 * C), 0)
    lane = lax.broadcasted_iota(jnp.int32, (2 * C, 2 * C), 1)
    hidden = 2 * lax.rem(lane, C // 2) + lax.div(lax.rem(lane, C), C // 2)
    pair = [
        [((row == C * odd + hidden) & (lax.div(lane, C) == k)).astype(jnp.bfloat16) for k in range(2)]
        for odd in range(2)
    ]
    in_order = (row == 2 * lax.rem(lane, C) + lax.div(lane, C)).astype(jnp.bfloat16)
    down = [[down_ref[a, b].reshape(3, C, 2 * C) for b in range(3)] for a in range(3)]
    for j in range(14):
        halves = []
        for odd in range(2):
            total = None
            for k in range(2):
                t = 2 * j + k
                if t < 27:
                    part = exact(down[t // 3 % 3][t // 9][t % 3], pair[odd][k])
                    total = part if total is None else total + part
            halves.append(total.astype(jnp.bfloat16))
        second_ref[:, pl.ds(2 * C * j, 2 * C)] = exact(in_order, jnp.concatenate(halves)).astype(jnp.bfloat16)
    conv = [[conv_ref[a, b].reshape(3, C // 2, 2 * C) for b in range(3)] for a in range(3)]
    taps = [[jnp.concatenate([conv[a][b][c] for a in range(3)]) for c in range(3)] for b in range(3)]
    for (start, channels), first_ref in zip(ranges, first_refs):
        row = lax.broadcasted_iota(jnp.int32, (2 * C, 12 * channels), 0)
        lane = lax.broadcasted_iota(jnp.int32, (2 * C, 12 * channels), 1)
        place = start + lax.rem(lane, channels)
        source = place
        if distances:
            me, count = lax.axis_index("filt"), C // len(distances)
            for i, d in enumerate(distances):
                moved = lax.bitwise_xor(me, d) * count + place - i * count
                source = jnp.where(lax.div(place, count) == i, moved, source)
        for odd in range(2):
            shift = jnp.where(row == C * odd + source, lax.div(lane, channels), -1)
            for parity in range(2):
                total = None
                for b in range(3):
                    for c in range(3):
                        part = exact(taps[b][c], (shift == 4 * b + c + parity).astype(jnp.bfloat16))
                        total = part if total is None else total + part
                total = total.astype(jnp.bfloat16)
                for a in range(3):
                    at = (2 - a) * 2 * C + parity * C + odd * C // 2
                    first_ref[pl.ds(at, C // 2), :] = total[a * C // 2 : (a + 1) * C // 2]


def swapped(block, axis):
    count = lax.axis_size(axis)
    results = []
    for start in (0, 1):
        pairs = [(i, i + 1) for i in range(start, count - 1, 2)]
        results.append(lax.ppermute(block, axis, pairs + [(j, i) for i, j in pairs]))
    return results


def after(value, *others):
    return lax.optimization_barrier((value, *others))[0]


def in_vmem(value):
    return pltpu.with_memory_space_constraint(value, pltpu.VMEM)


def local(volume, conv_weight, down_weight):
    bands = lax.axis_size("filt")
    count, planes, all_rows, width = volume.shape
    band = all_rows // bands
    window = BELOW + band + ABOVE
    half = width // 2
    hid_rows = band + 1
    vmem = pl.BlockSpec(memory_space=pltpu.VMEM)
    params = pltpu.CompilerParams(vmem_limit_bytes=VMEM_LIMIT)
    cost = pl.CostEstimate(flops=1, transcendentals=0, bytes_accessed=1)
    direct = count == 16 and bands == 4
    distances = (0, 1, 3, 2) if direct else ()
    ranges = [(0, 48), (0, 16), (16, 32), (48, 16)] if direct else [(0, C)]
    lay = pl.pallas_call(
        functools.partial(weight_kernel, distances, ranges),
        out_shape=[pltpu.VMEM((C2, 28 * C), jnp.bfloat16)]
        + [pltpu.VMEM((6 * C, 12 * channels), jnp.bfloat16) for _, channels in ranges],
        in_specs=[vmem] * 2,
        out_specs=[vmem] * (1 + len(ranges)),
        compiler_params=params,
        cost_estimate=cost,
    )
    def convolve(feature, groups, second=None):
        arrays = [] if feature is None else [feature]
        last = second is not None
        arrays += [second] if last else []
        for _, *given in groups:
            arrays += given
        kinds = [group for group, *_ in groups]
        scratch = [pltpu.VMEM((hid_rows * 9 * C, half), jnp.bfloat16)] * last
        for group in kinds:
            slots = 2 if group.inside else 4
            scratch.append(pltpu.VMEM((slots, window * 4 * group.channels, half), jnp.bfloat16))
        if last:
            shape = pltpu.VMEM((band // 2, C2, half), jnp.bfloat16)
        else:
            shape = pltpu.VMEM((hid_rows * 6 * C, half), jnp.float32)
        return pl.pallas_call(
            functools.partial(conv_kernel, kinds, window, feature is None, last),
            out_shape=shape,
            in_specs=[vmem] * len(arrays),
            out_specs=vmem,
            scratch_shapes=scratch,
            compiler_params=params,
            cost_estimate=pl.CostEstimate(flops=1 << 33, transcendentals=0, bytes_accessed=1 << 24),
        )(*map(in_vmem, arrays))

    if direct:
        step = 16
        sent = pl.pallas_call(
            functools.partial(send_kernel, band, distances),
            out_shape=[jax.ShapeDtypeStruct((window, planes, count, width), jnp.bfloat16)] * bands,
            in_specs=[pl.BlockSpec(memory_space=pltpu.HBM)],
            out_specs=[vmem] * bands,
            scratch_shapes=[
                pltpu.VMEM((planes * all_rows // step, count, step, width), jnp.bfloat16),
                pltpu.VMEM((BELOW + all_rows + ABOVE, planes, count, width), jnp.bfloat16),
                pltpu.SemaphoreType.DMA((planes * all_rows // step,)),
            ],
            compiler_params=params,
            cost_estimate=cost,
        )(pltpu.with_memory_space_constraint(volume, pltpu.HBM))
        second, *firsts = lay(conv_weight, down_weight)
        own = []
        for d, piece in zip(distances, sent):
            if d:
                piece = lax.ppermute(piece, "filt", [(i, i ^ d) for i in range(bands)])
            own.append(piece)
        mine = swapped(after(own[0], firsts[0]), "space")
        middle = pl.pallas_call(
            join_kernel,
            out_shape=pltpu.VMEM((2 * window, planes, count, width), jnp.bfloat16),
            in_specs=[vmem] * 2,
            out_specs=vmem,
            compiler_params=params,
            cost_estimate=cost,
        )(*map(in_vmem, own[1:3]))
        middles = swapped(middle, "space")
        all_three, of_own, of_middle, of_last = firsts
        feature = convolve(
            None,
            [
                (Group(True, 48, [(0, 0, 0), (1, 0, 16), (1, window, 32)]), all_three, own[0], middle),
                (Group(False, 16, [(0, 0, 0), (1, 0, 0)]), of_own, *mine),
            ],
        )
        tails = swapped(after(own[3], feature), "space")
        middles = [after(block, own[3]) for block in middles]
        in_middle = [(i, at * window, at * 16) for i in range(2) for at in range(2)]
        feature = convolve(
            feature,
            [
                (Group(True, 16, [(0, 0, 0)]), of_last, own[3]),
                (Group(False, 32, in_middle), of_middle, *middles),
            ],
        )
        coarse = convolve(feature, [(Group(False, 16, [(0, 0, 0), (1, 0, 0)]), of_last, *tails)], second)
    else:
        field = jnp.transpose(volume, (2, 1, 0, 3))
        field = jnp.concatenate([field[..., ::2], field[..., 1::2]], axis=-1)
        field = jnp.pad(field, ((BELOW, ABOVE), (0, 0), (0, 0), (0, 0)))
        sent = jnp.stack([field[t * band : t * band + window] for t in range(bands)])
        got = lax.all_to_all(sent, "filt", split_axis=0, concat_axis=0, tiled=True)
        own = jnp.transpose(got, (1, 2, 0, 3, 4)).reshape(window, planes, C, width)
        second, *firsts = lay(conv_weight, down_weight)
        inside = (Group(True, C, [(0, 0, 0)]), firsts[0], own)
        outside = (Group(False, C, [(0, 0, 0), (1, 0, 0)]), firsts[0], *swapped(own, "space"))
        coarse = convolve(None, [inside, outside], second)
    return jnp.transpose(coarse, (1, 0, 2))[:, None]


def solution(mesh):
    return jax.shard_map(
        local,
        mesh=mesh,
        in_specs=(P("filt", ("groups", "space"), None, None), P(), P()),
        out_specs=P(None, ("groups", "space"), "filt", None),
        check_vma=False,
    )
```

time: 83.9 us -> 51.8 us (0.62)
  the two profiles are of different devices: /device:TPU:13 before, /device:TPU:1 now
where the time goes in v6:
time: 51.8 us; the launch traced here: 51.6 us
  starting transfers between devices  18.3 us (35%)
  Pallas kernels  16 us (31%)
  waiting for transfers between devices  14.2 us (27%)
  local copies, waits for them, and re-layouts  2.93 us (6%)
    ppermute x6, starting transfers between devices, swapped(): lax.ppermute(block, axis, pairs + [(j, i) for i, j in pairs])  13.9 us
    ppermute x3, waiting for transfers between devices, local(): piece = lax.ppermute(piece, 'filt', [(i, i ^ d) for i in range(bands)])  11.3 us
    pallas_call x3, Pallas kernels, convolve(): pl.pallas_call(functools.partial(conv_kernel, kinds, window, feature is N...  7.51 us
    pallas_call x1, Pallas kernels, local(): second, *firsts = lay(conv_weight, down_weight)  5.37 us
    ppermute x3, starting transfers between devices, local(): piece = lax.ppermute(piece, 'filt', [(i, i ^ d) for i in range(bands)])  4.46 us
    pallas_call x1, Pallas kernels, local(): pl.pallas_call(functools.partial(send_kernel, band, distances), out_shape...  3.05 us
    ppermute x6, waiting for transfers between devices, swapped(): lax.ppermute(block, axis, pairs + [(j, i) for i, j in pairs])  2.87 us
    unnamed x4, local copies, waits for them, and re-layouts  2.02 us
  transfers between devices with their start and end apart: 9, of which 3 were waited for; matrix products, arithmetic and copies ran while one was open for 0% of the time, Pallas kernels for 22%

profile of v6, /device:TPU:1, one launch (start us, length us, event | category | flops | bytes accessed | tf_op | source)
XLA Modules:
  0.0 51.6 jit_solution(9825050970600307696)
XLA Ops:
  0.0 3.1 %shard_map.38 = (bf16[11,2,16,512]{3,2,1,0:T(8,128)(2,1)S(1)}, bf16[11,2,16,512]{3,2,1,0:T(8,128)(2,1)S(1)}, bf16[11,2,16,512]{3,2,1,0:T(8,128)(2,1)S(1)}, bf16[11,2,16,512]{3,2,1,0:T(8,128)(2,1)S(1)}) custom-call(bf16[16,2,32,512]{3,2,1,0:T(8,128)(2,1)} %volume_ref.1), custom_call_target="tpu_custom_call" | custom-call | flops 1 | bytes 1 | tf_op jit(solution)/shard_map/pallas_call | solution.py:258
  3.1 2.2 %collective-permute-start = (bf16[11,2,16,512]{3,2,1,0:T(8,128)(2,1)S(1)}, bf16[11,2,16,512]{3,2,1,0:T(8,128)(2,1)S(1)}, u32[]{:S(2)}, u32[]{:S(2)}) collective-permute-start(bf16[11,2,16,512]{3,2,1,0:T(8,128)(2,1)S(1)} %get-tuple-element.20), channel_id=1, source_target_pairs={{0,1},{1,0},{2,3},{3,2},{4,5},{5,4},{6,7},{7,6},{8,9},{9,8},{10,11... | collective-permute-start | bytes 1081352 | tf_op jit(solution)/shard_map/ppermute | solution.py:275
  5.3 2.2 %collective-permute-start.1 = (bf16[11,2,16,512]{3,2,1,0:T(8,128)(2,1)S(1)}, bf16[11,2,16,512]{3,2,1,0:T(8,128)(2,1)S(1)}, u32[]{:S(2)}, u32[]{:S(2)}) collective-permute-start(bf16[11,2,16,512]{3,2,1,0:T(8,128)(2,1)S(1)} %get-tuple-element.21), channel_id=1, source_target_pairs={{0,3},{1,2},{2,1},{3,0},{4,7},{5,6},{6,5},{7,4},{8,11},{9,10},{10,... | collective-permute-start | bytes 1081352 | tf_op jit(solution)/shard_map/ppermute | solution.py:275
  7.4 0.0 copy-start
  7.4 1.1 %copy-done = bf16[3,3,3,8192]{3,2,1,0:T(4,128)(2,1)S(1)} copy-done((bf16[3,3,3,8192]{3,2,1,0:T(4,128)(2,1)S(1)}, bf16[3,3,3,8192]{3,2,1,0:T(4,128)(2,1)}, u32[]{:S(2)}) %copy-start) | copy-done | bytes 442392
  8.5 0.0 copy-start.1
  8.5 1.0 %copy-done.1 = bf16[3,3,3,4096]{3,2,1,0:T(4,128)(2,1)S(1)} copy-done((bf16[3,3,3,4096]{3,2,1,0:T(4,128)(2,1)S(1)}, bf16[3,3,3,4096]{3,2,1,0:T(4,128)(2,1)}, u32[]{:S(2)}) %copy-start.1) | copy-done | bytes 221208
  9.5 5.4 %shard_map.37 = (bf16[128,1792]{1,0:T(8,128)(2,1)S(1)}, bf16[384,576]{1,0:T(8,128)(2,1)S(1)}, bf16[384,192]{1,0:T(8,128)(2,1)S(1)}, bf16[384,384]{1,0:T(8,128)(2,1)S(1)}, bf16[384,192]{1,0:T(8,128)(2,1)S(1)}) custom-call(bf16[3,3,3,4096]{3,2,1,0:T(4,128)(2,1)S(1)} %copy-done.1, bf16[3,3,3,8192]{3,2,1,0:T(4,128)(2,1)S(1)} %copy-done), custom_call_target="tpu_custom_call" | custom-call | flops 1 | bytes 1 | tf_op jit(solution)/shard_map/pallas_call | solution.py:271
  14.9 1.3 %collective-permute-start.2 = (bf16[11,2,16,512]{3,2,1,0:T(8,128)(2,1)S(1)}, bf16[11,2,16,512]{3,2,1,0:T(8,128)(2,1)S(1)}, u32[]{:S(2)}, u32[]{:S(2)}) collective-permute-start(bf16[11,2,16,512]{3,2,1,0:T(8,128)(2,1)S(1)} %get-tuple-element.23.refs_1_), channel_id=1, source_target_pairs={{0,4},{8,12},{4,0},{12,8},{1,5},{9,13},{5,1},{13,9},{2,6},{10,14},... | collective-permute-start | bytes 1081352 | tf_op jit(solution)/shard_map/ppermute | solution.py:197
  16.2 3.0 %collective-permute-start.3 = (bf16[11,2,16,512]{3,2,1,0:T(8,128)(2,1)S(1)}, bf16[11,2,16,512]{3,2,1,0:T(8,128)(2,1)S(1)}, u32[]{:S(2)}, u32[]{:S(2)}) collective-permute-start(bf16[11,2,16,512]{3,2,1,0:T(8,128)(2,1)S(1)} %get-tuple-element.23.refs_1_), channel_id=1, source_target_pairs={{4,8},{8,4},{5,9},{9,5},{6,10},{10,6},{7,11},{11,7},{20,24},{24,20... | collective-permute-start | bytes 1081352 | tf_op jit(solution)/shard_map/ppermute | solution.py:197
  19.2 0.1 collective-permute-start.4
  19.3 0.0 collective-permute-done.one_ref
  19.3 3.7 %collective-permute-done.1.two_ref = bf16[11,2,16,512]{3,2,1,0:T(8,128)(2,1)S(1)} collective-permute-done((bf16[11,2,16,512]{3,2,1,0:T(8,128)(2,1)S(1)}, bf16[11,2,16,512]{3,2,1,0:T(8,128)(2,1)S(1)}, u32[]{:S(2)}, u32[]{:S(2)}) %collective-permute-start.1) | collective-permute-done | bytes 360480 | tf_op jit(solution)/shard_map/ppermute | solution.py:275
  23.1 2.8 %collective-permute-start.5 = (bf16[22,2,16,512]{3,2,1,0:T(8,128)(2,1)S(1)}, bf16[22,2,16,512]{3,2,1,0:T(8,128)(2,1)S(1)}, u32[]{:S(2)}, u32[]{:S(2)}) collective-permute-start(bf16[22,2,16,512]{3,2,1,0:T(8,128)(2,1)S(1)} %shard_map.39.refs_2_), channel_id=1, source_target_pairs={{0,4},{8,12},{4,0},{12,8},{1,5},{9,13},{5,1},{13,9},{2,6},{10,14},... | collective-permute-start | bytes 2162696 | tf_op jit(solution)/shard_map/ppermute | solution.py:197
  25.9 3.0 %collective-permute-start.6 = (bf16[22,2,16,512]{3,2,1,0:T(8,128)(2,1)S(1)}, bf16[22,2,16,512]{3,2,1,0:T(8,128)(2,1)S(1)}, u32[]{:S(2)}, u32[]{:S(2)}) collective-permute-start(bf16[22,2,16,512]{3,2,1,0:T(8,128)(2,1)S(1)} %shard_map.39.refs_2_), channel_id=1, source_target_pairs={{4,8},{8,4},{5,9},{9,5},{6,10},{10,6},{7,11},{11,7},{20,24},{24,20... | collective-permute-start | bytes 2162696 | tf_op jit(solution)/shard_map/ppermute | solution.py:197
  28.9 0.0 collective-permute-done.2.refs_4_
  28.9 0.0 collective-permute-done.3.refs_5_
  29.0 3.2 %shard_map.40.refs_0_ = f32[3456,256]{1,0:T(8,128)S(1)} custom-call(bf16[384,576]{1,0:T(8,128)(2,1)S(1)} %get-tuple-element.18.refs_0_, bf16[11,2,16,512]{3,2,1,0:T(8,128)(2,1)S(1)} %get-tuple-element.23.refs_1_, bf16[22,2,16,512]{3,2,1,0:T(8,128)(2,1)S(1)} %shard_map.39.refs_2_, bf16[384,192]{1,0:T(8,128)(2,1)S(1)} %get-tuple-element.22.refs_3_, ...), custom_call_target="tpu_custom_call" | custom-call | flops 8589934592 | bytes 16777216 | tf_op jit(solution)/shard_map/pallas_call | solution.py:246
  32.1 7.6 %collective-permute-done.4.refs_2_ = bf16[11,2,16,512]{3,2,1,0:T(8,128)(2,1)S(1)} collective-permute-done((bf16[11,2,16,512]{3,2,1,0:T(8,128)(2,1)S(1)}, bf16[11,2,16,512]{3,2,1,0:T(8,128)(2,1)S(1)}, u32[]{:S(2)}, u32[]{:S(2)}) %collective-permute-start.4) | collective-permute-done | bytes 360480 | tf_op jit(solution)/shard_map/ppermute | solution.py:275
  39.7 0.4 collective-permute-start.7
  40.1 3.3 %collective-permute-start.8 = (bf16[11,2,16,512]{3,2,1,0:T(8,128)(2,1)S(1)}, bf16[11,2,16,512]{3,2,1,0:T(8,128)(2,1)S(1)}, u32[]{:S(2)}, u32[]{:S(2)}) collective-permute-start(bf16[11,2,16,512]{3,2,1,0:T(8,128)(2,1)S(1)} %collective-permute-done.4.refs_2_), channel_id=1, source_target_pairs={{4,8},{8,4},{5,9},{9,5},{6,10},{10,6},{7,11},{11,7},{20,24},{24,20... | collective-permute-start | bytes 1081352 | tf_op jit(solution)/shard_map/ppermute | solution.py:197
  43.4 0.0 collective-permute-done.5.refs_4_
  43.4 0.0 collective-permute-done.6.refs_5_
  43.4 2.6 %shard_map.41.refs_0_ = f32[3456,256]{1,0:T(8,128)S(1)} custom-call(f32[3456,256]{1,0:T(8,128)S(1)} %shard_map.40.refs_0_, bf16[384,192]{1,0:T(8,128)(2,1)S(1)} %get-tuple-element.24.refs_1_.refs_2_, bf16[11,2,16,512]{3,2,1,0:T(8,128)(2,1)S(1)} %collective-permute-done.4.refs_2_, bf16[384,384]{1,0:T(8,128)(2,1)S(1)} %get-tuple-element.26.refs_3_, ...), custom_call_target="tpu_custom_call" | custom-call | flops 8589934592 | bytes 16777216 | tf_op jit(solution)/shard_map/pallas_call | solution.py:246
  46.0 0.0 collective-permute-done.7.refs_3_
  46.0 2.9 %collective-permute-done.8.refs_4_ = bf16[11,2,16,512]{3,2,1,0:T(8,128)(2,1)S(1)} collective-permute-done((bf16[11,2,16,512]{3,2,1,0:T(8,128)(2,1)S(1)}, bf16[11,2,16,512]{3,2,1,0:T(8,128)(2,1)S(1)}, u32[]{:S(2)}, u32[]{:S(2)}) %collective-permute-start.8) | collective-permute-done | bytes 360480 | tf_op jit(solution)/shard_map/ppermute | solution.py:197
  48.8 1.8 %shard_map.42 = bf16[4,128,256]{2,1,0:T(8,128)(2,1)S(1)} custom-call(f32[3456,256]{1,0:T(8,128)S(1)} %shard_map.41.refs_0_, bf16[128,1792]{1,0:T(8,128)(2,1)S(1)} %get-tuple-element.29.refs_1_, bf16[384,192]{1,0:T(8,128)(2,1)S(1)} %get-tuple-element.24.refs_1_.refs_2_, bf16[11,2,16,512]{3,2,1,0:T(8,128)(2,1)S(1)} %collective-permute-done.7.refs_3_, ...), custom_call_target="tpu_custom_call" | custom-call | flops 8589934592 | bytes 16777216 | tf_op jit(solution)/shard_map/pallas_call | solution.py:246
  50.6 0.9 %copy.4 = bf16[128,1,4,256]{3,2,1,0:T(4,128)(2,1)} copy(bf16[128,1,4,256]{3,0,2,1:T(8,128)(2,1)S(1)} %bitcast.3) | data formatting | bytes 524288 | tf_op jit(solution)/shard_map/broadcast_in_dim | solution.py:317
  (1 shorter events, 0.0 us)
Async XLA Ops:
  3.1 16.2 %collective-permute-start = (bf16[11,2,16,512]{3,2,1,0:T(8,128)(2,1)S(1)}, bf16[11,2,16,512]{3,2,1,0:T(8,128)(2,1)S(1)}, u32[]{:S(2)}, u32[]{:S(2)}) collective-permute-start(bf16[11,2,16,512]{3,2,1,0:T(8,128)(2,1)S(1)} %get-tuple-element.20), channel_id=1, source_target_pairs={{0,1},{1,0},{2,3},{3,2},{4,5},{5,4},{6,7},{7,6},{8,9},{9,8},{10,11... | collective-permute-start | bytes 1081352 | tf_op jit(solution)/shard_map/ppermute | solution.py:275
  5.3 17.8 %collective-permute-start.1 = (bf16[11,2,16,512]{3,2,1,0:T(8,128)(2,1)S(1)}, bf16[11,2,16,512]{3,2,1,0:T(8,128)(2,1)S(1)}, u32[]{:S(2)}, u32[]{:S(2)}) collective-permute-start(bf16[11,2,16,512]{3,2,1,0:T(8,128)(2,1)S(1)} %get-tuple-element.21), channel_id=1, source_target_pairs={{0,3},{1,2},{2,1},{3,0},{4,7},{5,6},{6,5},{7,4},{8,11},{9,10},{10,... | collective-permute-start | bytes 1081352 | tf_op jit(solution)/shard_map/ppermute | solution.py:275
  7.4 1.1 %copy-start = (bf16[3,3,3,8192]{3,2,1,0:T(4,128)(2,1)S(1)}, bf16[3,3,3,8192]{3,2,1,0:T(4,128)(2,1)}, u32[]{:S(2)}) copy-start(bf16[3,3,3,8192]{3,2,1,0:T(4,128)(2,1)} %down_ref.1) | copy-start | bytes 1327108
  8.5 1.0 %copy-start.1 = (bf16[3,3,3,4096]{3,2,1,0:T(4,128)(2,1)S(1)}, bf16[3,3,3,4096]{3,2,1,0:T(4,128)(2,1)}, u32[]{:S(2)}) copy-start(bf16[3,3,3,4096]{3,2,1,0:T(4,128)(2,1)} %conv_ref.1) | copy-start | bytes 663556
  14.9 14.1 %collective-permute-start.2 = (bf16[11,2,16,512]{3,2,1,0:T(8,128)(2,1)S(1)}, bf16[11,2,16,512]{3,2,1,0:T(8,128)(2,1)S(1)}, u32[]{:S(2)}, u32[]{:S(2)}) collective-permute-start(bf16[11,2,16,512]{3,2,1,0:T(8,128)(2,1)S(1)} %get-tuple-element.23.refs_1_), channel_id=1, source_target_pairs={{0,4},{8,12},{4,0},{12,8},{1,5},{9,13},{5,1},{13,9},{2,6},{10,14},... | collective-permute-start | bytes 1081352 | tf_op jit(solution)/shard_map/ppermute | solution.py:197
  16.2 12.8 %collective-permute-start.3 = (bf16[11,2,16,512]{3,2,1,0:T(8,128)(2,1)S(1)}, bf16[11,2,16,512]{3,2,1,0:T(8,128)(2,1)S(1)}, u32[]{:S(2)}, u32[]{:S(2)}) collective-permute-start(bf16[11,2,16,512]{3,2,1,0:T(8,128)(2,1)S(1)} %get-tuple-element.23.refs_1_), channel_id=1, source_target_pairs={{4,8},{8,4},{5,9},{9,5},{6,10},{10,6},{7,11},{11,7},{20,24},{24,20... | collective-permute-start | bytes 1081352 | tf_op jit(solution)/shard_map/ppermute | solution.py:197
  19.2 20.5 %collective-permute-start.4 = (bf16[11,2,16,512]{3,2,1,0:T(8,128)(2,1)S(1)}, bf16[11,2,16,512]{3,2,1,0:T(8,128)(2,1)S(1)}, u32[]{:S(2)}, u32[]{:S(2)}) collective-permute-start(bf16[11,2,16,512]{3,2,1,0:T(8,128)(2,1)S(1)} %get-tuple-element.25), channel_id=1, source_target_pairs={{0,2},{1,3},{2,0},{3,1},{4,6},{5,7},{6,4},{7,5},{8,10},{9,11},{10,... | collective-permute-start | bytes 1081352 | tf_op jit(solution)/shard_map/ppermute | solution.py:275
  23.1 20.3 %collective-permute-start.5 = (bf16[22,2,16,512]{3,2,1,0:T(8,128)(2,1)S(1)}, bf16[22,2,16,512]{3,2,1,0:T(8,128)(2,1)S(1)}, u32[]{:S(2)}, u32[]{:S(2)}) collective-permute-start(bf16[22,2,16,512]{3,2,1,0:T(8,128)(2,1)S(1)} %shard_map.39.refs_2_), channel_id=1, source_target_pairs={{0,4},{8,12},{4,0},{12,8},{1,5},{9,13},{5,1},{13,9},{2,6},{10,14},... | collective-permute-start | bytes 2162696 | tf_op jit(solution)/shard_map/ppermute | solution.py:197
  25.9 17.5 %collective-permute-start.6 = (bf16[22,2,16,512]{3,2,1,0:T(8,128)(2,1)S(1)}, bf16[22,2,16,512]{3,2,1,0:T(8,128)(2,1)S(1)}, u32[]{:S(2)}, u32[]{:S(2)}) collective-permute-start(bf16[22,2,16,512]{3,2,1,0:T(8,128)(2,1)S(1)} %shard_map.39.refs_2_), channel_id=1, source_target_pairs={{4,8},{8,4},{5,9},{9,5},{6,10},{10,6},{7,11},{11,7},{20,24},{24,20... | collective-permute-start | bytes 2162696 | tf_op jit(solution)/shard_map/ppermute | solution.py:197
  39.7 6.3 %collective-permute-start.7 = (bf16[11,2,16,512]{3,2,1,0:T(8,128)(2,1)S(1)}, bf16[11,2,16,512]{3,2,1,0:T(8,128)(2,1)S(1)}, u32[]{:S(2)}, u32[]{:S(2)}) collective-permute-start(bf16[11,2,16,512]{3,2,1,0:T(8,128)(2,1)S(1)} %collective-permute-done.4.refs_2_), channel_id=1, source_target_pairs={{0,4},{8,12},{4,0},{12,8},{1,5},{9,13},{5,1},{13,9},{2,6},{10,14},... | collective-permute-start | bytes 1081352 | tf_op jit(solution)/shard_map/ppermute | solution.py:197
  40.1 8.7 %collective-permute-start.8 = (bf16[11,2,16,512]{3,2,1,0:T(8,128)(2,1)S(1)}, bf16[11,2,16,512]{3,2,1,0:T(8,128)(2,1)S(1)}, u32[]{:S(2)}, u32[]{:S(2)}) collective-permute-start(bf16[11,2,16,512]{3,2,1,0:T(8,128)(2,1)S(1)} %collective-permute-done.4.refs_2_), channel_id=1, source_target_pairs={{4,8},{8,4},{5,9},{9,5},{6,10},{10,6},{7,11},{11,7},{20,24},{24,20... | collective-permute-start | bytes 1081352 | tf_op jit(solution)/shard_map/ppermute | solution.py:197

commit v7 on v6

--- a/solution.py
+++ b/solution.py
@@ -41,13 +41,18 @@
     ]
     for copy in copies:
         copy.start()
-    split, turn = split_matrix(width), turn_matrix(count, step)
+    part = width // 2
+    split, turn = split_matrix(part), turn_matrix(count, step)
     field_ref[pl.ds(0, BELOW)] = jnp.zeros((BELOW, planes, count, width), jnp.bfloat16)
     field_ref[pl.ds(BELOW + all_rows, ABOVE)] = jnp.zeros((ABOVE, planes, count, width), jnp.bfloat16)
     for i, (p, at) in enumerate(places):
         copies[i].wait()
         block = block_ref[i].reshape(count * step, width)
+        block = jnp.concatenate([block[:, :part], block[:, part:]])
         block = jnp.dot(block, split, preferred_element_type=jnp.float32).astype(jnp.bfloat16)
+        left, right = block[: count * step], block[count * step :]
+        cut = part // 2
+        block = jnp.concatenate([left[:, :cut], right[:, :cut], left[:, cut:], right[:, cut:]], axis=1)
         block = jnp.dot(turn, block, preferred_element_type=jnp.float32).astype(jnp.bfloat16)
         field_ref[pl.ds(BELOW + at, step), p] = block.reshape(step, count, width)
     me = lax.axis_index("filt")
@@ -217,7 +222,7 @@
     params = pltpu.CompilerParams(vmem_limit_bytes=VMEM_LIMIT)
     cost = pl.CostEstimate(flops=1, transcendentals=0, bytes_accessed=1)
     direct = count == 16 and bands == 4
-    distances = (0, 1, 3, 2) if direct else ()
+    distances = (0, 3, 1, 2) if direct else ()
     ranges = [(0, 48), (0, 16), (16, 32), (48, 16)] if direct else [(0, C)]
     lay = pl.pallas_call(
         functools.partial(weight_kernel, distances, ranges),

time: 51.8 us -> 50.8 us (0.981)
  starting transfers between devices: 18.3 us -> 16.5 us
  waiting for transfers between devices: 14.2 us -> 14.9 us
    ppermute x6, starting transfers between devices: 13.9 us -> 11.7 us  [swapped(): lax.ppermute(block, axis, pairs + [(j, i) for i, j in pairs])]
    ppermute x3, waiting for transfers between devices: 11.3 us -> 11.9 us  [local(): piece = lax.ppermute(piece, 'filt', [(i, i ^ d) for i in range(bands)])]
where the time goes in v7:
time: 50.8 us; the launch traced here: 50.6 us
  starting transfers between devices  16.5 us (32%)
  Pallas kernels  16.1 us (32%)
  waiting for transfers between devices  14.9 us (29%)
  local copies, waits for them, and re-layouts  2.93 us (6%)
    ppermute x3, waiting for transfers between devices, local(): piece = lax.ppermute(piece, 'filt', [(i, i ^ d) for i in range(bands)])  11.9 us
    ppermute x6, starting transfers between devices, swapped(): lax.ppermute(block, axis, pairs + [(j, i) for i, j in pairs])  11.7 us
    pallas_call x3, Pallas kernels, convolve(): pl.pallas_call(functools.partial(conv_kernel, kinds, window, feature is N...  7.51 us
    pallas_call x1, Pallas kernels, local(): second, *firsts = lay(conv_weight, down_weight)  5.37 us
    ppermute x3, starting transfers between devices, local(): piece = lax.ppermute(piece, 'filt', [(i, i ^ d) for i in range(bands)])  4.78 us
    pallas_call x1, Pallas kernels, local(): pl.pallas_call(functools.partial(send_kernel, band, distances), out_shape...  3.2 us
    ppermute x6, waiting for transfers between devices, swapped(): lax.ppermute(block, axis, pairs + [(j, i) for i, j in pairs])  2.96 us
    unnamed x4, local copies, waits for them, and re-layouts  2.03 us
  transfers between devices with their start and end apart: 9, of which 3 were waited for; matrix products, arithmetic and copies ran while one was open for 0% of the time, Pallas kernels for 22%

profile of v7, /device:TPU:1, one launch (start us, length us, event | category | flops | bytes accessed | tf_op | source)
XLA Modules:
  0.0 50.6 jit_solution(7749921606439267683)
XLA Ops:
  0.0 3.2 %shard_map.38 = (bf16[11,2,16,512]{3,2,1,0:T(8,128)(2,1)S(1)}, bf16[11,2,16,512]{3,2,1,0:T(8,128)(2,1)S(1)}, bf16[11,2,16,512]{3,2,1,0:T(8,128)(2,1)S(1)}, bf16[11,2,16,512]{3,2,1,0:T(8,128)(2,1)S(1)}) custom-call(bf16[16,2,32,512]{3,2,1,0:T(8,128)(2,1)} %volume_ref.1), custom_call_target="tpu_custom_call" | custom-call | flops 1 | bytes 1 | tf_op jit(solution)/shard_map/pallas_call | solution.py:263
  3.2 4.3 %collective-permute-start = (bf16[11,2,16,512]{3,2,1,0:T(8,128)(2,1)S(1)}, bf16[11,2,16,512]{3,2,1,0:T(8,128)(2,1)S(1)}, u32[]{:S(2)}, u32[]{:S(2)}) collective-permute-start(bf16[11,2,16,512]{3,2,1,0:T(8,128)(2,1)S(1)} %get-tuple-element.20), channel_id=1, source_target_pairs={{0,3},{1,2},{2,1},{3,0},{4,7},{5,6},{6,5},{7,4},{8,11},{9,10},{10,... | collective-permute-start | bytes 1081352 | tf_op jit(solution)/shard_map/ppermute | solution.py:280
  7.5 0.0 collective-permute-start.1
  7.5 0.0 copy-start
  7.5 1.1 %copy-done = bf16[3,3,3,8192]{3,2,1,0:T(4,128)(2,1)S(1)} copy-done((bf16[3,3,3,8192]{3,2,1,0:T(4,128)(2,1)S(1)}, bf16[3,3,3,8192]{3,2,1,0:T(4,128)(2,1)}, u32[]{:S(2)}) %copy-start) | copy-done | bytes 442392
  8.5 0.0 copy-start.1
  8.5 1.0 %copy-done.1 = bf16[3,3,3,4096]{3,2,1,0:T(4,128)(2,1)S(1)} copy-done((bf16[3,3,3,4096]{3,2,1,0:T(4,128)(2,1)S(1)}, bf16[3,3,3,4096]{3,2,1,0:T(4,128)(2,1)}, u32[]{:S(2)}) %copy-start.1) | copy-done | bytes 221208
  9.5 5.4 %shard_map.37 = (bf16[128,1792]{1,0:T(8,128)(2,1)S(1)}, bf16[384,576]{1,0:T(8,128)(2,1)S(1)}, bf16[384,192]{1,0:T(8,128)(2,1)S(1)}, bf16[384,384]{1,0:T(8,128)(2,1)S(1)}, bf16[384,192]{1,0:T(8,128)(2,1)S(1)}) custom-call(bf16[3,3,3,4096]{3,2,1,0:T(4,128)(2,1)S(1)} %copy-done.1, bf16[3,3,3,8192]{3,2,1,0:T(4,128)(2,1)S(1)} %copy-done), custom_call_target="tpu_custom_call" | custom-call | flops 1 | bytes 1 | tf_op jit(solution)/shard_map/pallas_call | solution.py:276
  14.9 1.0 %collective-permute-start.2 = (bf16[11,2,16,512]{3,2,1,0:T(8,128)(2,1)S(1)}, bf16[11,2,16,512]{3,2,1,0:T(8,128)(2,1)S(1)}, u32[]{:S(2)}, u32[]{:S(2)}) collective-permute-start(bf16[11,2,16,512]{3,2,1,0:T(8,128)(2,1)S(1)} %get-tuple-element.23.refs_1_), channel_id=1, source_target_pairs={{0,4},{8,12},{4,0},{12,8},{1,5},{9,13},{5,1},{13,9},{2,6},{10,14},... | collective-permute-start | bytes 1081352 | tf_op jit(solution)/shard_map/ppermute | solution.py:202
  15.9 3.0 %collective-permute-start.3 = (bf16[11,2,16,512]{3,2,1,0:T(8,128)(2,1)S(1)}, bf16[11,2,16,512]{3,2,1,0:T(8,128)(2,1)S(1)}, u32[]{:S(2)}, u32[]{:S(2)}) collective-permute-start(bf16[11,2,16,512]{3,2,1,0:T(8,128)(2,1)S(1)} %get-tuple-element.23.refs_1_), channel_id=1, source_target_pairs={{4,8},{8,4},{5,9},{9,5},{6,10},{10,6},{7,11},{11,7},{20,24},{24,20... | collective-permute-start | bytes 1081352 | tf_op jit(solution)/shard_map/ppermute | solution.py:202
  18.9 0.5 %collective-permute-start.4 = (bf16[11,2,16,512]{3,2,1,0:T(8,128)(2,1)S(1)}, bf16[11,2,16,512]{3,2,1,0:T(8,128)(2,1)S(1)}, u32[]{:S(2)}, u32[]{:S(2)}) collective-permute-start(bf16[11,2,16,512]{3,2,1,0:T(8,128)(2,1)S(1)} %get-tuple-element.25), channel_id=1, source_target_pairs={{0,2},{1,3},{2,0},{3,1},{4,6},{5,7},{6,4},{7,5},{8,10},{9,11},{10,... | collective-permute-start | bytes 1081352 | tf_op jit(solution)/shard_map/ppermute | solution.py:280
  19.4 0.0 collective-permute-done.one_ref
  19.4 5.8 %collective-permute-done.1.two_ref = bf16[11,2,16,512]{3,2,1,0:T(8,128)(2,1)S(1)} collective-permute-done((bf16[11,2,16,512]{3,2,1,0:T(8,128)(2,1)S(1)}, bf16[11,2,16,512]{3,2,1,0:T(8,128)(2,1)S(1)}, u32[]{:S(2)}, u32[]{:S(2)}) %collective-permute-start.1) | collective-permute-done | bytes 360480 | tf_op jit(solution)/shard_map/ppermute | solution.py:280
  25.3 0.6 %collective-permute-start.5 = (bf16[22,2,16,512]{3,2,1,0:T(8,128)(2,1)S(1)}, bf16[22,2,16,512]{3,2,1,0:T(8,128)(2,1)S(1)}, u32[]{:S(2)}, u32[]{:S(2)}) collective-permute-start(bf16[22,2,16,512]{3,2,1,0:T(8,128)(2,1)S(1)} %shard_map.39.refs_2_), channel_id=1, source_target_pairs={{0,4},{8,12},{4,0},{12,8},{1,5},{9,13},{5,1},{13,9},{2,6},{10,14},... | collective-permute-start | bytes 2162696 | tf_op jit(solution)/shard_map/ppermute | solution.py:202
  25.8 2.9 %collective-permute-start.6 = (bf16[22,2,16,512]{3,2,1,0:T(8,128)(2,1)S(1)}, bf16[22,2,16,512]{3,2,1,0:T(8,128)(2,1)S(1)}, u32[]{:S(2)}, u32[]{:S(2)}) collective-permute-start(bf16[22,2,16,512]{3,2,1,0:T(8,128)(2,1)S(1)} %shard_map.39.refs_2_), channel_id=1, source_target_pairs={{4,8},{8,4},{5,9},{9,5},{6,10},{10,6},{7,11},{11,7},{20,24},{24,20... | collective-permute-start | bytes 2162696 | tf_op jit(solution)/shard_map/ppermute | solution.py:202
  28.8 0.0 collective-permute-done.2.refs_4_
  28.8 0.0 collective-permute-done.3.refs_5_
  28.8 3.2 %shard_map.40.refs_0_ = f32[3456,256]{1,0:T(8,128)S(1)} custom-call(bf16[384,576]{1,0:T(8,128)(2,1)S(1)} %get-tuple-element.18.refs_0_, bf16[11,2,16,512]{3,2,1,0:T(8,128)(2,1)S(1)} %get-tuple-element.23.refs_1_, bf16[22,2,16,512]{3,2,1,0:T(8,128)(2,1)S(1)} %shard_map.39.refs_2_, bf16[384,192]{1,0:T(8,128)(2,1)S(1)} %get-tuple-element.22.refs_3_, ...), custom_call_target="tpu_custom_call" | custom-call | flops 8589934592 | bytes 16777216 | tf_op jit(solution)/shard_map/pallas_call | solution.py:251
  32.0 6.1 %collective-permute-done.4.refs_2_ = bf16[11,2,16,512]{3,2,1,0:T(8,128)(2,1)S(1)} collective-permute-done((bf16[11,2,16,512]{3,2,1,0:T(8,128)(2,1)S(1)}, bf16[11,2,16,512]{3,2,1,0:T(8,128)(2,1)S(1)}, u32[]{:S(2)}, u32[]{:S(2)}) %collective-permute-start.4) | collective-permute-done | bytes 360480 | tf_op jit(solution)/shard_map/ppermute | solution.py:280
  38.1 1.0 %collective-permute-start.7 = (bf16[11,2,16,512]{3,2,1,0:T(8,128)(2,1)S(1)}, bf16[11,2,16,512]{3,2,1,0:T(8,128)(2,1)S(1)}, u32[]{:S(2)}, u32[]{:S(2)}) collective-permute-start(bf16[11,2,16,512]{3,2,1,0:T(8,128)(2,1)S(1)} %collective-permute-done.4.refs_2_), channel_id=1, source_target_pairs={{0,4},{8,12},{4,0},{12,8},{1,5},{9,13},{5,1},{13,9},{2,6},{10,14},... | collective-permute-start | bytes 1081352 | tf_op jit(solution)/shard_map/ppermute | solution.py:202
  39.1 3.2 %collective-permute-start.8 = (bf16[11,2,16,512]{3,2,1,0:T(8,128)(2,1)S(1)}, bf16[11,2,16,512]{3,2,1,0:T(8,128)(2,1)S(1)}, u32[]{:S(2)}, u32[]{:S(2)}) collective-permute-start(bf16[11,2,16,512]{3,2,1,0:T(8,128)(2,1)S(1)} %collective-permute-done.4.refs_2_), channel_id=1, source_target_pairs={{4,8},{8,4},{5,9},{9,5},{6,10},{10,6},{7,11},{11,7},{20,24},{24,20... | collective-permute-start | bytes 1081352 | tf_op jit(solution)/shard_map/ppermute | solution.py:202
  42.3 0.0 collective-permute-done.5.refs_4_
  42.3 0.0 collective-permute-done.6.refs_5_
  42.3 2.6 %shard_map.41.refs_0_ = f32[3456,256]{1,0:T(8,128)S(1)} custom-call(f32[3456,256]{1,0:T(8,128)S(1)} %shard_map.40.refs_0_, bf16[384,192]{1,0:T(8,128)(2,1)S(1)} %get-tuple-element.24.refs_1_.refs_2_, bf16[11,2,16,512]{3,2,1,0:T(8,128)(2,1)S(1)} %collective-permute-done.4.refs_2_, bf16[384,384]{1,0:T(8,128)(2,1)S(1)} %get-tuple-element.26.refs_3_, ...), custom_call_target="tpu_custom_call" | custom-call | flops 8589934592 | bytes 16777216 | tf_op jit(solution)/shard_map/pallas_call | solution.py:251
  44.9 0.0 collective-permute-done.7.refs_3_
  44.9 3.0 %collective-permute-done.8.refs_4_ = bf16[11,2,16,512]{3,2,1,0:T(8,128)(2,1)S(1)} collective-permute-done((bf16[11,2,16,512]{3,2,1,0:T(8,128)(2,1)S(1)}, bf16[11,2,16,512]{3,2,1,0:T(8,128)(2,1)S(1)}, u32[]{:S(2)}, u32[]{:S(2)}) %collective-permute-start.8) | collective-permute-done | bytes 360480 | tf_op jit(solution)/shard_map/ppermute | solution.py:202
  47.9 1.8 %shard_map.42 = bf16[4,128,256]{2,1,0:T(8,128)(2,1)S(1)} custom-call(f32[3456,256]{1,0:T(8,128)S(1)} %shard_map.41.refs_0_, bf16[128,1792]{1,0:T(8,128)(2,1)S(1)} %get-tuple-element.29.refs_1_, bf16[384,192]{1,0:T(8,128)(2,1)S(1)} %get-tuple-element.24.refs_1_.refs_2_, bf16[11,2,16,512]{3,2,1,0:T(8,128)(2,1)S(1)} %collective-permute-done.7.refs_3_, ...), custom_call_target="tpu_custom_call" | custom-call | flops 8589934592 | bytes 16777216 | tf_op jit(solution)/shard_map/pallas_call | solution.py:251
  49.7 0.9 %copy.4 = bf16[128,1,4,256]{3,2,1,0:T(4,128)(2,1)} copy(bf16[128,1,4,256]{3,0,2,1:T(8,128)(2,1)S(1)} %bitcast.3) | data formatting | bytes 524288 | tf_op jit(solution)/shard_map/broadcast_in_dim | solution.py:322
  (1 shorter events, 0.0 us)
Async XLA Ops:
  3.2 16.2 %collective-permute-start = (bf16[11,2,16,512]{3,2,1,0:T(8,128)(2,1)S(1)}, bf16[11,2,16,512]{3,2,1,0:T(8,128)(2,1)S(1)}, u32[]{:S(2)}, u32[]{:S(2)}) collective-permute-start(bf16[11,2,16,512]{3,2,1,0:T(8,128)(2,1)S(1)} %get-tuple-element.20), channel_id=1, source_target_pairs={{0,3},{1,2},{2,1},{3,0},{4,7},{5,6},{6,5},{7,4},{8,11},{9,10},{10,... | collective-permute-start | bytes 1081352 | tf_op jit(solution)/shard_map/ppermute | solution.py:280
  7.5 17.8 %collective-permute-start.1 = (bf16[11,2,16,512]{3,2,1,0:T(8,128)(2,1)S(1)}, bf16[11,2,16,512]{3,2,1,0:T(8,128)(2,1)S(1)}, u32[]{:S(2)}, u32[]{:S(2)}) collective-permute-start(bf16[11,2,16,512]{3,2,1,0:T(8,128)(2,1)S(1)} %get-tuple-element.21), channel_id=1, source_target_pairs={{0,1},{1,0},{2,3},{3,2},{4,5},{5,4},{6,7},{7,6},{8,9},{9,8},{10,11... | collective-permute-start | bytes 1081352 | tf_op jit(solution)/shard_map/ppermute | solution.py:280
  7.5 1.1 %copy-start = (bf16[3,3,3,8192]{3,2,1,0:T(4,128)(2,1)S(1)}, bf16[3,3,3,8192]{3,2,1,0:T(4,128)(2,1)}, u32[]{:S(2)}) copy-start(bf16[3,3,3,8192]{3,2,1,0:T(4,128)(2,1)} %down_ref.1) | copy-start | bytes 1327108
  8.5 1.0 %copy-start.1 = (bf16[3,3,3,4096]{3,2,1,0:T(4,128)(2,1)S(1)}, bf16[3,3,3,4096]{3,2,1,0:T(4,128)(2,1)}, u32[]{:S(2)}) copy-start(bf16[3,3,3,4096]{3,2,1,0:T(4,128)(2,1)} %conv_ref.1) | copy-start | bytes 663556
  14.9 13.9 %collective-permute-start.2 = (bf16[11,2,16,512]{3,2,1,0:T(8,128)(2,1)S(1)}, bf16[11,2,16,512]{3,2,1,0:T(8,128)(2,1)S(1)}, u32[]{:S(2)}, u32[]{:S(2)}) collective-permute-start(bf16[11,2,16,512]{3,2,1,0:T(8,128)(2,1)S(1)} %get-tuple-element.23.refs_1_), channel_id=1, source_target_pairs={{0,4},{8,12},{4,0},{12,8},{1,5},{9,13},{5,1},{13,9},{2,6},{10,14},... | collective-permute-start | bytes 1081352 | tf_op jit(solution)/shard_map/ppermute | solution.py:202
  15.9 12.9 %collective-permute-start.3 = (bf16[11,2,16,512]{3,2,1,0:T(8,128)(2,1)S(1)}, bf16[11,2,16,512]{3,2,1,0:T(8,128)(2,1)S(1)}, u32[]{:S(2)}, u32[]{:S(2)}) collective-permute-start(bf16[11,2,16,512]{3,2,1,0:T(8,128)(2,1)S(1)} %get-tuple-element.23.refs_1_), channel_id=1, source_target_pairs={{4,8},{8,4},{5,9},{9,5},{6,10},{10,6},{7,11},{11,7},{20,24},{24,20... | collective-permute-start | bytes 1081352 | tf_op jit(solution)/shard_map/ppermute | solution.py:202
  18.9 19.2 %collective-permute-start.4 = (bf16[11,2,16,512]{3,2,1,0:T(8,128)(2,1)S(1)}, bf16[11,2,16,512]{3,2,1,0:T(8,128)(2,1)S(1)}, u32[]{:S(2)}, u32[]{:S(2)}) collective-permute-start(bf16[11,2,16,512]{3,2,1,0:T(8,128)(2,1)S(1)} %get-tuple-element.25), channel_id=1, source_target_pairs={{0,2},{1,3},{2,0},{3,1},{4,6},{5,7},{6,4},{7,5},{8,10},{9,11},{10,... | collective-permute-start | bytes 1081352 | tf_op jit(solution)/shard_map/ppermute | solution.py:280
  25.3 17.0 %collective-permute-start.5 = (bf16[22,2,16,512]{3,2,1,0:T(8,128)(2,1)S(1)}, bf16[22,2,16,512]{3,2,1,0:T(8,128)(2,1)S(1)}, u32[]{:S(2)}, u32[]{:S(2)}) collective-permute-start(bf16[22,2,16,512]{3,2,1,0:T(8,128)(2,1)S(1)} %shard_map.39.refs_2_), channel_id=1, source_target_pairs={{0,4},{8,12},{4,0},{12,8},{1,5},{9,13},{5,1},{13,9},{2,6},{10,14},... | collective-permute-start | bytes 2162696 | tf_op jit(solution)/shard_map/ppermute | solution.py:202
  25.8 16.5 %collective-permute-start.6 = (bf16[22,2,16,512]{3,2,1,0:T(8,128)(2,1)S(1)}, bf16[22,2,16,512]{3,2,1,0:T(8,128)(2,1)S(1)}, u32[]{:S(2)}, u32[]{:S(2)}) collective-permute-start(bf16[22,2,16,512]{3,2,1,0:T(8,128)(2,1)S(1)} %shard_map.39.refs_2_), channel_id=1, source_target_pairs={{4,8},{8,4},{5,9},{9,5},{6,10},{10,6},{7,11},{11,7},{20,24},{24,20... | collective-permute-start | bytes 2162696 | tf_op jit(solution)/shard_map/ppermute | solution.py:202
  38.1 6.8 %collective-permute-start.7 = (bf16[11,2,16,512]{3,2,1,0:T(8,128)(2,1)S(1)}, bf16[11,2,16,512]{3,2,1,0:T(8,128)(2,1)S(1)}, u32[]{:S(2)}, u32[]{:S(2)}) collective-permute-start(bf16[11,2,16,512]{3,2,1,0:T(8,128)(2,1)S(1)} %collective-permute-done.4.refs_2_), channel_id=1, source_target_pairs={{0,4},{8,12},{4,0},{12,8},{1,5},{9,13},{5,1},{13,9},{2,6},{10,14},... | collective-permute-start | bytes 1081352 | tf_op jit(solution)/shard_map/ppermute | solution.py:202
  39.1 8.7 %collective-permute-start.8 = (bf16[11,2,16,512]{3,2,1,0:T(8,128)(2,1)S(1)}, bf16[11,2,16,512]{3,2,1,0:T(8,128)(2,1)S(1)}, u32[]{:S(2)}, u32[]{:S(2)}) collective-permute-start(bf16[11,2,16,512]{3,2,1,0:T(8,128)(2,1)S(1)} %collective-permute-done.4.refs_2_), channel_id=1, source_target_pairs={{4,8},{8,4},{5,9},{9,5},{6,10},{10,6},{7,11},{11,7},{20,24},{24,20... | collective-permute-start | bytes 1081352 | tf_op jit(solution)/shard_map/ppermute | solution.py:202

commit v8 on v6

--- a/solution.py
+++ b/solution.py
@@ -41,14 +41,20 @@
     ]
     for copy in copies:
         copy.start()
-    split, turn = split_matrix(width), turn_matrix(count, step)
+    turn = turn_matrix(count, step)
     field_ref[pl.ds(0, BELOW)] = jnp.zeros((BELOW, planes, count, width), jnp.bfloat16)
     field_ref[pl.ds(BELOW + all_rows, ABOVE)] = jnp.zeros((ABOVE, planes, count, width), jnp.bfloat16)
+    for copy in copies:
+        copy.wait()
+    size = count * step
+    wide = jnp.concatenate([block_ref[i].reshape(size, width) for i in range(len(places))], axis=1)
+    wide = jnp.dot(turn, wide, preferred_element_type=jnp.float32).astype(jnp.bfloat16)
+    tall = jnp.concatenate([wide[:, i * width // 2 : (i + 1) * width // 2] for i in range(2 * len(places))])
+    tall = jnp.dot(tall, split_matrix(width // 2), preferred_element_type=jnp.float32).astype(jnp.bfloat16)
+    cut = width // 4
     for i, (p, at) in enumerate(places):
-        copies[i].wait()
-        block = block_ref[i].reshape(count * step, width)
-        block = jnp.dot(block, split, preferred_element_type=jnp.float32).astype(jnp.bfloat16)
-        block = jnp.dot(turn, block, preferred_element_type=jnp.float32).astype(jnp.bfloat16)
+        left, right = tall[2 * i * size : (2 * i + 1) * size], tall[(2 * i + 1) * size : (2 * i + 2) * size]
+        block = jnp.concatenate([left[:, :cut], right[:, :cut], left[:, cut:], right[:, cut:]], axis=1)
         field_ref[pl.ds(BELOW + at, step), p] = block.reshape(step, count, width)
     me = lax.axis_index("filt")
     for d, out_ref in zip(distances, out_refs):
@@ -217,7 +223,7 @@
     params = pltpu.CompilerParams(vmem_limit_bytes=VMEM_LIMIT)
     cost = pl.CostEstimate(flops=1, transcendentals=0, bytes_accessed=1)
     direct = count == 16 and bands == 4
-    distances = (0, 1, 3, 2) if direct else ()
+    distances = (0, 3, 1, 2) if direct else ()
     ranges = [(0, 48), (0, 16), (16, 32), (48, 16)] if direct else [(0, C)]
     lay = pl.pallas_call(
         functools.partial(weight_kernel, distances, ranges),

time: 51.8 us -> 49.7 us (0.959)
  starting transfers between devices: 18.3 us -> 16.5 us
  Pallas kernels: 16 us -> 15 us
  waiting for transfers between devices: 14.2 us -> 14.9 us
    ppermute x6, starting transfers between devices: 13.9 us -> 11.7 us  [swapped(): lax.ppermute(block, axis, pairs + [(j, i) for i, j in pairs])]
    pallas_call x1, Pallas kernels: 3.05 us -> 2.07 us  [local(): pl.pallas_call(functools.partial(send_kernel, band, distances), out_shape...]
    ppermute x3, waiting for transfers between devices: 11.3 us -> 11.9 us  [local(): piece = lax.ppermute(piece, 'filt', [(i, i ^ d) for i in range(bands)])]
  transfers between devices with their start and end apart: 9 -> 9, of which waited for: 3 -> 3; matrix products, arithmetic and copies ran while one was open for 0% -> 0% of each run, Pallas kernels for 22% -> 23%
where the time goes in v8:
time: 49.7 us; the launch traced here: 49.4 us
  starting transfers between devices  16.5 us (33%)
  Pallas kernels  15 us (30%)
  waiting for transfers between devices  14.9 us (30%)
  local copies, waits for them, and re-layouts  2.93 us (6%)
    ppermute x3, waiting for transfers between devices, local(): piece = lax.ppermute(piece, 'filt', [(i, i ^ d) for i in range(bands)])  11.9 us
    ppermute x6, starting transfers between devices, swapped(): lax.ppermute(block, axis, pairs + [(j, i) for i, j in pairs])  11.7 us
    pallas_call x3, Pallas kernels, convolve(): pl.pallas_call(functools.partial(conv_kernel, kinds, window, feature is N...  7.51 us
    pallas_call x1, Pallas kernels, local(): second, *firsts = lay(conv_weight, down_weight)  5.37 us
    ppermute x3, starting transfers between devices, local(): piece = lax.ppermute(piece, 'filt', [(i, i ^ d) for i in range(bands)])  4.78 us
    ppermute x6, waiting for transfers between devices, swapped(): lax.ppermute(block, axis, pairs + [(j, i) for i, j in pairs])  2.97 us
    pallas_call x1, Pallas kernels, local(): pl.pallas_call(functools.partial(send_kernel, band, distances), out_shape...  2.07 us
    unnamed x4, local copies, waits for them, and re-layouts  2.03 us
  transfers between devices with their start and end apart: 9, of which 3 were waited for; matrix products, arithmetic and copies ran while one was open for 0% of the time, Pallas kernels for 23%

profile of v8, /device:TPU:1, one launch (start us, length us, event | category | flops | bytes accessed | tf_op | source)
XLA Modules:
  0.0 49.4 jit_solution(9120705189684291333)
XLA Ops:
  0.0 2.1 %shard_map.38 = (bf16[11,2,16,512]{3,2,1,0:T(8,128)(2,1)S(1)}, bf16[11,2,16,512]{3,2,1,0:T(8,128)(2,1)S(1)}, bf16[11,2,16,512]{3,2,1,0:T(8,128)(2,1)S(1)}, bf16[11,2,16,512]{3,2,1,0:T(8,128)(2,1)S(1)}) custom-call(bf16[16,2,32,512]{3,2,1,0:T(8,128)(2,1)} %volume_ref.1), custom_call_target="tpu_custom_call" | custom-call | flops 1 | bytes 1 | tf_op jit(solution)/shard_map/pallas_call | solution.py:264
  2.1 4.2 %collective-permute-start = (bf16[11,2,16,512]{3,2,1,0:T(8,128)(2,1)S(1)}, bf16[11,2,16,512]{3,2,1,0:T(8,128)(2,1)S(1)}, u32[]{:S(2)}, u32[]{:S(2)}) collective-permute-start(bf16[11,2,16,512]{3,2,1,0:T(8,128)(2,1)S(1)} %get-tuple-element.20), channel_id=1, source_target_pairs={{0,3},{1,2},{2,1},{3,0},{4,7},{5,6},{6,5},{7,4},{8,11},{9,10},{10,... | collective-permute-start | bytes 1081352 | tf_op jit(solution)/shard_map/ppermute | solution.py:281
  6.3 0.0 collective-permute-start.1
  6.3 0.0 copy-start
  6.3 1.1 %copy-done = bf16[3,3,3,8192]{3,2,1,0:T(4,128)(2,1)S(1)} copy-done((bf16[3,3,3,8192]{3,2,1,0:T(4,128)(2,1)S(1)}, bf16[3,3,3,8192]{3,2,1,0:T(4,128)(2,1)}, u32[]{:S(2)}) %copy-start) | copy-done | bytes 442392
  7.4 0.0 copy-start.1
  7.4 1.0 %copy-done.1 = bf16[3,3,3,4096]{3,2,1,0:T(4,128)(2,1)S(1)} copy-done((bf16[3,3,3,4096]{3,2,1,0:T(4,128)(2,1)S(1)}, bf16[3,3,3,4096]{3,2,1,0:T(4,128)(2,1)}, u32[]{:S(2)}) %copy-start.1) | copy-done | bytes 221208
  8.3 5.4 %shard_map.37 = (bf16[128,1792]{1,0:T(8,128)(2,1)S(1)}, bf16[384,576]{1,0:T(8,128)(2,1)S(1)}, bf16[384,192]{1,0:T(8,128)(2,1)S(1)}, bf16[384,384]{1,0:T(8,128)(2,1)S(1)}, bf16[384,192]{1,0:T(8,128)(2,1)S(1)}) custom-call(bf16[3,3,3,4096]{3,2,1,0:T(4,128)(2,1)S(1)} %copy-done.1, bf16[3,3,3,8192]{3,2,1,0:T(4,128)(2,1)S(1)} %copy-done), custom_call_target="tpu_custom_call" | custom-call | flops 1 | bytes 1 | tf_op jit(solution)/shard_map/pallas_call | solution.py:277
  13.7 1.0 %collective-permute-start.2 = (bf16[11,2,16,512]{3,2,1,0:T(8,128)(2,1)S(1)}, bf16[11,2,16,512]{3,2,1,0:T(8,128)(2,1)S(1)}, u32[]{:S(2)}, u32[]{:S(2)}) collective-permute-start(bf16[11,2,16,512]{3,2,1,0:T(8,128)(2,1)S(1)} %get-tuple-element.23.refs_1_), channel_id=1, source_target_pairs={{0,4},{8,12},{4,0},{12,8},{1,5},{9,13},{5,1},{13,9},{2,6},{10,14},... | collective-permute-start | bytes 1081352 | tf_op jit(solution)/shard_map/ppermute | solution.py:203
  14.7 3.0 %collective-permute-start.3 = (bf16[11,2,16,512]{3,2,1,0:T(8,128)(2,1)S(1)}, bf16[11,2,16,512]{3,2,1,0:T(8,128)(2,1)S(1)}, u32[]{:S(2)}, u32[]{:S(2)}) collective-permute-start(bf16[11,2,16,512]{3,2,1,0:T(8,128)(2,1)S(1)} %get-tuple-element.23.refs_1_), channel_id=1, source_target_pairs={{4,8},{8,4},{5,9},{9,5},{6,10},{10,6},{7,11},{11,7},{20,24},{24,20... | collective-permute-start | bytes 1081352 | tf_op jit(solution)/shard_map/ppermute | solution.py:203
  17.8 0.6 %collective-permute-start.4 = (bf16[11,2,16,512]{3,2,1,0:T(8,128)(2,1)S(1)}, bf16[11,2,16,512]{3,2,1,0:T(8,128)(2,1)S(1)}, u32[]{:S(2)}, u32[]{:S(2)}) collective-permute-start(bf16[11,2,16,512]{3,2,1,0:T(8,128)(2,1)S(1)} %get-tuple-element.25), channel_id=1, source_target_pairs={{0,2},{1,3},{2,0},{3,1},{4,6},{5,7},{6,4},{7,5},{8,10},{9,11},{10,... | collective-permute-start | bytes 1081352 | tf_op jit(solution)/shard_map/ppermute | solution.py:281
  18.3 0.0 collective-permute-done.one_ref
  18.3 5.7 %collective-permute-done.1.two_ref = bf16[11,2,16,512]{3,2,1,0:T(8,128)(2,1)S(1)} collective-permute-done((bf16[11,2,16,512]{3,2,1,0:T(8,128)(2,1)S(1)}, bf16[11,2,16,512]{3,2,1,0:T(8,128)(2,1)S(1)}, u32[]{:S(2)}, u32[]{:S(2)}) %collective-permute-start.1) | collective-permute-done | bytes 360480 | tf_op jit(solution)/shard_map/ppermute | solution.py:281
  24.1 0.6 %collective-permute-start.5 = (bf16[22,2,16,512]{3,2,1,0:T(8,128)(2,1)S(1)}, bf16[22,2,16,512]{3,2,1,0:T(8,128)(2,1)S(1)}, u32[]{:S(2)}, u32[]{:S(2)}) collective-permute-start(bf16[22,2,16,512]{3,2,1,0:T(8,128)(2,1)S(1)} %shard_map.39.refs_2_), channel_id=1, source_target_pairs={{0,4},{8,12},{4,0},{12,8},{1,5},{9,13},{5,1},{13,9},{2,6},{10,14},... | collective-permute-start | bytes 2162696 | tf_op jit(solution)/shard_map/ppermute | solution.py:203
  24.7 2.9 %collective-permute-start.6 = (bf16[22,2,16,512]{3,2,1,0:T(8,128)(2,1)S(1)}, bf16[22,2,16,512]{3,2,1,0:T(8,128)(2,1)S(1)}, u32[]{:S(2)}, u32[]{:S(2)}) collective-permute-start(bf16[22,2,16,512]{3,2,1,0:T(8,128)(2,1)S(1)} %shard_map.39.refs_2_), channel_id=1, source_target_pairs={{4,8},{8,4},{5,9},{9,5},{6,10},{10,6},{7,11},{11,7},{20,24},{24,20... | collective-permute-start | bytes 2162696 | tf_op jit(solution)/shard_map/ppermute | solution.py:203
  27.6 0.0 collective-permute-done.2.refs_4_
  27.6 0.0 collective-permute-done.3.refs_5_
  27.6 3.2 %shard_map.40.refs_0_ = f32[3456,256]{1,0:T(8,128)S(1)} custom-call(bf16[384,576]{1,0:T(8,128)(2,1)S(1)} %get-tuple-element.18.refs_0_, bf16[11,2,16,512]{3,2,1,0:T(8,128)(2,1)S(1)} %get-tuple-element.23.refs_1_, bf16[22,2,16,512]{3,2,1,0:T(8,128)(2,1)S(1)} %shard_map.39.refs_2_, bf16[384,192]{1,0:T(8,128)(2,1)S(1)} %get-tuple-element.22.refs_3_, ...), custom_call_target="tpu_custom_call" | custom-call | flops 8589934592 | bytes 16777216 | tf_op jit(solution)/shard_map/pallas_call | solution.py:252
  30.8 6.2 %collective-permute-done.4.refs_2_ = bf16[11,2,16,512]{3,2,1,0:T(8,128)(2,1)S(1)} collective-permute-done((bf16[11,2,16,512]{3,2,1,0:T(8,128)(2,1)S(1)}, bf16[11,2,16,512]{3,2,1,0:T(8,128)(2,1)S(1)}, u32[]{:S(2)}, u32[]{:S(2)}) %collective-permute-start.4) | collective-permute-done | bytes 360480 | tf_op jit(solution)/shard_map/ppermute | solution.py:281
  36.9 1.0 %collective-permute-start.7 = (bf16[11,2,16,512]{3,2,1,0:T(8,128)(2,1)S(1)}, bf16[11,2,16,512]{3,2,1,0:T(8,128)(2,1)S(1)}, u32[]{:S(2)}, u32[]{:S(2)}) collective-permute-start(bf16[11,2,16,512]{3,2,1,0:T(8,128)(2,1)S(1)} %collective-permute-done.4.refs_2_), channel_id=1, source_target_pairs={{0,4},{8,12},{4,0},{12,8},{1,5},{9,13},{5,1},{13,9},{2,6},{10,14},... | collective-permute-start | bytes 1081352 | tf_op jit(solution)/shard_map/ppermute | solution.py:203
  38.0 3.2 %collective-permute-start.8 = (bf16[11,2,16,512]{3,2,1,0:T(8,128)(2,1)S(1)}, bf16[11,2,16,512]{3,2,1,0:T(8,128)(2,1)S(1)}, u32[]{:S(2)}, u32[]{:S(2)}) collective-permute-start(bf16[11,2,16,512]{3,2,1,0:T(8,128)(2,1)S(1)} %collective-permute-done.4.refs_2_), channel_id=1, source_target_pairs={{4,8},{8,4},{5,9},{9,5},{6,10},{10,6},{7,11},{11,7},{20,24},{24,20... | collective-permute-start | bytes 1081352 | tf_op jit(solution)/shard_map/ppermute | solution.py:203
  41.2 0.0 collective-permute-done.5.refs_4_
  41.2 0.0 collective-permute-done.6.refs_5_
  41.2 2.6 %shard_map.41.refs_0_ = f32[3456,256]{1,0:T(8,128)S(1)} custom-call(f32[3456,256]{1,0:T(8,128)S(1)} %shard_map.40.refs_0_, bf16[384,192]{1,0:T(8,128)(2,1)S(1)} %get-tuple-element.24.refs_1_.refs_2_, bf16[11,2,16,512]{3,2,1,0:T(8,128)(2,1)S(1)} %collective-permute-done.4.refs_2_, bf16[384,384]{1,0:T(8,128)(2,1)S(1)} %get-tuple-element.26.refs_3_, ...), custom_call_target="tpu_custom_call" | custom-call | flops 8589934592 | bytes 16777216 | tf_op jit(solution)/shard_map/pallas_call | solution.py:252
  43.8 0.0 collective-permute-done.7.refs_3_
  43.8 3.0 %collective-permute-done.8.refs_4_ = bf16[11,2,16,512]{3,2,1,0:T(8,128)(2,1)S(1)} collective-permute-done((bf16[11,2,16,512]{3,2,1,0:T(8,128)(2,1)S(1)}, bf16[11,2,16,512]{3,2,1,0:T(8,128)(2,1)S(1)}, u32[]{:S(2)}, u32[]{:S(2)}) %collective-permute-start.8) | collective-permute-done | bytes 360480 | tf_op jit(solution)/shard_map/ppermute | solution.py:203
  46.7 1.8 %shard_map.42 = bf16[4,128,256]{2,1,0:T(8,128)(2,1)S(1)} custom-call(f32[3456,256]{1,0:T(8,128)S(1)} %shard_map.41.refs_0_, bf16[128,1792]{1,0:T(8,128)(2,1)S(1)} %get-tuple-element.29.refs_1_, bf16[384,192]{1,0:T(8,128)(2,1)S(1)} %get-tuple-element.24.refs_1_.refs_2_, bf16[11,2,16,512]{3,2,1,0:T(8,128)(2,1)S(1)} %collective-permute-done.7.refs_3_, ...), custom_call_target="tpu_custom_call" | custom-call | flops 8589934592 | bytes 16777216 | tf_op jit(solution)/shard_map/pallas_call | solution.py:252
  48.5 0.9 %copy.4 = bf16[128,1,4,256]{3,2,1,0:T(4,128)(2,1)} copy(bf16[128,1,4,256]{3,0,2,1:T(8,128)(2,1)S(1)} %bitcast.3) | data formatting | bytes 524288 | tf_op jit(solution)/shard_map/broadcast_in_dim | solution.py:323
  (1 shorter events, 0.0 us)
Async XLA Ops:
  2.1 16.2 %collective-permute-start = (bf16[11,2,16,512]{3,2,1,0:T(8,128)(2,1)S(1)}, bf16[11,2,16,512]{3,2,1,0:T(8,128)(2,1)S(1)}, u32[]{:S(2)}, u32[]{:S(2)}) collective-permute-start(bf16[11,2,16,512]{3,2,1,0:T(8,128)(2,1)S(1)} %get-tuple-element.20), channel_id=1, source_target_pairs={{0,3},{1,2},{2,1},{3,0},{4,7},{5,6},{6,5},{7,4},{8,11},{9,10},{10,... | collective-permute-start | bytes 1081352 | tf_op jit(solution)/shard_map/ppermute | solution.py:281
  6.3 17.7 %collective-permute-start.1 = (bf16[11,2,16,512]{3,2,1,0:T(8,128)(2,1)S(1)}, bf16[11,2,16,512]{3,2,1,0:T(8,128)(2,1)S(1)}, u32[]{:S(2)}, u32[]{:S(2)}) collective-permute-start(bf16[11,2,16,512]{3,2,1,0:T(8,128)(2,1)S(1)} %get-tuple-element.21), channel_id=1, source_target_pairs={{0,1},{1,0},{2,3},{3,2},{4,5},{5,4},{6,7},{7,6},{8,9},{9,8},{10,11... | collective-permute-start | bytes 1081352 | tf_op jit(solution)/shard_map/ppermute | solution.py:281
  6.3 1.1 %copy-start = (bf16[3,3,3,8192]{3,2,1,0:T(4,128)(2,1)S(1)}, bf16[3,3,3,8192]{3,2,1,0:T(4,128)(2,1)}, u32[]{:S(2)}) copy-start(bf16[3,3,3,8192]{3,2,1,0:T(4,128)(2,1)} %down_ref.1) | copy-start | bytes 1327108
  7.4 1.0 %copy-start.1 = (bf16[3,3,3,4096]{3,2,1,0:T(4,128)(2,1)S(1)}, bf16[3,3,3,4096]{3,2,1,0:T(4,128)(2,1)}, u32[]{:S(2)}) copy-start(bf16[3,3,3,4096]{3,2,1,0:T(4,128)(2,1)} %conv_ref.1) | copy-start | bytes 663556
  13.7 13.9 %collective-permute-start.2 = (bf16[11,2,16,512]{3,2,1,0:T(8,128)(2,1)S(1)}, bf16[11,2,16,512]{3,2,1,0:T(8,128)(2,1)S(1)}, u32[]{:S(2)}, u32[]{:S(2)}) collective-permute-start(bf16[11,2,16,512]{3,2,1,0:T(8,128)(2,1)S(1)} %get-tuple-element.23.refs_1_), channel_id=1, source_target_pairs={{0,4},{8,12},{4,0},{12,8},{1,5},{9,13},{5,1},{13,9},{2,6},{10,14},... | collective-permute-start | bytes 1081352 | tf_op jit(solution)/shard_map/ppermute | solution.py:203
  14.7 12.9 %collective-permute-start.3 = (bf16[11,2,16,512]{3,2,1,0:T(8,128)(2,1)S(1)}, bf16[11,2,16,512]{3,2,1,0:T(8,128)(2,1)S(1)}, u32[]{:S(2)}, u32[]{:S(2)}) collective-permute-start(bf16[11,2,16,512]{3,2,1,0:T(8,128)(2,1)S(1)} %get-tuple-element.23.refs_1_), channel_id=1, source_target_pairs={{4,8},{8,4},{5,9},{9,5},{6,10},{10,6},{7,11},{11,7},{20,24},{24,20... | collective-permute-start | bytes 1081352 | tf_op jit(solution)/shard_map/ppermute | solution.py:203
  17.8 19.2 %collective-permute-start.4 = (bf16[11,2,16,512]{3,2,1,0:T(8,128)(2,1)S(1)}, bf16[11,2,16,512]{3,2,1,0:T(8,128)(2,1)S(1)}, u32[]{:S(2)}, u32[]{:S(2)}) collective-permute-start(bf16[11,2,16,512]{3,2,1,0:T(8,128)(2,1)S(1)} %get-tuple-element.25), channel_id=1, source_target_pairs={{0,2},{1,3},{2,0},{3,1},{4,6},{5,7},{6,4},{7,5},{8,10},{9,11},{10,... | collective-permute-start | bytes 1081352 | tf_op jit(solution)/shard_map/ppermute | solution.py:281
  24.1 17.1 %collective-permute-start.5 = (bf16[22,2,16,512]{3,2,1,0:T(8,128)(2,1)S(1)}, bf16[22,2,16,512]{3,2,1,0:T(8,128)(2,1)S(1)}, u32[]{:S(2)}, u32[]{:S(2)}) collective-permute-start(bf16[22,2,16,512]{3,2,1,0:T(8,128)(2,1)S(1)} %shard_map.39.refs_2_), channel_id=1, source_target_pairs={{0,4},{8,12},{4,0},{12,8},{1,5},{9,13},{5,1},{13,9},{2,6},{10,14},... | collective-permute-start | bytes 2162696 | tf_op jit(solution)/shard_map/ppermute | solution.py:203
  24.7 16.5 %collective-permute-start.6 = (bf16[22,2,16,512]{3,2,1,0:T(8,128)(2,1)S(1)}, bf16[22,2,16,512]{3,2,1,0:T(8,128)(2,1)S(1)}, u32[]{:S(2)}, u32[]{:S(2)}) collective-permute-start(bf16[22,2,16,512]{3,2,1,0:T(8,128)(2,1)S(1)} %shard_map.39.refs_2_), channel_id=1, source_target_pairs={{4,8},{8,4},{5,9},{9,5},{6,10},{10,6},{7,11},{11,7},{20,24},{24,20... | collective-permute-start | bytes 2162696 | tf_op jit(solution)/shard_map/ppermute | solution.py:203
  36.9 6.8 %collective-permute-start.7 = (bf16[11,2,16,512]{3,2,1,0:T(8,128)(2,1)S(1)}, bf16[11,2,16,512]{3,2,1,0:T(8,128)(2,1)S(1)}, u32[]{:S(2)}, u32[]{:S(2)}) collective-permute-start(bf16[11,2,16,512]{3,2,1,0:T(8,128)(2,1)S(1)} %collective-permute-done.4.refs_2_), channel_id=1, source_target_pairs={{0,4},{8,12},{4,0},{12,8},{1,5},{9,13},{5,1},{13,9},{2,6},{10,14},... | collective-permute-start | bytes 1081352 | tf_op jit(solution)/shard_map/ppermute | solution.py:203
  38.0 8.7 %collective-permute-start.8 = (bf16[11,2,16,512]{3,2,1,0:T(8,128)(2,1)S(1)}, bf16[11,2,16,512]{3,2,1,0:T(8,128)(2,1)S(1)}, u32[]{:S(2)}, u32[]{:S(2)}) collective-permute-start(bf16[11,2,16,512]{3,2,1,0:T(8,128)(2,1)S(1)} %collective-permute-done.4.refs_2_), channel_id=1, source_target_pairs={{4,8},{8,4},{5,9},{9,5},{6,10},{10,6},{7,11},{11,7},{20,24},{24,20... | collective-permute-start | bytes 1081352 | tf_op jit(solution)/shard_map/ppermute | solution.py:203

commit v9 on v8

--- a/solution.py
+++ b/solution.py
@@ -30,7 +30,7 @@
     return jnp.where(source == wanted, 1.0, 0.0).astype(jnp.bfloat16)
 
 
-def send_kernel(band, distances, volume_ref, *refs):
+def send_kernel(band, parts, volume_ref, *refs):
     out_refs, (block_ref, field_ref, sems) = refs[:-3], refs[-3:]
     count, planes, all_rows, width = volume_ref.shape
     step = block_ref.shape[2]
@@ -57,8 +57,8 @@
         block = jnp.concatenate([left[:, :cut], right[:, :cut], left[:, cut:], right[:, cut:]], axis=1)
         field_ref[pl.ds(BELOW + at, step), p] = block.reshape(step, count, width)
     me = lax.axis_index("filt")
-    for d, out_ref in zip(distances, out_refs):
-        start = lax.bitwise_xor(me, d) * band
+    for (d, low, _), out_ref in zip(parts, out_refs):
+        start = lax.bitwise_xor(me, d) * band + low
         out_ref[...] = field_ref[pl.ds(start, out_ref.shape[0])]
 
 
@@ -93,13 +93,13 @@
     def __init__(self, inside, channels, blocks):
         self.inside, self.channels, self.blocks = inside, channels, blocks
         self.planes = (2, 3) if inside else (0, 1, 4)
-        self.arrays = 1 + max(i for i, _, _ in blocks)
+        self.arrays = 1 + max(block[0] for block in blocks)
 
 
 def conv_kernel(groups, window, first, last, *refs):
     space, band = lax.axis_index("space"), lax.axis_index("filt")
     odd = lax.rem(space, 2)
-    places = ((2 - 2 * odd, 3 - 2 * odd), (2 * odd, 1 + 2 * odd))
+    places = ((2 * odd, 1 + 2 * odd), (2 - 2 * odd, 3 - 2 * odd))
     refs = list(refs)
     feature_ref = None if first else refs.pop(0)
     second_ref = refs.pop(0) if last else None
@@ -108,11 +108,11 @@
     hid_ref = refs.pop(0) if last else None
     half = out_ref.shape[-1]
     for group, (_, *blocks), taps_ref in zip(groups, inputs, refs):
-        for i, row, at in group.blocks:
-            for r in range(window):
+        for i, row, at, low, high in group.blocks:
+            for r in range(low, high):
                 for k in range(2):
                     place = k if group.inside else places[i % 2][k]
-                    store_taps(taps_ref.at[place], r, at, group.channels, blocks[i][row + r, k])
+                    store_taps(taps_ref.at[place], r, at, group.channels, blocks[i][row + r - low, k])
     size = 2 * C
     lane = lax.broadcasted_iota(jnp.int32, (C, half), 1)
     for y in range(window - 2):
@@ -195,11 +195,13 @@
                     first_ref[pl.ds(at, C // 2), :] = total[a * C // 2 : (a + 1) * C // 2]
 
 
-def swapped(block, axis):
+def swapped(block, axis, *others):
     count = lax.axis_size(axis)
     results = []
-    for start in (0, 1):
+    for start in (1, 0):
         pairs = [(i, i + 1) for i in range(start, count - 1, 2)]
+        if start == 0 and others:
+            block = after(block, *others)
         results.append(lax.ppermute(block, axis, pairs + [(j, i) for i, j in pairs]))
     return results
 
@@ -261,11 +263,16 @@
 
     if direct:
         step = 16
+        cut = (window + 1) // 2
+        sends = [(d, 0, window) for d in distances[:3]] + [(2, 0, cut), (2, cut, window)]
         sent = pl.pallas_call(
-            functools.partial(send_kernel, band, distances),
-            out_shape=[jax.ShapeDtypeStruct((window, planes, count, width), jnp.bfloat16)] * bands,
+            functools.partial(send_kernel, band, sends),
+            out_shape=[
+                jax.ShapeDtypeStruct((high - low, planes, count, width), jnp.bfloat16)
+                for _, low, high in sends
+            ],
             in_specs=[pl.BlockSpec(memory_space=pltpu.HBM)],
-            out_specs=[vmem] * bands,
+            out_specs=[vmem] * len(sends),
             scratch_shapes=[
                 pltpu.VMEM((planes * all_rows // step, count, step, width), jnp.bfloat16),
                 pltpu.VMEM((BELOW + all_rows + ABOVE, planes, count, width), jnp.bfloat16),
@@ -276,7 +283,7 @@
         )(pltpu.with_memory_space_constraint(volume, pltpu.HBM))
         second, *firsts = lay(conv_weight, down_weight)
         own = []
-        for d, piece in zip(distances, sent):
+        for (d, _, _), piece in zip(sends, sent):
             if d:
                 piece = lax.ppermute(piece, "filt", [(i, i ^ d) for i in range(bands)])
             own.append(piece)
@@ -291,24 +298,33 @@
         )(*map(in_vmem, own[1:3]))
         middles = swapped(middle, "space")
         all_three, of_own, of_middle, of_last = firsts
+        full = (0, window)
         feature = convolve(
             None,
             [
-                (Group(True, 48, [(0, 0, 0), (1, 0, 16), (1, window, 32)]), all_three, own[0], middle),
-                (Group(False, 16, [(0, 0, 0), (1, 0, 0)]), of_own, *mine),
+                (
+                    Group(True, 48, [(0, 0, 0, *full), (1, 0, 16, *full), (1, window, 32, *full)]),
+                    all_three,
+                    own[0],
+                    middle,
+                ),
+                (Group(False, 16, [(0, 0, 0, *full), (1, 0, 0, *full)]), of_own, *mine),
             ],
         )
-        tails = swapped(after(own[3], feature), "space")
-        middles = [after(block, own[3]) for block in middles]
-        in_middle = [(i, at * window, at * 16) for i in range(2) for at in range(2)]
+        heads = swapped(after(own[3], feature), "space")
+        tails = swapped(after(own[4], feature), "space")
+        middles = [after(block, own[4]) for block in middles]
+        in_middle = [(i, at * window, at * 16, *full) for i in range(2) for at in range(2)]
+        halves = ((0, cut), (cut, window))
         feature = convolve(
             feature,
             [
-                (Group(True, 16, [(0, 0, 0)]), of_last, own[3]),
+                (Group(True, 16, [(i, 0, 0, *halves[i]) for i in range(2)]), of_last, own[3], own[4]),
                 (Group(False, 32, in_middle), of_middle, *middles),
             ],
         )
-        coarse = convolve(feature, [(Group(False, 16, [(0, 0, 0), (1, 0, 0)]), of_last, *tails)], second)
+        in_last = [(i, 0, 0, *halves[i // 2]) for i in range(4)]
+        coarse = convolve(feature, [(Group(False, 16, in_last), of_last, *heads, *tails)], second)
     else:
         field = jnp.transpose(volume, (2, 1, 0, 3))
         field = jnp.concatenate([field[..., ::2], field[..., 1::2]], axis=-1)
@@ -317,8 +333,8 @@
         got = lax.all_to_all(sent, "filt", split_axis=0, concat_axis=0, tiled=True)
         own = jnp.transpose(got, (1, 2, 0, 3, 4)).reshape(window, planes, C, width)
         second, *firsts = lay(conv_weight, down_weight)
-        inside = (Group(True, C, [(0, 0, 0)]), firsts[0], own)
-        outside = (Group(False, C, [(0, 0, 0), (1, 0, 0)]), firsts[0], *swapped(own, "space"))
+        inside = (Group(True, C, [(0, 0, 0, 0, window)]), firsts[0], own)
+        outside = (Group(False, C, [(0, 0, 0, 0, window), (1, 0, 0, 0, window)]), firsts[0], *swapped(own, "space"))
         coarse = convolve(None, [inside, outside], second)
     return jnp.transpose(coarse, (1, 0, 2))[:, None]
 

time: 49.7 us -> 47.8 us (0.962)
  waiting for transfers between devices: 14.9 us -> 3.6 us
  starting transfers between devices: 16.5 us -> 25.8 us
    ppermute x3 -> x4, waiting for transfers between devices: 11.9 us -> 2.61 us  [local(): piece = lax.ppermute(piece, 'filt', [(i, i ^ d) for i in range(bands)])]
    ppermute x6 -> x8, starting transfers between devices: 11.7 us -> 17.1 us  [swapped(): lax.ppermute(block, axis, pairs + [(j, i) for i, j in pairs])]
    ppermute x3 -> x4, starting transfers between devices: 4.78 us -> 8.75 us  [local(): piece = lax.ppermute(piece, 'filt', [(i, i ^ d) for i in range(bands)])]
    ppermute x6 -> x8, waiting for transfers between devices: 2.97 us -> 0.98 us  [swapped(): lax.ppermute(block, axis, pairs + [(j, i) for i, j in pairs])]
  transfers between devices with their start and end apart: 9 -> 12, of which waited for: 3 -> 3; matrix products, arithmetic and copies ran while one was open for 0% -> 0% of each run, Pallas kernels for 23% -> 23%
where the time goes in v9:
time: 47.8 us; the launch traced here: 47.6 us
  starting transfers between devices  25.8 us (54%)
  Pallas kernels  15 us (31%)
  waiting for transfers between devices  3.6 us (8%)
  local copies, waits for them, and re-layouts  2.93 us (6%)
    ppermute x8, starting transfers between devices, swapped(): lax.ppermute(block, axis, pairs + [(j, i) for i, j in pairs])  17.1 us
    ppermute x4, starting transfers between devices, local(): piece = lax.ppermute(piece, 'filt', [(i, i ^ d) for i in range(bands)])  8.75 us
    pallas_call x3, Pallas kernels, convolve(): pl.pallas_call(functools.partial(conv_kernel, kinds, window, feature is N...  7.53 us
    pallas_call x1, Pallas kernels, local(): second, *firsts = lay(conv_weight, down_weight)  5.37 us
    ppermute x4, waiting for transfers between devices, local(): piece = lax.ppermute(piece, 'filt', [(i, i ^ d) for i in range(bands)])  2.61 us
    pallas_call x1, Pallas kernels, local(): pl.pallas_call(functools.partial(send_kernel, band, sends), out_shape=[ja...  2.07 us
    unnamed x4, local copies, waits for them, and re-layouts  2.03 us
    ppermute x8, waiting for transfers between devices, swapped(): lax.ppermute(block, axis, pairs + [(j, i) for i, j in pairs])  0.98 us
  transfers between devices with their start and end apart: 12, of which 3 were waited for; matrix products, arithmetic and copies ran while one was open for 0% of the time, Pallas kernels for 23%

profile of v9, /device:TPU:1, one launch (start us, length us, event | category | flops | bytes accessed | tf_op | source)
XLA Modules:
  0.0 47.6 jit_solution(2820473895147386892)
XLA Ops:
  0.0 2.1 %shard_map.38 = (bf16[11,2,16,512]{3,2,1,0:T(8,128)(2,1)S(1)}, bf16[11,2,16,512]{3,2,1,0:T(8,128)(2,1)S(1)}, bf16[11,2,16,512]{3,2,1,0:T(8,128)(2,1)S(1)}, bf16[...) custom-call(bf16[16,2,32,512]{3,2,1,0:T(8,128)(2,1)} %volume_ref.1), custom_call_target="tpu_custom_call" | custom-call | flops 1 | bytes 1 | tf_op jit(solution)/shard_map/pallas_call | solution.py:268
  2.1 4.2 %collective-permute-start = (bf16[11,2,16,512]{3,2,1,0:T(8,128)(2,1)S(1)}, bf16[11,2,16,512]{3,2,1,0:T(8,128)(2,1)S(1)}, u32[]{:S(2)}, u32[]{:S(2)}) collective-permute-start(bf16[11,2,16,512]{3,2,1,0:T(8,128)(2,1)S(1)} %get-tuple-element.22), channel_id=1, source_target_pairs={{0,3},{1,2},{2,1},{3,0},{4,7},{5,6},{6,5},{7,4},{8,11},{9,10},{10,... | collective-permute-start | bytes 1081352 | tf_op jit(solution)/shard_map/ppermute | solution.py:288
  6.3 0.0 collective-permute-start.1
  6.3 1.1 %copy-done = bf16[3,3,3,8192]{3,2,1,0:T(4,128)(2,1)S(1)} copy-done((bf16[3,3,3,8192]{3,2,1,0:T(4,128)(2,1)S(1)}, bf16[3,3,3,8192]{3,2,1,0:T(4,128)(2,1)}, u32[]{:S(2)}) %copy-start) | copy-done | bytes 442392
  7.4 1.0 %copy-done.1 = bf16[3,3,3,4096]{3,2,1,0:T(4,128)(2,1)S(1)} copy-done((bf16[3,3,3,4096]{3,2,1,0:T(4,128)(2,1)S(1)}, bf16[3,3,3,4096]{3,2,1,0:T(4,128)(2,1)}, u32[]{:S(2)}) %copy-start.1) | copy-done | bytes 221208
  8.3 5.4 %shard_map.37 = (bf16[128,1792]{1,0:T(8,128)(2,1)S(1)}, bf16[384,576]{1,0:T(8,128)(2,1)S(1)}, bf16[384,192]{1,0:T(8,128)(2,1)S(1)}, bf16[384,384]{1,0:T(8,128)(2,1)S(1)}, bf16[384,192]{1,0:T(8,128)(2,1)S(1)}) custom-call(bf16[3,3,3,4096]{3,2,1,0:T(4,128)(2,1)S(1)} %copy-done.1, bf16[3,3,3,8192]{3,2,1,0:T(4,128)(2,1)S(1)} %copy-done), custom_call_target="tpu_custom_call" | custom-call | flops 1 | bytes 1 | tf_op jit(solution)/shard_map/pallas_call | solution.py:284
  13.7 4.0 %collective-permute-start.2 = (bf16[11,2,16,512]{3,2,1,0:T(8,128)(2,1)S(1)}, bf16[11,2,16,512]{3,2,1,0:T(8,128)(2,1)S(1)}, u32[]{:S(2)}, u32[]{:S(2)}) collective-permute-start(bf16[11,2,16,512]{3,2,1,0:T(8,128)(2,1)S(1)} %get-tuple-element.25.refs_1_), channel_id=1, source_target_pairs={{4,8},{8,4},{5,9},{9,5},{6,10},{10,6},{7,11},{11,7},{20,24},{24,20... | collective-permute-start | bytes 1081352 | tf_op jit(solution)/shard_map/ppermute | solution.py:205
  17.7 0.1 collective-permute-start.3
  17.8 0.6 %collective-permute-start.5 = (bf16[5,2,16,512]{3,2,1,0:T(8,128)(2,1)S(1)}, bf16[5,2,16,512]{3,2,1,0:T(8,128)(2,1)S(1)}, u32[]{:S(2)}, u32[]{:S(2)}) collective-permute-start(bf16[5,2,16,512]{3,2,1,0:T(8,128)(2,1)S(1)} %get-tuple-element.28), channel_id=1, source_target_pairs={{0,2},{1,3},{2,0},{3,1},{4,6},{5,7},{6,4},{7,5},{8,10},{9,11},{10,... | collective-permute-start | bytes 491528 | tf_op jit(solution)/shard_map/ppermute | solution.py:288
  18.3 0.0 collective-permute-done.one_ref
  18.3 4.0 %collective-permute-start.4 = (bf16[6,2,16,512]{3,2,1,0:T(8,128)(2,1)S(1)}, bf16[6,2,16,512]{3,2,1,0:T(8,128)(2,1)S(1)}, u32[]{:S(2)}, u32[]{:S(2)}) collective-permute-start(bf16[6,2,16,512]{3,2,1,0:T(8,128)(2,1)S(1)} %get-tuple-element.27), channel_id=1, source_target_pairs={{0,2},{1,3},{2,0},{3,1},{4,6},{5,7},{6,4},{7,5},{8,10},{9,11},{10,... | collective-permute-start | bytes 589832 | tf_op jit(solution)/shard_map/ppermute | solution.py:288
  22.3 1.8 %collective-permute-done.1.two_ref = bf16[11,2,16,512]{3,2,1,0:T(8,128)(2,1)S(1)} collective-permute-done((bf16[11,2,16,512]{3,2,1,0:T(8,128)(2,1)S(1)}, bf16[11,2,16,512]{3,2,1,0:T(8,128)(2,1)S(1)}, u32[]{:S(2)}, u32[]{:S(2)}) %collective-permute-start.1) | collective-permute-done | bytes 360480 | tf_op jit(solution)/shard_map/ppermute | solution.py:288
  24.1 4.5 %collective-permute-start.6 = (bf16[22,2,16,512]{3,2,1,0:T(8,128)(2,1)S(1)}, bf16[22,2,16,512]{3,2,1,0:T(8,128)(2,1)S(1)}, u32[]{:S(2)}, u32[]{:S(2)}) collective-permute-start(bf16[22,2,16,512]{3,2,1,0:T(8,128)(2,1)S(1)} %shard_map.39.refs_2_), channel_id=1, source_target_pairs={{4,8},{8,4},{5,9},{9,5},{6,10},{10,6},{7,11},{11,7},{20,24},{24,20... | collective-permute-start | bytes 2162696 | tf_op jit(solution)/shard_map/ppermute | solution.py:205
  28.6 0.0 collective-permute-done.2.refs_4_
  28.6 0.1 collective-permute-start.7
  28.7 0.0 collective-permute-done.3.refs_5_
  28.7 3.2 %shard_map.40.refs_0_ = f32[3456,256]{1,0:T(8,128)S(1)} custom-call(bf16[384,576]{1,0:T(8,128)(2,1)S(1)} %get-tuple-element.20.refs_0_, bf16[11,2,16,512]{3,2,1,0:T(8,128)(2,1)S(1)} %get-tuple-element.25.refs_1_, bf16[22,2,16,512]{3,2,1,0:T(8,128)(2,1)S(1)} %shard_map.39.refs_2_, bf16[384,192]{1,0:T(8,128)(2,1)S(1)} %get-tuple-element.24.refs_3_, ...), custom_call_target="tpu_custom_call" | custom-call | flops 8589934592 | bytes 16777216 | tf_op jit(solution)/shard_map/pallas_call | solution.py:254
  31.9 0.8 %collective-permute-done.5.refs_3_ = bf16[5,2,16,512]{3,2,1,0:T(8,128)(2,1)S(1)} collective-permute-done((bf16[5,2,16,512]{3,2,1,0:T(8,128)(2,1)S(1)}, bf16[5,2,16,512]{3,2,1,0:T(8,128)(2,1)S(1)}, u32[]{:S(2)}, u32[]{:S(2)}) %collective-permute-start.5) | collective-permute-done | bytes 163872 | tf_op jit(solution)/shard_map/ppermute | solution.py:288
  32.7 5.0 %collective-permute-start.10 = (bf16[5,2,16,512]{3,2,1,0:T(8,128)(2,1)S(1)}, bf16[5,2,16,512]{3,2,1,0:T(8,128)(2,1)S(1)}, u32[]{:S(2)}, u32[]{:S(2)}) collective-permute-start(bf16[5,2,16,512]{3,2,1,0:T(8,128)(2,1)S(1)} %collective-permute-done.5.refs_3_), channel_id=1, source_target_pairs={{4,8},{8,4},{5,9},{9,5},{6,10},{10,6},{7,11},{11,7},{20,24},{24,20... | collective-permute-start | bytes 491528 | tf_op jit(solution)/shard_map/ppermute | solution.py:205
  37.8 0.1 collective-permute-start.11
  37.8 0.0 collective-permute-done.4.refs_2_
  37.8 3.3 %collective-permute-start.8 = (bf16[6,2,16,512]{3,2,1,0:T(8,128)(2,1)S(1)}, bf16[6,2,16,512]{3,2,1,0:T(8,128)(2,1)S(1)}, u32[]{:S(2)}, u32[]{:S(2)}) collective-permute-start(bf16[6,2,16,512]{3,2,1,0:T(8,128)(2,1)S(1)} %collective-permute-done.4.refs_2_), channel_id=1, source_target_pairs={{4,8},{8,4},{5,9},{9,5},{6,10},{10,6},{7,11},{11,7},{20,24},{24,20... | collective-permute-start | bytes 589832 | tf_op jit(solution)/shard_map/ppermute | solution.py:205
  41.2 0.0 collective-permute-done.6.refs_5_
  41.2 0.1 collective-permute-start.9
  41.3 0.0 collective-permute-done.7.refs_6_
  41.3 2.6 %shard_map.41.refs_0_ = f32[3456,256]{1,0:T(8,128)S(1)} custom-call(f32[3456,256]{1,0:T(8,128)S(1)} %shard_map.40.refs_0_, bf16[384,192]{1,0:T(8,128)(2,1)S(1)} %get-tuple-element.26.refs_1_.refs_2_, bf16[6,2,16,512]{3,2,1,0:T(8,128)(2,1)S(1)} %collective-permute-done.4.refs_2_, bf16[5,2,16,512]{3,2,1,0:T(8,128)(2,1)S(1)} %collective-permute-done.5.refs_3_, ...), custom_call_target="tpu_custom_call" | custom-call | flops 8589934592 | bytes 16777216 | tf_op jit(solution)/shard_map/pallas_call | solution.py:254
  43.8 0.0 collective-permute-done.10.refs_5_
  43.9 0.0 collective-permute-done.11.refs_6_
  43.9 1.0 %collective-permute-done.8.refs_3_ = bf16[6,2,16,512]{3,2,1,0:T(8,128)(2,1)S(1)} collective-permute-done((bf16[6,2,16,512]{3,2,1,0:T(8,128)(2,1)S(1)}, bf16[6,2,16,512]{3,2,1,0:T(8,128)(2,1)S(1)}, u32[]{:S(2)}, u32[]{:S(2)}) %collective-permute-start.8) | collective-permute-done | bytes 196640 | tf_op jit(solution)/shard_map/ppermute | solution.py:205
  44.8 0.0 collective-permute-done.9.refs_4_
  44.8 1.8 %shard_map.42 = bf16[4,128,256]{2,1,0:T(8,128)(2,1)S(1)} custom-call(f32[3456,256]{1,0:T(8,128)S(1)} %shard_map.41.refs_0_, bf16[128,1792]{1,0:T(8,128)(2,1)S(1)} %get-tuple-element.32.refs_1_, bf16[384,192]{1,0:T(8,128)(2,1)S(1)} %get-tuple-element.26.refs_1_.refs_2_, bf16[6,2,16,512]{3,2,1,0:T(8,128)(2,1)S(1)} %collective-permute-done.8.refs_3_, ...), custom_call_target="tpu_custom_call" | custom-call | flops 8589934592 | bytes 16777216 | tf_op jit(solution)/shard_map/pallas_call | solution.py:254
  46.7 0.9 %copy.4 = bf16[128,1,4,256]{3,2,1,0:T(4,128)(2,1)} copy(bf16[128,1,4,256]{3,0,2,1:T(8,128)(2,1)S(1)} %bitcast.3) | data formatting | bytes 524288 | tf_op jit(solution)/shard_map/broadcast_in_dim | solution.py:339
  (3 shorter events, 0.1 us)
Async XLA Ops:
  2.1 16.2 %collective-permute-start = (bf16[11,2,16,512]{3,2,1,0:T(8,128)(2,1)S(1)}, bf16[11,2,16,512]{3,2,1,0:T(8,128)(2,1)S(1)}, u32[]{:S(2)}, u32[]{:S(2)}) collective-permute-start(bf16[11,2,16,512]{3,2,1,0:T(8,128)(2,1)S(1)} %get-tuple-element.22), channel_id=1, source_target_pairs={{0,3},{1,2},{2,1},{3,0},{4,7},{5,6},{6,5},{7,4},{8,11},{9,10},{10,... | collective-permute-start | bytes 1081352 | tf_op jit(solution)/shard_map/ppermute | solution.py:288
  6.3 17.7 %collective-permute-start.1 = (bf16[11,2,16,512]{3,2,1,0:T(8,128)(2,1)S(1)}, bf16[11,2,16,512]{3,2,1,0:T(8,128)(2,1)S(1)}, u32[]{:S(2)}, u32[]{:S(2)}) collective-permute-start(bf16[11,2,16,512]{3,2,1,0:T(8,128)(2,1)S(1)} %get-tuple-element.23), channel_id=1, source_target_pairs={{0,1},{1,0},{2,3},{3,2},{4,5},{5,4},{6,7},{7,6},{8,9},{9,8},{10,11... | collective-permute-start | bytes 1081352 | tf_op jit(solution)/shard_map/ppermute | solution.py:288
  6.3 1.1 %copy-start = (bf16[3,3,3,8192]{3,2,1,0:T(4,128)(2,1)S(1)}, bf16[3,3,3,8192]{3,2,1,0:T(4,128)(2,1)}, u32[]{:S(2)}) copy-start(bf16[3,3,3,8192]{3,2,1,0:T(4,128)(2,1)} %down_ref.1) | copy-start | bytes 1327108
  7.4 1.0 %copy-start.1 = (bf16[3,3,3,4096]{3,2,1,0:T(4,128)(2,1)S(1)}, bf16[3,3,3,4096]{3,2,1,0:T(4,128)(2,1)}, u32[]{:S(2)}) copy-start(bf16[3,3,3,4096]{3,2,1,0:T(4,128)(2,1)} %conv_ref.1) | copy-start | bytes 663556
  13.7 14.9 %collective-permute-start.2 = (bf16[11,2,16,512]{3,2,1,0:T(8,128)(2,1)S(1)}, bf16[11,2,16,512]{3,2,1,0:T(8,128)(2,1)S(1)}, u32[]{:S(2)}, u32[]{:S(2)}) collective-permute-start(bf16[11,2,16,512]{3,2,1,0:T(8,128)(2,1)S(1)} %get-tuple-element.25.refs_1_), channel_id=1, source_target_pairs={{4,8},{8,4},{5,9},{9,5},{6,10},{10,6},{7,11},{11,7},{20,24},{24,20... | collective-permute-start | bytes 1081352 | tf_op jit(solution)/shard_map/ppermute | solution.py:205
  17.7 11.0 %collective-permute-start.3 = (bf16[11,2,16,512]{3,2,1,0:T(8,128)(2,1)S(1)}, bf16[11,2,16,512]{3,2,1,0:T(8,128)(2,1)S(1)}, u32[]{:S(2)}, u32[]{:S(2)}) collective-permute-start(bf16[11,2,16,512]{3,2,1,0:T(8,128)(2,1)S(1)} %get-tuple-element.25.refs_1_), channel_id=1, source_target_pairs={{0,4},{8,12},{4,0},{12,8},{1,5},{9,13},{5,1},{13,9},{2,6},{10,14},... | collective-permute-start | bytes 1081352 | tf_op jit(solution)/shard_map/ppermute | solution.py:205
  17.8 15.0 %collective-permute-start.5 = (bf16[5,2,16,512]{3,2,1,0:T(8,128)(2,1)S(1)}, bf16[5,2,16,512]{3,2,1,0:T(8,128)(2,1)S(1)}, u32[]{:S(2)}, u32[]{:S(2)}) collective-permute-start(bf16[5,2,16,512]{3,2,1,0:T(8,128)(2,1)S(1)} %get-tuple-element.28), channel_id=1, source_target_pairs={{0,2},{1,3},{2,0},{3,1},{4,6},{5,7},{6,4},{7,5},{8,10},{9,11},{10,... | collective-permute-start | bytes 491528 | tf_op jit(solution)/shard_map/ppermute | solution.py:288
  18.3 19.5 %collective-permute-start.4 = (bf16[6,2,16,512]{3,2,1,0:T(8,128)(2,1)S(1)}, bf16[6,2,16,512]{3,2,1,0:T(8,128)(2,1)S(1)}, u32[]{:S(2)}, u32[]{:S(2)}) collective-permute-start(bf16[6,2,16,512]{3,2,1,0:T(8,128)(2,1)S(1)} %get-tuple-element.27), channel_id=1, source_target_pairs={{0,2},{1,3},{2,0},{3,1},{4,6},{5,7},{6,4},{7,5},{8,10},{9,11},{10,... | collective-permute-start | bytes 589832 | tf_op jit(solution)/shard_map/ppermute | solution.py:288
  24.1 17.1 %collective-permute-start.6 = (bf16[22,2,16,512]{3,2,1,0:T(8,128)(2,1)S(1)}, bf16[22,2,16,512]{3,2,1,0:T(8,128)(2,1)S(1)}, u32[]{:S(2)}, u32[]{:S(2)}) collective-permute-start(bf16[22,2,16,512]{3,2,1,0:T(8,128)(2,1)S(1)} %shard_map.39.refs_2_), channel_id=1, source_target_pairs={{4,8},{8,4},{5,9},{9,5},{6,10},{10,6},{7,11},{11,7},{20,24},{24,20... | collective-permute-start | bytes 2162696 | tf_op jit(solution)/shard_map/ppermute | solution.py:205
  28.6 12.6 %collective-permute-start.7 = (bf16[22,2,16,512]{3,2,1,0:T(8,128)(2,1)S(1)}, bf16[22,2,16,512]{3,2,1,0:T(8,128)(2,1)S(1)}, u32[]{:S(2)}, u32[]{:S(2)}) collective-permute-start(bf16[22,2,16,512]{3,2,1,0:T(8,128)(2,1)S(1)} %shard_map.39.refs_2_), channel_id=1, source_target_pairs={{0,4},{8,12},{4,0},{12,8},{1,5},{9,13},{5,1},{13,9},{2,6},{10,14},... | collective-permute-start | bytes 2162696 | tf_op jit(solution)/shard_map/ppermute | solution.py:205
  32.7 11.1 %collective-permute-start.10 = (bf16[5,2,16,512]{3,2,1,0:T(8,128)(2,1)S(1)}, bf16[5,2,16,512]{3,2,1,0:T(8,128)(2,1)S(1)}, u32[]{:S(2)}, u32[]{:S(2)}) collective-permute-start(bf16[5,2,16,512]{3,2,1,0:T(8,128)(2,1)S(1)} %collective-permute-done.5.refs_3_), channel_id=1, source_target_pairs={{4,8},{8,4},{5,9},{9,5},{6,10},{10,6},{7,11},{11,7},{20,24},{24,20... | collective-permute-start | bytes 491528 | tf_op jit(solution)/shard_map/ppermute | solution.py:205
  37.8 6.1 %collective-permute-start.11 = (bf16[5,2,16,512]{3,2,1,0:T(8,128)(2,1)S(1)}, bf16[5,2,16,512]{3,2,1,0:T(8,128)(2,1)S(1)}, u32[]{:S(2)}, u32[]{:S(2)}) collective-permute-start(bf16[5,2,16,512]{3,2,1,0:T(8,128)(2,1)S(1)} %collective-permute-done.5.refs_3_), channel_id=1, source_target_pairs={{0,4},{8,12},{4,0},{12,8},{1,5},{9,13},{5,1},{13,9},{2,6},{10,14},... | collective-permute-start | bytes 491528 | tf_op jit(solution)/shard_map/ppermute | solution.py:205
  37.8 7.0 %collective-permute-start.8 = (bf16[6,2,16,512]{3,2,1,0:T(8,128)(2,1)S(1)}, bf16[6,2,16,512]{3,2,1,0:T(8,128)(2,1)S(1)}, u32[]{:S(2)}, u32[]{:S(2)}) collective-permute-start(bf16[6,2,16,512]{3,2,1,0:T(8,128)(2,1)S(1)} %collective-permute-done.4.refs_2_), channel_id=1, source_target_pairs={{4,8},{8,4},{5,9},{9,5},{6,10},{10,6},{7,11},{11,7},{20,24},{24,20... | collective-permute-start | bytes 589832 | tf_op jit(solution)/shard_map/ppermute | solution.py:205
  41.2 3.6 %collective-permute-start.9 = (bf16[6,2,16,512]{3,2,1,0:T(8,128)(2,1)S(1)}, bf16[6,2,16,512]{3,2,1,0:T(8,128)(2,1)S(1)}, u32[]{:S(2)}, u32[]{:S(2)}) collective-permute-start(bf16[6,2,16,512]{3,2,1,0:T(8,128)(2,1)S(1)} %collective-permute-done.4.refs_2_), channel_id=1, source_target_pairs={{0,4},{8,12},{4,0},{12,8},{1,5},{9,13},{5,1},{13,9},{2,6},{10,14},... | collective-permute-start | bytes 589832 | tf_op jit(solution)/shard_map/ppermute | solution.py:205

commit v10 on v9

--- a/solution.py
+++ b/solution.py
@@ -225,7 +225,7 @@
     params = pltpu.CompilerParams(vmem_limit_bytes=VMEM_LIMIT)
     cost = pl.CostEstimate(flops=1, transcendentals=0, bytes_accessed=1)
     direct = count == 16 and bands == 4
-    distances = (0, 3, 1, 2) if direct else ()
+    distances = (0, 2, 1, 3) if direct else ()
     ranges = [(0, 48), (0, 16), (16, 32), (48, 16)] if direct else [(0, C)]
     lay = pl.pallas_call(
         functools.partial(weight_kernel, distances, ranges),
@@ -264,7 +264,7 @@
     if direct:
         step = 16
         cut = (window + 1) // 2
-        sends = [(d, 0, window) for d in distances[:3]] + [(2, 0, cut), (2, cut, window)]
+        sends = [(d, 0, window) for d in distances[:3]] + [(distances[3], 0, cut), (distances[3], cut, window)]
         sent = pl.pallas_call(
             functools.partial(send_kernel, band, sends),
             out_shape=[

time: 47.8 us -> 46.6 us (0.975); the launches traced: 47.6 us -> 45.8 us
  starting transfers between devices: 25.8 us -> 23.8 us
    ppermute x8, starting transfers between devices: 17.1 us -> 14.3 us  [swapped(): lax.ppermute(block, axis, pairs + [(j, i) for i, j in pairs])]
    ppermute x4, starting transfers between devices: 8.75 us -> 9.54 us  [local(): piece = lax.ppermute(piece, 'filt', [(i, i ^ d) for i in range(bands)])]
  transfers between devices with their start and end apart: 12 -> 12, of which waited for: 3 -> 2; matrix products, arithmetic and copies ran while one was open for 0% -> 0% of each run, Pallas kernels for 23% -> 24%
where the time goes in v10:
time: 46.6 us; the launch traced here: 45.8 us
  starting transfers between devices  23.8 us (51%)
  Pallas kernels  15 us (32%)
  waiting for transfers between devices  3.83 us (8%)
  local copies, waits for them, and re-layouts  2.93 us (6%)
    ppermute x8, starting transfers between devices, swapped(): lax.ppermute(block, axis, pairs + [(j, i) for i, j in pairs])  14.3 us
    ppermute x4, starting transfers between devices, local(): piece = lax.ppermute(piece, 'filt', [(i, i ^ d) for i in range(bands)])  9.54 us
    pallas_call x3, Pallas kernels, convolve(): pl.pallas_call(functools.partial(conv_kernel, kinds, window, feature is N...  7.53 us
    pallas_call x1, Pallas kernels, local(): second, *firsts = lay(conv_weight, down_weight)  5.37 us
    ppermute x4, waiting for transfers between devices, local(): piece = lax.ppermute(piece, 'filt', [(i, i ^ d) for i in range(bands)])  2.8 us
    pallas_call x1, Pallas kernels, local(): pl.pallas_call(functools.partial(send_kernel, band, sends), out_shape=[ja...  2.07 us
    unnamed x4, local copies, waits for them, and re-layouts  2.02 us
    ppermute x8, waiting for transfers between devices, swapped(): lax.ppermute(block, axis, pairs + [(j, i) for i, j in pairs])  1.03 us
  transfers between devices with their start and end apart: 12, of which 2 were waited for; matrix products, arithmetic and copies ran while one was open for 0% of the time, Pallas kernels for 24%

profile of v10, /device:TPU:1, one launch (start us, length us, event | category | flops | bytes accessed | tf_op | source)
XLA Modules:
  0.0 45.8 jit_solution(11671020127755823924)
XLA Ops:
  0.0 2.1 %shard_map.38 = (bf16[11,2,16,512]{3,2,1,0:T(8,128)(2,1)S(1)}, bf16[11,2,16,512]{3,2,1,0:T(8,128)(2,1)S(1)}, bf16[11,2,16,512]{3,2,1,0:T(8,128)(2,1)S(1)}, bf16[...) custom-call(bf16[16,2,32,512]{3,2,1,0:T(8,128)(2,1)} %volume_ref.1), custom_call_target="tpu_custom_call" | custom-call | flops 1 | bytes 1 | tf_op jit(solution)/shard_map/pallas_call | solution.py:268
  2.1 3.2 %collective-permute-start = (bf16[11,2,16,512]{3,2,1,0:T(8,128)(2,1)S(1)}, bf16[11,2,16,512]{3,2,1,0:T(8,128)(2,1)S(1)}, u32[]{:S(2)}, u32[]{:S(2)}) collective-permute-start(bf16[11,2,16,512]{3,2,1,0:T(8,128)(2,1)S(1)} %get-tuple-element.22), channel_id=1, source_target_pairs={{0,2},{1,3},{2,0},{3,1},{4,6},{5,7},{6,4},{7,5},{8,10},{9,11},{10,... | collective-permute-start | bytes 1081352 | tf_op jit(solution)/shard_map/ppermute | solution.py:288
  5.3 1.3 %collective-permute-start.1 = (bf16[11,2,16,512]{3,2,1,0:T(8,128)(2,1)S(1)}, bf16[11,2,16,512]{3,2,1,0:T(8,128)(2,1)S(1)}, u32[]{:S(2)}, u32[]{:S(2)}) collective-permute-start(bf16[11,2,16,512]{3,2,1,0:T(8,128)(2,1)S(1)} %get-tuple-element.23), channel_id=1, source_target_pairs={{0,1},{1,0},{2,3},{3,2},{4,5},{5,4},{6,7},{7,6},{8,9},{9,8},{10,11... | collective-permute-start | bytes 1081352 | tf_op jit(solution)/shard_map/ppermute | solution.py:288
  6.6 1.1 %copy-done = bf16[3,3,3,8192]{3,2,1,0:T(4,128)(2,1)S(1)} copy-done((bf16[3,3,3,8192]{3,2,1,0:T(4,128)(2,1)S(1)}, bf16[3,3,3,8192]{3,2,1,0:T(4,128)(2,1)}, u32[]{:S(2)}) %copy-start) | copy-done | bytes 442392
  7.7 1.0 %copy-done.1 = bf16[3,3,3,4096]{3,2,1,0:T(4,128)(2,1)S(1)} copy-done((bf16[3,3,3,4096]{3,2,1,0:T(4,128)(2,1)S(1)}, bf16[3,3,3,4096]{3,2,1,0:T(4,128)(2,1)}, u32[]{:S(2)}) %copy-start.1) | copy-done | bytes 221208
  8.6 5.4 %shard_map.37 = (bf16[128,1792]{1,0:T(8,128)(2,1)S(1)}, bf16[384,576]{1,0:T(8,128)(2,1)S(1)}, bf16[384,192]{1,0:T(8,128)(2,1)S(1)}, bf16[384,384]{1,0:T(8,128)(2,1)S(1)}, bf16[384,192]{1,0:T(8,128)(2,1)S(1)}) custom-call(bf16[3,3,3,4096]{3,2,1,0:T(4,128)(2,1)S(1)} %copy-done.1, bf16[3,3,3,8192]{3,2,1,0:T(4,128)(2,1)S(1)} %copy-done), custom_call_target="tpu_custom_call" | custom-call | flops 1 | bytes 1 | tf_op jit(solution)/shard_map/pallas_call | solution.py:284
  14.0 4.2 %collective-permute-start.2 = (bf16[11,2,16,512]{3,2,1,0:T(8,128)(2,1)S(1)}, bf16[11,2,16,512]{3,2,1,0:T(8,128)(2,1)S(1)}, u32[]{:S(2)}, u32[]{:S(2)}) collective-permute-start(bf16[11,2,16,512]{3,2,1,0:T(8,128)(2,1)S(1)} %get-tuple-element.25.refs_1_), channel_id=1, source_target_pairs={{4,8},{8,4},{5,9},{9,5},{6,10},{10,6},{7,11},{11,7},{20,24},{24,20... | collective-permute-start | bytes 1081352 | tf_op jit(solution)/shard_map/ppermute | solution.py:205
  18.2 0.1 collective-permute-start.3
  18.3 0.1 collective-permute-start.5
  18.4 2.8 %collective-permute-done.one_ref = bf16[11,2,16,512]{3,2,1,0:T(8,128)(2,1)S(1)} collective-permute-done((bf16[11,2,16,512]{3,2,1,0:T(8,128)(2,1)S(1)}, bf16[11,2,16,512]{3,2,1,0:T(8,128)(2,1)S(1)}, u32[]{:S(2)}, u32[]{:S(2)}) %collective-permute-start) | collective-permute-done | bytes 360480 | tf_op jit(solution)/shard_map/ppermute | solution.py:288
  21.2 5.0 %collective-permute-start.4 = (bf16[6,2,16,512]{3,2,1,0:T(8,128)(2,1)S(1)}, bf16[6,2,16,512]{3,2,1,0:T(8,128)(2,1)S(1)}, u32[]{:S(2)}, u32[]{:S(2)}) collective-permute-start(bf16[6,2,16,512]{3,2,1,0:T(8,128)(2,1)S(1)} %get-tuple-element.27), channel_id=1, source_target_pairs={{0,3},{1,2},{2,1},{3,0},{4,7},{5,6},{6,5},{7,4},{8,11},{9,10},{10,... | collective-permute-start | bytes 589832 | tf_op jit(solution)/shard_map/ppermute | solution.py:288
  26.2 0.0 collective-permute-done.1.two_ref
  26.2 4.0 %collective-permute-start.6 = (bf16[22,2,16,512]{3,2,1,0:T(8,128)(2,1)S(1)}, bf16[22,2,16,512]{3,2,1,0:T(8,128)(2,1)S(1)}, u32[]{:S(2)}, u32[]{:S(2)}) collective-permute-start(bf16[22,2,16,512]{3,2,1,0:T(8,128)(2,1)S(1)} %shard_map.39.refs_2_), channel_id=1, source_target_pairs={{4,8},{8,4},{5,9},{9,5},{6,10},{10,6},{7,11},{11,7},{20,24},{24,20... | collective-permute-start | bytes 2162696 | tf_op jit(solution)/shard_map/ppermute | solution.py:205
  30.2 0.0 collective-permute-done.2.refs_4_
  30.3 0.1 collective-permute-start.7
  30.3 0.0 collective-permute-done.3.refs_5_
  30.3 3.2 %shard_map.40.refs_0_ = f32[3456,256]{1,0:T(8,128)S(1)} custom-call(bf16[384,576]{1,0:T(8,128)(2,1)S(1)} %get-tuple-element.20.refs_0_, bf16[11,2,16,512]{3,2,1,0:T(8,128)(2,1)S(1)} %get-tuple-element.25.refs_1_, bf16[22,2,16,512]{3,2,1,0:T(8,128)(2,1)S(1)} %shard_map.39.refs_2_, bf16[384,192]{1,0:T(8,128)(2,1)S(1)} %get-tuple-element.24.refs_3_, ...), custom_call_target="tpu_custom_call" | custom-call | flops 8589934592 | bytes 16777216 | tf_op jit(solution)/shard_map/pallas_call | solution.py:254
  33.5 0.0 collective-permute-done.5.refs_3_
  33.5 1.9 %collective-permute-start.10 = (bf16[5,2,16,512]{3,2,1,0:T(8,128)(2,1)S(1)}, bf16[5,2,16,512]{3,2,1,0:T(8,128)(2,1)S(1)}, u32[]{:S(2)}, u32[]{:S(2)}) collective-permute-start(bf16[5,2,16,512]{3,2,1,0:T(8,128)(2,1)S(1)} %collective-permute-done.5.refs_3_), channel_id=1, source_target_pairs={{4,8},{8,4},{5,9},{9,5},{6,10},{10,6},{7,11},{11,7},{20,24},{24,20... | collective-permute-start | bytes 491528 | tf_op jit(solution)/shard_map/ppermute | solution.py:205
  35.4 0.1 collective-permute-start.11
  35.5 0.0 collective-permute-done.4.refs_2_
  35.5 3.8 %collective-permute-start.8 = (bf16[6,2,16,512]{3,2,1,0:T(8,128)(2,1)S(1)}, bf16[6,2,16,512]{3,2,1,0:T(8,128)(2,1)S(1)}, u32[]{:S(2)}, u32[]{:S(2)}) collective-permute-start(bf16[6,2,16,512]{3,2,1,0:T(8,128)(2,1)S(1)} %collective-permute-done.4.refs_2_), channel_id=1, source_target_pairs={{4,8},{8,4},{5,9},{9,5},{6,10},{10,6},{7,11},{11,7},{20,24},{24,20... | collective-permute-start | bytes 589832 | tf_op jit(solution)/shard_map/ppermute | solution.py:205
  39.4 0.0 collective-permute-done.6.refs_5_
  39.4 0.1 collective-permute-start.9
  39.5 0.0 collective-permute-done.7.refs_6_
  39.5 2.6 %shard_map.41.refs_0_ = f32[3456,256]{1,0:T(8,128)S(1)} custom-call(f32[3456,256]{1,0:T(8,128)S(1)} %shard_map.40.refs_0_, bf16[384,192]{1,0:T(8,128)(2,1)S(1)} %get-tuple-element.26.refs_1_.refs_2_, bf16[6,2,16,512]{3,2,1,0:T(8,128)(2,1)S(1)} %collective-permute-done.4.refs_2_, bf16[5,2,16,512]{3,2,1,0:T(8,128)(2,1)S(1)} %collective-permute-done.5.refs_3_, ...), custom_call_target="tpu_custom_call" | custom-call | flops 8589934592 | bytes 16777216 | tf_op jit(solution)/shard_map/pallas_call | solution.py:254
  42.0 0.0 collective-permute-done.10.refs_5_
  42.0 0.0 collective-permute-done.11.refs_6_
  42.1 1.0 %collective-permute-done.8.refs_3_ = bf16[6,2,16,512]{3,2,1,0:T(8,128)(2,1)S(1)} collective-permute-done((bf16[6,2,16,512]{3,2,1,0:T(8,128)(2,1)S(1)}, bf16[6,2,16,512]{3,2,1,0:T(8,128)(2,1)S(1)}, u32[]{:S(2)}, u32[]{:S(2)}) %collective-permute-start.8) | collective-permute-done | bytes 196640 | tf_op jit(solution)/shard_map/ppermute | solution.py:205
  43.1 0.0 collective-permute-done.9.refs_4_
  43.1 1.8 %shard_map.42 = bf16[4,128,256]{2,1,0:T(8,128)(2,1)S(1)} custom-call(f32[3456,256]{1,0:T(8,128)S(1)} %shard_map.41.refs_0_, bf16[128,1792]{1,0:T(8,128)(2,1)S(1)} %get-tuple-element.32.refs_1_, bf16[384,192]{1,0:T(8,128)(2,1)S(1)} %get-tuple-element.26.refs_1_.refs_2_, bf16[6,2,16,512]{3,2,1,0:T(8,128)(2,1)S(1)} %collective-permute-done.8.refs_3_, ...), custom_call_target="tpu_custom_call" | custom-call | flops 8589934592 | bytes 16777216 | tf_op jit(solution)/shard_map/pallas_call | solution.py:254
  44.9 0.9 %copy.4 = bf16[128,1,4,256]{3,2,1,0:T(4,128)(2,1)} copy(bf16[128,1,4,256]{3,0,2,1:T(8,128)(2,1)S(1)} %bitcast.3) | data formatting | bytes 524288 | tf_op jit(solution)/shard_map/broadcast_in_dim | solution.py:339
  (3 shorter events, 0.1 us)
Async XLA Ops:
  2.1 19.1 %collective-permute-start = (bf16[11,2,16,512]{3,2,1,0:T(8,128)(2,1)S(1)}, bf16[11,2,16,512]{3,2,1,0:T(8,128)(2,1)S(1)}, u32[]{:S(2)}, u32[]{:S(2)}) collective-permute-start(bf16[11,2,16,512]{3,2,1,0:T(8,128)(2,1)S(1)} %get-tuple-element.22), channel_id=1, source_target_pairs={{0,2},{1,3},{2,0},{3,1},{4,6},{5,7},{6,4},{7,5},{8,10},{9,11},{10,... | collective-permute-start | bytes 1081352 | tf_op jit(solution)/shard_map/ppermute | solution.py:288
  5.3 20.9 %collective-permute-start.1 = (bf16[11,2,16,512]{3,2,1,0:T(8,128)(2,1)S(1)}, bf16[11,2,16,512]{3,2,1,0:T(8,128)(2,1)S(1)}, u32[]{:S(2)}, u32[]{:S(2)}) collective-permute-start(bf16[11,2,16,512]{3,2,1,0:T(8,128)(2,1)S(1)} %get-tuple-element.23), channel_id=1, source_target_pairs={{0,1},{1,0},{2,3},{3,2},{4,5},{5,4},{6,7},{7,6},{8,9},{9,8},{10,11... | collective-permute-start | bytes 1081352 | tf_op jit(solution)/shard_map/ppermute | solution.py:288
  6.6 1.1 %copy-start = (bf16[3,3,3,8192]{3,2,1,0:T(4,128)(2,1)S(1)}, bf16[3,3,3,8192]{3,2,1,0:T(4,128)(2,1)}, u32[]{:S(2)}) copy-start(bf16[3,3,3,8192]{3,2,1,0:T(4,128)(2,1)} %down_ref.1) | copy-start | bytes 1327108
  7.7 1.0 %copy-start.1 = (bf16[3,3,3,4096]{3,2,1,0:T(4,128)(2,1)S(1)}, bf16[3,3,3,4096]{3,2,1,0:T(4,128)(2,1)}, u32[]{:S(2)}) copy-start(bf16[3,3,3,4096]{3,2,1,0:T(4,128)(2,1)} %conv_ref.1) | copy-start | bytes 663556
  14.0 16.2 %collective-permute-start.2 = (bf16[11,2,16,512]{3,2,1,0:T(8,128)(2,1)S(1)}, bf16[11,2,16,512]{3,2,1,0:T(8,128)(2,1)S(1)}, u32[]{:S(2)}, u32[]{:S(2)}) collective-permute-start(bf16[11,2,16,512]{3,2,1,0:T(8,128)(2,1)S(1)} %get-tuple-element.25.refs_1_), channel_id=1, source_target_pairs={{4,8},{8,4},{5,9},{9,5},{6,10},{10,6},{7,11},{11,7},{20,24},{24,20... | collective-permute-start | bytes 1081352 | tf_op jit(solution)/shard_map/ppermute | solution.py:205
  18.2 12.1 %collective-permute-start.3 = (bf16[11,2,16,512]{3,2,1,0:T(8,128)(2,1)S(1)}, bf16[11,2,16,512]{3,2,1,0:T(8,128)(2,1)S(1)}, u32[]{:S(2)}, u32[]{:S(2)}) collective-permute-start(bf16[11,2,16,512]{3,2,1,0:T(8,128)(2,1)S(1)} %get-tuple-element.25.refs_1_), channel_id=1, source_target_pairs={{0,4},{8,12},{4,0},{12,8},{1,5},{9,13},{5,1},{13,9},{2,6},{10,14},... | collective-permute-start | bytes 1081352 | tf_op jit(solution)/shard_map/ppermute | solution.py:205
  18.3 15.2 %collective-permute-start.5 = (bf16[5,2,16,512]{3,2,1,0:T(8,128)(2,1)S(1)}, bf16[5,2,16,512]{3,2,1,0:T(8,128)(2,1)S(1)}, u32[]{:S(2)}, u32[]{:S(2)}) collective-permute-start(bf16[5,2,16,512]{3,2,1,0:T(8,128)(2,1)S(1)} %get-tuple-element.28), channel_id=1, source_target_pairs={{0,3},{1,2},{2,1},{3,0},{4,7},{5,6},{6,5},{7,4},{8,11},{9,10},{10,... | collective-permute-start | bytes 491528 | tf_op jit(solution)/shard_map/ppermute | solution.py:288
  21.2 14.3 %collective-permute-start.4 = (bf16[6,2,16,512]{3,2,1,0:T(8,128)(2,1)S(1)}, bf16[6,2,16,512]{3,2,1,0:T(8,128)(2,1)S(1)}, u32[]{:S(2)}, u32[]{:S(2)}) collective-permute-start(bf16[6,2,16,512]{3,2,1,0:T(8,128)(2,1)S(1)} %get-tuple-element.27), channel_id=1, source_target_pairs={{0,3},{1,2},{2,1},{3,0},{4,7},{5,6},{6,5},{7,4},{8,11},{9,10},{10,... | collective-permute-start | bytes 589832 | tf_op jit(solution)/shard_map/ppermute | solution.py:288
  26.2 13.2 %collective-permute-start.6 = (bf16[22,2,16,512]{3,2,1,0:T(8,128)(2,1)S(1)}, bf16[22,2,16,512]{3,2,1,0:T(8,128)(2,1)S(1)}, u32[]{:S(2)}, u32[]{:S(2)}) collective-permute-start(bf16[22,2,16,512]{3,2,1,0:T(8,128)(2,1)S(1)} %shard_map.39.refs_2_), channel_id=1, source_target_pairs={{4,8},{8,4},{5,9},{9,5},{6,10},{10,6},{7,11},{11,7},{20,24},{24,20... | collective-permute-start | bytes 2162696 | tf_op jit(solution)/shard_map/ppermute | solution.py:205
  30.3 9.2 %collective-permute-start.7 = (bf16[22,2,16,512]{3,2,1,0:T(8,128)(2,1)S(1)}, bf16[22,2,16,512]{3,2,1,0:T(8,128)(2,1)S(1)}, u32[]{:S(2)}, u32[]{:S(2)}) collective-permute-start(bf16[22,2,16,512]{3,2,1,0:T(8,128)(2,1)S(1)} %shard_map.39.refs_2_), channel_id=1, source_target_pairs={{0,4},{8,12},{4,0},{12,8},{1,5},{9,13},{5,1},{13,9},{2,6},{10,14},... | collective-permute-start | bytes 2162696 | tf_op jit(solution)/shard_map/ppermute | solution.py:205
  33.5 8.5 %collective-permute-start.10 = (bf16[5,2,16,512]{3,2,1,0:T(8,128)(2,1)S(1)}, bf16[5,2,16,512]{3,2,1,0:T(8,128)(2,1)S(1)}, u32[]{:S(2)}, u32[]{:S(2)}) collective-permute-start(bf16[5,2,16,512]{3,2,1,0:T(8,128)(2,1)S(1)} %collective-permute-done.5.refs_3_), channel_id=1, source_target_pairs={{4,8},{8,4},{5,9},{9,5},{6,10},{10,6},{7,11},{11,7},{20,24},{24,20... | collective-permute-start | bytes 491528 | tf_op jit(solution)/shard_map/ppermute | solution.py:205
  35.4 6.6 %collective-permute-start.11 = (bf16[5,2,16,512]{3,2,1,0:T(8,128)(2,1)S(1)}, bf16[5,2,16,512]{3,2,1,0:T(8,128)(2,1)S(1)}, u32[]{:S(2)}, u32[]{:S(2)}) collective-permute-start(bf16[5,2,16,512]{3,2,1,0:T(8,128)(2,1)S(1)} %collective-permute-done.5.refs_3_), channel_id=1, source_target_pairs={{0,4},{8,12},{4,0},{12,8},{1,5},{9,13},{5,1},{13,9},{2,6},{10,14},... | collective-permute-start | bytes 491528 | tf_op jit(solution)/shard_map/ppermute | solution.py:205
  35.5 7.5 %collective-permute-start.8 = (bf16[6,2,16,512]{3,2,1,0:T(8,128)(2,1)S(1)}, bf16[6,2,16,512]{3,2,1,0:T(8,128)(2,1)S(1)}, u32[]{:S(2)}, u32[]{:S(2)}) collective-permute-start(bf16[6,2,16,512]{3,2,1,0:T(8,128)(2,1)S(1)} %collective-permute-done.4.refs_2_), channel_id=1, source_target_pairs={{4,8},{8,4},{5,9},{9,5},{6,10},{10,6},{7,11},{11,7},{20,24},{24,20... | collective-permute-start | bytes 589832 | tf_op jit(solution)/shard_map/ppermute | solution.py:205
  39.4 3.7 %collective-permute-start.9 = (bf16[6,2,16,512]{3,2,1,0:T(8,128)(2,1)S(1)}, bf16[6,2,16,512]{3,2,1,0:T(8,128)(2,1)S(1)}, u32[]{:S(2)}, u32[]{:S(2)}) collective-permute-start(bf16[6,2,16,512]{3,2,1,0:T(8,128)(2,1)S(1)} %collective-permute-done.4.refs_2_), channel_id=1, source_target_pairs={{0,4},{8,12},{4,0},{12,8},{1,5},{9,13},{5,1},{13,9},{2,6},{10,14},... | collective-permute-start | bytes 589832 | tf_op jit(solution)/shard_map/ppermute | solution.py:205

commit v11 on v10

--- a/solution.py
+++ b/solution.py
@@ -281,7 +281,10 @@
             compiler_params=params,
             cost_estimate=cost,
         )(pltpu.with_memory_space_constraint(volume, pltpu.HBM))
-        second, *firsts = lay(conv_weight, down_weight)
+        second, *firsts = lay(
+            pltpu.with_memory_space_constraint(conv_weight, pltpu.HBM),
+            pltpu.with_memory_space_constraint(down_weight, pltpu.HBM),
+        )
         own = []
         for (d, _, _), piece in zip(sends, sent):
             if d:

time: 46.6 us -> 46.5 us (level)
  local copies, waits for them, and re-layouts: 2.93 us -> 0.91 us
  Pallas kernels: 15 us -> 16.2 us
  waiting for transfers between devices: 3.83 us -> 4.7 us
    unnamed x4 -> x0, local copies, waits for them, and re-layouts: 2.02 us -> none
    pallas_call x1, Pallas kernels: 5.37 us -> 6.52 us  [local(): lay(pltpu.with_memory_space_constraint(conv_weight, pltpu.HBM), pltpu.wit...]
    ppermute x4, waiting for transfers between devices: 2.8 us -> 3.67 us  [local(): piece = lax.ppermute(piece, 'filt', [(i, i ^ d) for i in range(bands)])]
  transfers between devices with their start and end apart: 12 -> 12, of which waited for: 2 -> 2; matrix products, arithmetic and copies ran while one was open for 0% -> 0% of each run, Pallas kernels for 24% -> 27%
where the time goes in v11:
time: 46.5 us; the launch traced here: 45.8 us
  starting transfers between devices  23.8 us (51%)
  Pallas kernels  16.2 us (35%)
  waiting for transfers between devices  4.7 us (10%)
  local copies, waits for them, and re-layouts  0.91 us (2%)
    ppermute x8, starting transfers between devices, swapped(): lax.ppermute(block, axis, pairs + [(j, i) for i, j in pairs])  14.3 us
    ppermute x4, starting transfers between devices, local(): piece = lax.ppermute(piece, 'filt', [(i, i ^ d) for i in range(bands)])  9.54 us
    pallas_call x3, Pallas kernels, convolve(): pl.pallas_call(functools.partial(conv_kernel, kinds, window, feature is N...  7.53 us
    pallas_call x1, Pallas kernels, local(): lay(pltpu.with_memory_space_constraint(conv_weight, pltpu.HBM), pltpu.wit...  6.52 us
    ppermute x4, waiting for transfers between devices, local(): piece = lax.ppermute(piece, 'filt', [(i, i ^ d) for i in range(bands)])  3.67 us
    pallas_call x1, Pallas kernels, local(): pl.pallas_call(functools.partial(send_kernel, band, sends), out_shape=[ja...  2.07 us
    ppermute x8, waiting for transfers between devices, swapped(): lax.ppermute(block, axis, pairs + [(j, i) for i, j in pairs])  1.03 us
  transfers between devices with their start and end apart: 12, of which 2 were waited for; matrix products, arithmetic and copies ran while one was open for 0% of the time, Pallas kernels for 27%

profile of v11, /device:TPU:1, one launch (start us, length us, event | category | flops | bytes accessed | tf_op | source)
XLA Modules:
  0.0 45.8 jit_solution(3331089839411831206)
XLA Ops:
  0.0 2.1 %shard_map.38 = (bf16[11,2,16,512]{3,2,1,0:T(8,128)(2,1)S(1)}, bf16[11,2,16,512]{3,2,1,0:T(8,128)(2,1)S(1)}, bf16[11,2,16,512]{3,2,1,0:T(8,128)(2,1)S(1)}, bf16[...) custom-call(bf16[16,2,32,512]{3,2,1,0:T(8,128)(2,1)} %volume_ref.1), custom_call_target="tpu_custom_call" | custom-call | flops 1 | bytes 1 | tf_op jit(solution)/shard_map/pallas_call | solution.py:268
  2.1 3.2 %collective-permute-start = (bf16[11,2,16,512]{3,2,1,0:T(8,128)(2,1)S(1)}, bf16[11,2,16,512]{3,2,1,0:T(8,128)(2,1)S(1)}, u32[]{:S(2)}, u32[]{:S(2)}) collective-permute-start(bf16[11,2,16,512]{3,2,1,0:T(8,128)(2,1)S(1)} %get-tuple-element.22), channel_id=1, source_target_pairs={{0,2},{1,3},{2,0},{3,1},{4,6},{5,7},{6,4},{7,5},{8,10},{9,11},{10,... | collective-permute-start | bytes 1081352 | tf_op jit(solution)/shard_map/ppermute | solution.py:291
  5.3 1.3 %collective-permute-start.1 = (bf16[11,2,16,512]{3,2,1,0:T(8,128)(2,1)S(1)}, bf16[11,2,16,512]{3,2,1,0:T(8,128)(2,1)S(1)}, u32[]{:S(2)}, u32[]{:S(2)}) collective-permute-start(bf16[11,2,16,512]{3,2,1,0:T(8,128)(2,1)S(1)} %get-tuple-element.23), channel_id=1, source_target_pairs={{0,1},{1,0},{2,3},{3,2},{4,5},{5,4},{6,7},{7,6},{8,9},{9,8},{10,11... | collective-permute-start | bytes 1081352 | tf_op jit(solution)/shard_map/ppermute | solution.py:291
  6.6 6.5 %shard_map.37 = (bf16[128,1792]{1,0:T(8,128)(2,1)S(1)}, bf16[384,576]{1,0:T(8,128)(2,1)S(1)}, bf16[384,192]{1,0:T(8,128)(2,1)S(1)}, bf16[384,384]{1,0:T(8,128)(2,1)S(1)}, bf16[384,192]{1,0:T(8,128)(2,1)S(1)}) custom-call(bf16[3,3,3,4096]{3,2,1,0:T(4,128)(2,1)} %conv_ref.1, bf16[3,3,3,8192]{3,2,1,0:T(4,128)(2,1)} %down_ref.1), custom_call_target="tpu_custom_call" | custom-call | flops 1 | bytes 1 | tf_op jit(solution)/shard_map/pallas_call | solution.py:284
  13.1 4.2 %collective-permute-start.2 = (bf16[11,2,16,512]{3,2,1,0:T(8,128)(2,1)S(1)}, bf16[11,2,16,512]{3,2,1,0:T(8,128)(2,1)S(1)}, u32[]{:S(2)}, u32[]{:S(2)}) collective-permute-start(bf16[11,2,16,512]{3,2,1,0:T(8,128)(2,1)S(1)} %get-tuple-element.25.refs_1_), channel_id=1, source_target_pairs={{4,8},{8,4},{5,9},{9,5},{6,10},{10,6},{7,11},{11,7},{20,24},{24,20... | collective-permute-start | bytes 1081352 | tf_op jit(solution)/shard_map/ppermute | solution.py:205
  17.4 0.1 collective-permute-start.3
  17.5 0.1 collective-permute-start.5
  17.5 3.7 %collective-permute-done.one_ref = bf16[11,2,16,512]{3,2,1,0:T(8,128)(2,1)S(1)} collective-permute-done((bf16[11,2,16,512]{3,2,1,0:T(8,128)(2,1)S(1)}, bf16[11,2,16,512]{3,2,1,0:T(8,128)(2,1)S(1)}, u32[]{:S(2)}, u32[]{:S(2)}) %collective-permute-start) | collective-permute-done | bytes 360480 | tf_op jit(solution)/shard_map/ppermute | solution.py:291
  21.2 5.0 %collective-permute-start.4 = (bf16[6,2,16,512]{3,2,1,0:T(8,128)(2,1)S(1)}, bf16[6,2,16,512]{3,2,1,0:T(8,128)(2,1)S(1)}, u32[]{:S(2)}, u32[]{:S(2)}) collective-permute-start(bf16[6,2,16,512]{3,2,1,0:T(8,128)(2,1)S(1)} %get-tuple-element.27), channel_id=1, source_target_pairs={{0,3},{1,2},{2,1},{3,0},{4,7},{5,6},{6,5},{7,4},{8,11},{9,10},{10,... | collective-permute-start | bytes 589832 | tf_op jit(solution)/shard_map/ppermute | solution.py:291
  26.2 0.0 collective-permute-done.1.two_ref
  26.2 4.0 %collective-permute-start.6 = (bf16[22,2,16,512]{3,2,1,0:T(8,128)(2,1)S(1)}, bf16[22,2,16,512]{3,2,1,0:T(8,128)(2,1)S(1)}, u32[]{:S(2)}, u32[]{:S(2)}) collective-permute-start(bf16[22,2,16,512]{3,2,1,0:T(8,128)(2,1)S(1)} %shard_map.39.refs_2_), channel_id=1, source_target_pairs={{4,8},{8,4},{5,9},{9,5},{6,10},{10,6},{7,11},{11,7},{20,24},{24,20... | collective-permute-start | bytes 2162696 | tf_op jit(solution)/shard_map/ppermute | solution.py:205
  30.2 0.0 collective-permute-done.2.refs_4_
  30.3 0.1 collective-permute-start.7
  30.3 0.0 collective-permute-done.3.refs_5_
  30.3 3.2 %shard_map.40.refs_0_ = f32[3456,256]{1,0:T(8,128)S(1)} custom-call(bf16[384,576]{1,0:T(8,128)(2,1)S(1)} %get-tuple-element.20.refs_0_, bf16[11,2,16,512]{3,2,1,0:T(8,128)(2,1)S(1)} %get-tuple-element.25.refs_1_, bf16[22,2,16,512]{3,2,1,0:T(8,128)(2,1)S(1)} %shard_map.39.refs_2_, bf16[384,192]{1,0:T(8,128)(2,1)S(1)} %get-tuple-element.24.refs_3_, ...), custom_call_target="tpu_custom_call" | custom-call | flops 8589934592 | bytes 16777216 | tf_op jit(solution)/shard_map/pallas_call | solution.py:254
  33.5 0.0 collective-permute-done.5.refs_3_
  33.5 1.9 %collective-permute-start.10 = (bf16[5,2,16,512]{3,2,1,0:T(8,128)(2,1)S(1)}, bf16[5,2,16,512]{3,2,1,0:T(8,128)(2,1)S(1)}, u32[]{:S(2)}, u32[]{:S(2)}) collective-permute-start(bf16[5,2,16,512]{3,2,1,0:T(8,128)(2,1)S(1)} %collective-permute-done.5.refs_3_), channel_id=1, source_target_pairs={{4,8},{8,4},{5,9},{9,5},{6,10},{10,6},{7,11},{11,7},{20,24},{24,20... | collective-permute-start | bytes 491528 | tf_op jit(solution)/shard_map/ppermute | solution.py:205
  35.4 0.1 collective-permute-start.11
  35.5 0.0 collective-permute-done.4.refs_2_
  35.5 3.8 %collective-permute-start.8 = (bf16[6,2,16,512]{3,2,1,0:T(8,128)(2,1)S(1)}, bf16[6,2,16,512]{3,2,1,0:T(8,128)(2,1)S(1)}, u32[]{:S(2)}, u32[]{:S(2)}) collective-permute-start(bf16[6,2,16,512]{3,2,1,0:T(8,128)(2,1)S(1)} %collective-permute-done.4.refs_2_), channel_id=1, source_target_pairs={{4,8},{8,4},{5,9},{9,5},{6,10},{10,6},{7,11},{11,7},{20,24},{24,20... | collective-permute-start | bytes 589832 | tf_op jit(solution)/shard_map/ppermute | solution.py:205
  39.4 0.0 collective-permute-done.6.refs_5_
  39.4 0.1 collective-permute-start.9
  39.5 0.0 collective-permute-done.7.refs_6_
  39.5 2.6 %shard_map.41.refs_0_ = f32[3456,256]{1,0:T(8,128)S(1)} custom-call(f32[3456,256]{1,0:T(8,128)S(1)} %shard_map.40.refs_0_, bf16[384,192]{1,0:T(8,128)(2,1)S(1)} %get-tuple-element.26.refs_1_.refs_2_, bf16[6,2,16,512]{3,2,1,0:T(8,128)(2,1)S(1)} %collective-permute-done.4.refs_2_, bf16[5,2,16,512]{3,2,1,0:T(8,128)(2,1)S(1)} %collective-permute-done.5.refs_3_, ...), custom_call_target="tpu_custom_call" | custom-call | flops 8589934592 | bytes 16777216 | tf_op jit(solution)/shard_map/pallas_call | solution.py:254
  42.0 0.0 collective-permute-done.10.refs_5_
  42.0 0.0 collective-permute-done.11.refs_6_
  42.1 1.0 %collective-permute-done.8.refs_3_ = bf16[6,2,16,512]{3,2,1,0:T(8,128)(2,1)S(1)} collective-permute-done((bf16[6,2,16,512]{3,2,1,0:T(8,128)(2,1)S(1)}, bf16[6,2,16,512]{3,2,1,0:T(8,128)(2,1)S(1)}, u32[]{:S(2)}, u32[]{:S(2)}) %collective-permute-start.8) | collective-permute-done | bytes 196640 | tf_op jit(solution)/shard_map/ppermute | solution.py:205
  43.1 0.0 collective-permute-done.9.refs_4_
  43.1 1.8 %shard_map.42 = bf16[4,128,256]{2,1,0:T(8,128)(2,1)S(1)} custom-call(f32[3456,256]{1,0:T(8,128)S(1)} %shard_map.41.refs_0_, bf16[128,1792]{1,0:T(8,128)(2,1)S(1)} %get-tuple-element.32.refs_1_, bf16[384,192]{1,0:T(8,128)(2,1)S(1)} %get-tuple-element.26.refs_1_.refs_2_, bf16[6,2,16,512]{3,2,1,0:T(8,128)(2,1)S(1)} %collective-permute-done.8.refs_3_, ...), custom_call_target="tpu_custom_call" | custom-call | flops 8589934592 | bytes 16777216 | tf_op jit(solution)/shard_map/pallas_call | solution.py:254
  44.9 0.9 %copy.4 = bf16[128,1,4,256]{3,2,1,0:T(4,128)(2,1)} copy(bf16[128,1,4,256]{3,0,2,1:T(8,128)(2,1)S(1)} %bitcast.3) | data formatting | bytes 524288 | tf_op jit(solution)/shard_map/broadcast_in_dim | solution.py:342
  (1 shorter events, 0.0 us)
Async XLA Ops:
  2.1 19.1 %collective-permute-start = (bf16[11,2,16,512]{3,2,1,0:T(8,128)(2,1)S(1)}, bf16[11,2,16,512]{3,2,1,0:T(8,128)(2,1)S(1)}, u32[]{:S(2)}, u32[]{:S(2)}) collective-permute-start(bf16[11,2,16,512]{3,2,1,0:T(8,128)(2,1)S(1)} %get-tuple-element.22), channel_id=1, source_target_pairs={{0,2},{1,3},{2,0},{3,1},{4,6},{5,7},{6,4},{7,5},{8,10},{9,11},{10,... | collective-permute-start | bytes 1081352 | tf_op jit(solution)/shard_map/ppermute | solution.py:291
  5.3 20.9 %collective-permute-start.1 = (bf16[11,2,16,512]{3,2,1,0:T(8,128)(2,1)S(1)}, bf16[11,2,16,512]{3,2,1,0:T(8,128)(2,1)S(1)}, u32[]{:S(2)}, u32[]{:S(2)}) collective-permute-start(bf16[11,2,16,512]{3,2,1,0:T(8,128)(2,1)S(1)} %get-tuple-element.23), channel_id=1, source_target_pairs={{0,1},{1,0},{2,3},{3,2},{4,5},{5,4},{6,7},{7,6},{8,9},{9,8},{10,11... | collective-permute-start | bytes 1081352 | tf_op jit(solution)/shard_map/ppermute | solution.py:291
  13.1 17.1 %collective-permute-start.2 = (bf16[11,2,16,512]{3,2,1,0:T(8,128)(2,1)S(1)}, bf16[11,2,16,512]{3,2,1,0:T(8,128)(2,1)S(1)}, u32[]{:S(2)}, u32[]{:S(2)}) collective-permute-start(bf16[11,2,16,512]{3,2,1,0:T(8,128)(2,1)S(1)} %get-tuple-element.25.refs_1_), channel_id=1, source_target_pairs={{4,8},{8,4},{5,9},{9,5},{6,10},{10,6},{7,11},{11,7},{20,24},{24,20... | collective-permute-start | bytes 1081352 | tf_op jit(solution)/shard_map/ppermute | solution.py:205
  17.4 13.0 %collective-permute-start.3 = (bf16[11,2,16,512]{3,2,1,0:T(8,128)(2,1)S(1)}, bf16[11,2,16,512]{3,2,1,0:T(8,128)(2,1)S(1)}, u32[]{:S(2)}, u32[]{:S(2)}) collective-permute-start(bf16[11,2,16,512]{3,2,1,0:T(8,128)(2,1)S(1)} %get-tuple-element.25.refs_1_), channel_id=1, source_target_pairs={{0,4},{8,12},{4,0},{12,8},{1,5},{9,13},{5,1},{13,9},{2,6},{10,14},... | collective-permute-start | bytes 1081352 | tf_op jit(solution)/shard_map/ppermute | solution.py:205
  17.5 16.1 %collective-permute-start.5 = (bf16[5,2,16,512]{3,2,1,0:T(8,128)(2,1)S(1)}, bf16[5,2,16,512]{3,2,1,0:T(8,128)(2,1)S(1)}, u32[]{:S(2)}, u32[]{:S(2)}) collective-permute-start(bf16[5,2,16,512]{3,2,1,0:T(8,128)(2,1)S(1)} %get-tuple-element.28), channel_id=1, source_target_pairs={{0,3},{1,2},{2,1},{3,0},{4,7},{5,6},{6,5},{7,4},{8,11},{9,10},{10,... | collective-permute-start | bytes 491528 | tf_op jit(solution)/shard_map/ppermute | solution.py:291
  21.2 14.3 %collective-permute-start.4 = (bf16[6,2,16,512]{3,2,1,0:T(8,128)(2,1)S(1)}, bf16[6,2,16,512]{3,2,1,0:T(8,128)(2,1)S(1)}, u32[]{:S(2)}, u32[]{:S(2)}) collective-permute-start(bf16[6,2,16,512]{3,2,1,0:T(8,128)(2,1)S(1)} %get-tuple-element.27), channel_id=1, source_target_pairs={{0,3},{1,2},{2,1},{3,0},{4,7},{5,6},{6,5},{7,4},{8,11},{9,10},{10,... | collective-permute-start | bytes 589832 | tf_op jit(solution)/shard_map/ppermute | solution.py:291
  26.2 13.2 %collective-permute-start.6 = (bf16[22,2,16,512]{3,2,1,0:T(8,128)(2,1)S(1)}, bf16[22,2,16,512]{3,2,1,0:T(8,128)(2,1)S(1)}, u32[]{:S(2)}, u32[]{:S(2)}) collective-permute-start(bf16[22,2,16,512]{3,2,1,0:T(8,128)(2,1)S(1)} %shard_map.39.refs_2_), channel_id=1, source_target_pairs={{4,8},{8,4},{5,9},{9,5},{6,10},{10,6},{7,11},{11,7},{20,24},{24,20... | collective-permute-start | bytes 2162696 | tf_op jit(solution)/shard_map/ppermute | solution.py:205
  30.3 9.2 %collective-permute-start.7 = (bf16[22,2,16,512]{3,2,1,0:T(8,128)(2,1)S(1)}, bf16[22,2,16,512]{3,2,1,0:T(8,128)(2,1)S(1)}, u32[]{:S(2)}, u32[]{:S(2)}) collective-permute-start(bf16[22,2,16,512]{3,2,1,0:T(8,128)(2,1)S(1)} %shard_map.39.refs_2_), channel_id=1, source_target_pairs={{0,4},{8,12},{4,0},{12,8},{1,5},{9,13},{5,1},{13,9},{2,6},{10,14},... | collective-permute-start | bytes 2162696 | tf_op jit(solution)/shard_map/ppermute | solution.py:205
  33.5 8.5 %collective-permute-start.10 = (bf16[5,2,16,512]{3,2,1,0:T(8,128)(2,1)S(1)}, bf16[5,2,16,512]{3,2,1,0:T(8,128)(2,1)S(1)}, u32[]{:S(2)}, u32[]{:S(2)}) collective-permute-start(bf16[5,2,16,512]{3,2,1,0:T(8,128)(2,1)S(1)} %collective-permute-done.5.refs_3_), channel_id=1, source_target_pairs={{4,8},{8,4},{5,9},{9,5},{6,10},{10,6},{7,11},{11,7},{20,24},{24,20... | collective-permute-start | bytes 491528 | tf_op jit(solution)/shard_map/ppermute | solution.py:205
  35.4 6.6 %collective-permute-start.11 = (bf16[5,2,16,512]{3,2,1,0:T(8,128)(2,1)S(1)}, bf16[5,2,16,512]{3,2,1,0:T(8,128)(2,1)S(1)}, u32[]{:S(2)}, u32[]{:S(2)}) collective-permute-start(bf16[5,2,16,512]{3,2,1,0:T(8,128)(2,1)S(1)} %collective-permute-done.5.refs_3_), channel_id=1, source_target_pairs={{0,4},{8,12},{4,0},{12,8},{1,5},{9,13},{5,1},{13,9},{2,6},{10,14},... | collective-permute-start | bytes 491528 | tf_op jit(solution)/shard_map/ppermute | solution.py:205
  35.5 7.5 %collective-permute-start.8 = (bf16[6,2,16,512]{3,2,1,0:T(8,128)(2,1)S(1)}, bf16[6,2,16,512]{3,2,1,0:T(8,128)(2,1)S(1)}, u32[]{:S(2)}, u32[]{:S(2)}) collective-permute-start(bf16[6,2,16,512]{3,2,1,0:T(8,128)(2,1)S(1)} %collective-permute-done.4.refs_2_), channel_id=1, source_target_pairs={{4,8},{8,4},{5,9},{9,5},{6,10},{10,6},{7,11},{11,7},{20,24},{24,20... | collective-permute-start | bytes 589832 | tf_op jit(solution)/shard_map/ppermute | solution.py:205
  39.4 3.7 %collective-permute-start.9 = (bf16[6,2,16,512]{3,2,1,0:T(8,128)(2,1)S(1)}, bf16[6,2,16,512]{3,2,1,0:T(8,128)(2,1)S(1)}, u32[]{:S(2)}, u32[]{:S(2)}) collective-permute-start(bf16[6,2,16,512]{3,2,1,0:T(8,128)(2,1)S(1)} %collective-permute-done.4.refs_2_), channel_id=1, source_target_pairs={{0,4},{8,12},{4,0},{12,8},{1,5},{9,13},{5,1},{13,9},{2,6},{10,14},... | collective-permute-start | bytes 589832 | tf_op jit(solution)/shard_map/ppermute | solution.py:205

commit v12 on v11

--- a/solution.py
+++ b/solution.py
@@ -299,7 +299,7 @@
             compiler_params=params,
             cost_estimate=cost,
         )(*map(in_vmem, own[1:3]))
-        middles = swapped(middle, "space")
+        middles = swapped(middle, "space", *mine)
         all_three, of_own, of_middle, of_last = firsts
         full = (0, window)
         feature = convolve(

time: 46.5 us -> 46.5 us (level)
  no operation moved by 1% of the time
where the time goes in v12:
time: 46.5 us; the launch traced here: 45.8 us
  starting transfers between devices  23.8 us (51%)
  Pallas kernels  16.2 us (35%)
  waiting for transfers between devices  4.7 us (10%)
  local copies, waits for them, and re-layouts  0.91 us (2%)
    ppermute x8, starting transfers between devices, swapped(): lax.ppermute(block, axis, pairs + [(j, i) for i, j in pairs])  14.3 us
    ppermute x4, starting transfers between devices, local(): piece = lax.ppermute(piece, 'filt', [(i, i ^ d) for i in range(bands)])  9.54 us
    pallas_call x3, Pallas kernels, convolve(): pl.pallas_call(functools.partial(conv_kernel, kinds, window, feature is N...  7.53 us
    pallas_call x1, Pallas kernels, local(): lay(pltpu.with_memory_space_constraint(conv_weight, pltpu.HBM), pltpu.wit...  6.52 us
    ppermute x4, waiting for transfers between devices, local(): piece = lax.ppermute(piece, 'filt', [(i, i ^ d) for i in range(bands)])  3.67 us
    pallas_call x1, Pallas kernels, local(): pl.pallas_call(functools.partial(send_kernel, band, sends), out_shape=[ja...  2.07 us
    ppermute x8, waiting for transfers between devices, swapped(): lax.ppermute(block, axis, pairs + [(j, i) for i, j in pairs])  1.03 us
  transfers between devices with their start and end apart: 12, of which 2 were waited for; matrix products, arithmetic and copies ran while one was open for 0% of the time, Pallas kernels for 27%

profile of v12, /device:TPU:1, one launch (start us, length us, event | category | flops | bytes accessed | tf_op | source)
XLA Modules:
  0.0 45.8 jit_solution(9849440173109405477)
XLA Ops:
  0.0 2.1 %shard_map.38 = (bf16[11,2,16,512]{3,2,1,0:T(8,128)(2,1)S(1)}, bf16[11,2,16,512]{3,2,1,0:T(8,128)(2,1)S(1)}, bf16[11,2,16,512]{3,2,1,0:T(8,128)(2,1)S(1)}, bf16[...) custom-call(bf16[16,2,32,512]{3,2,1,0:T(8,128)(2,1)} %volume_ref.1), custom_call_target="tpu_custom_call" | custom-call | flops 1 | bytes 1 | tf_op jit(solution)/shard_map/pallas_call | solution.py:268
  2.1 3.2 %collective-permute-start = (bf16[11,2,16,512]{3,2,1,0:T(8,128)(2,1)S(1)}, bf16[11,2,16,512]{3,2,1,0:T(8,128)(2,1)S(1)}, u32[]{:S(2)}, u32[]{:S(2)}) collective-permute-start(bf16[11,2,16,512]{3,2,1,0:T(8,128)(2,1)S(1)} %get-tuple-element.23), channel_id=1, source_target_pairs={{0,2},{1,3},{2,0},{3,1},{4,6},{5,7},{6,4},{7,5},{8,10},{9,11},{10,... | collective-permute-start | bytes 1081352 | tf_op jit(solution)/shard_map/ppermute | solution.py:291
  5.3 1.3 %collective-permute-start.1 = (bf16[11,2,16,512]{3,2,1,0:T(8,128)(2,1)S(1)}, bf16[11,2,16,512]{3,2,1,0:T(8,128)(2,1)S(1)}, u32[]{:S(2)}, u32[]{:S(2)}) collective-permute-start(bf16[11,2,16,512]{3,2,1,0:T(8,128)(2,1)S(1)} %get-tuple-element.24), channel_id=1, source_target_pairs={{0,1},{1,0},{2,3},{3,2},{4,5},{5,4},{6,7},{7,6},{8,9},{9,8},{10,11... | collective-permute-start | bytes 1081352 | tf_op jit(solution)/shard_map/ppermute | solution.py:291
  6.6 6.5 %shard_map.37 = (bf16[128,1792]{1,0:T(8,128)(2,1)S(1)}, bf16[384,576]{1,0:T(8,128)(2,1)S(1)}, bf16[384,192]{1,0:T(8,128)(2,1)S(1)}, bf16[384,384]{1,0:T(8,128)(2,1)S(1)}, bf16[384,192]{1,0:T(8,128)(2,1)S(1)}) custom-call(bf16[3,3,3,4096]{3,2,1,0:T(4,128)(2,1)} %conv_ref.1, bf16[3,3,3,8192]{3,2,1,0:T(4,128)(2,1)} %down_ref.1), custom_call_target="tpu_custom_call" | custom-call | flops 1 | bytes 1 | tf_op jit(solution)/shard_map/pallas_call | solution.py:284
  13.1 4.2 %collective-permute-start.2 = (bf16[11,2,16,512]{3,2,1,0:T(8,128)(2,1)S(1)}, bf16[11,2,16,512]{3,2,1,0:T(8,128)(2,1)S(1)}, u32[]{:S(2)}, u32[]{:S(2)}) collective-permute-start(bf16[11,2,16,512]{3,2,1,0:T(8,128)(2,1)S(1)} %get-tuple-element.26.refs_1_), channel_id=1, source_target_pairs={{4,8},{8,4},{5,9},{9,5},{6,10},{10,6},{7,11},{11,7},{20,24},{24,20... | collective-permute-start | bytes 1081352 | tf_op jit(solution)/shard_map/ppermute | solution.py:205
  17.4 0.1 collective-permute-start.3
  17.5 0.1 collective-permute-start.5
  17.5 3.7 %collective-permute-done.one_ref = bf16[11,2,16,512]{3,2,1,0:T(8,128)(2,1)S(1)} collective-permute-done((bf16[11,2,16,512]{3,2,1,0:T(8,128)(2,1)S(1)}, bf16[11,2,16,512]{3,2,1,0:T(8,128)(2,1)S(1)}, u32[]{:S(2)}, u32[]{:S(2)}) %collective-permute-start) | collective-permute-done | bytes 360480 | tf_op jit(solution)/shard_map/ppermute | solution.py:291
  21.2 5.0 %collective-permute-start.4 = (bf16[6,2,16,512]{3,2,1,0:T(8,128)(2,1)S(1)}, bf16[6,2,16,512]{3,2,1,0:T(8,128)(2,1)S(1)}, u32[]{:S(2)}, u32[]{:S(2)}) collective-permute-start(bf16[6,2,16,512]{3,2,1,0:T(8,128)(2,1)S(1)} %get-tuple-element.28), channel_id=1, source_target_pairs={{0,3},{1,2},{2,1},{3,0},{4,7},{5,6},{6,5},{7,4},{8,11},{9,10},{10,... | collective-permute-start | bytes 589832 | tf_op jit(solution)/shard_map/ppermute | solution.py:291
  26.2 0.0 collective-permute-done.1.two_ref
  26.2 4.0 %collective-permute-start.6 = (bf16[22,2,16,512]{3,2,1,0:T(8,128)(2,1)S(1)}, bf16[22,2,16,512]{3,2,1,0:T(8,128)(2,1)S(1)}, u32[]{:S(2)}, u32[]{:S(2)}) collective-permute-start(bf16[22,2,16,512]{3,2,1,0:T(8,128)(2,1)S(1)} %shard_map.39.refs_2_), channel_id=1, source_target_pairs={{4,8},{8,4},{5,9},{9,5},{6,10},{10,6},{7,11},{11,7},{20,24},{24,20... | collective-permute-start | bytes 2162696 | tf_op jit(solution)/shard_map/ppermute | solution.py:205
  30.2 0.0 collective-permute-done.2.refs_4_
  30.3 0.0 collective-permute-done.3.refs_5_
  30.3 0.1 collective-permute-start.7
  30.3 3.2 %shard_map.40.refs_0_ = f32[3456,256]{1,0:T(8,128)S(1)} custom-call(bf16[384,576]{1,0:T(8,128)(2,1)S(1)} %get-tuple-element.21.refs_0_, bf16[11,2,16,512]{3,2,1,0:T(8,128)(2,1)S(1)} %get-tuple-element.26.refs_1_, bf16[22,2,16,512]{3,2,1,0:T(8,128)(2,1)S(1)} %shard_map.39.refs_2_, bf16[384,192]{1,0:T(8,128)(2,1)S(1)} %get-tuple-element.25.refs_3_, ...), custom_call_target="tpu_custom_call" | custom-call | flops 8589934592 | bytes 16777216 | tf_op jit(solution)/shard_map/pallas_call | solution.py:254
  33.5 0.0 collective-permute-done.5.refs_3_
  33.5 1.9 %collective-permute-start.10 = (bf16[5,2,16,512]{3,2,1,0:T(8,128)(2,1)S(1)}, bf16[5,2,16,512]{3,2,1,0:T(8,128)(2,1)S(1)}, u32[]{:S(2)}, u32[]{:S(2)}) collective-permute-start(bf16[5,2,16,512]{3,2,1,0:T(8,128)(2,1)S(1)} %collective-permute-done.5.refs_3_), channel_id=1, source_target_pairs={{4,8},{8,4},{5,9},{9,5},{6,10},{10,6},{7,11},{11,7},{20,24},{24,20... | collective-permute-start | bytes 491528 | tf_op jit(solution)/shard_map/ppermute | solution.py:205
  35.4 0.1 collective-permute-start.11
  35.5 0.0 collective-permute-done.4.refs_2_
  35.5 3.8 %collective-permute-start.8 = (bf16[6,2,16,512]{3,2,1,0:T(8,128)(2,1)S(1)}, bf16[6,2,16,512]{3,2,1,0:T(8,128)(2,1)S(1)}, u32[]{:S(2)}, u32[]{:S(2)}) collective-permute-start(bf16[6,2,16,512]{3,2,1,0:T(8,128)(2,1)S(1)} %collective-permute-done.4.refs_2_), channel_id=1, source_target_pairs={{4,8},{8,4},{5,9},{9,5},{6,10},{10,6},{7,11},{11,7},{20,24},{24,20... | collective-permute-start | bytes 589832 | tf_op jit(solution)/shard_map/ppermute | solution.py:205
  39.4 0.0 collective-permute-done.7.refs_6_
  39.4 0.1 collective-permute-start.9
  39.5 0.0 collective-permute-done.6.refs_5_
  39.5 2.6 %shard_map.41.refs_0_ = f32[3456,256]{1,0:T(8,128)S(1)} custom-call(f32[3456,256]{1,0:T(8,128)S(1)} %shard_map.40.refs_0_, bf16[384,192]{1,0:T(8,128)(2,1)S(1)} %get-tuple-element.27.refs_1_.refs_2_, bf16[6,2,16,512]{3,2,1,0:T(8,128)(2,1)S(1)} %collective-permute-done.4.refs_2_, bf16[5,2,16,512]{3,2,1,0:T(8,128)(2,1)S(1)} %collective-permute-done.5.refs_3_, ...), custom_call_target="tpu_custom_call" | custom-call | flops 8589934592 | bytes 16777216 | tf_op jit(solution)/shard_map/pallas_call | solution.py:254
  42.0 0.0 collective-permute-done.10.refs_5_
  42.0 0.0 collective-permute-done.11.refs_6_
  42.1 1.0 %collective-permute-done.8.refs_3_ = bf16[6,2,16,512]{3,2,1,0:T(8,128)(2,1)S(1)} collective-permute-done((bf16[6,2,16,512]{3,2,1,0:T(8,128)(2,1)S(1)}, bf16[6,2,16,512]{3,2,1,0:T(8,128)(2,1)S(1)}, u32[]{:S(2)}, u32[]{:S(2)}) %collective-permute-start.8) | collective-permute-done | bytes 196640 | tf_op jit(solution)/shard_map/ppermute | solution.py:205
  43.1 0.0 collective-permute-done.9.refs_4_
  43.1 1.8 %shard_map.42 = bf16[4,128,256]{2,1,0:T(8,128)(2,1)S(1)} custom-call(f32[3456,256]{1,0:T(8,128)S(1)} %shard_map.41.refs_0_, bf16[128,1792]{1,0:T(8,128)(2,1)S(1)} %get-tuple-element.34.refs_1_, bf16[384,192]{1,0:T(8,128)(2,1)S(1)} %get-tuple-element.27.refs_1_.refs_2_, bf16[6,2,16,512]{3,2,1,0:T(8,128)(2,1)S(1)} %collective-permute-done.8.refs_3_, ...), custom_call_target="tpu_custom_call" | custom-call | flops 8589934592 | bytes 16777216 | tf_op jit(solution)/shard_map/pallas_call | solution.py:254
  44.9 0.9 %copy.4 = bf16[128,1,4,256]{3,2,1,0:T(4,128)(2,1)} copy(bf16[128,1,4,256]{3,0,2,1:T(8,128)(2,1)S(1)} %bitcast.3) | data formatting | bytes 524288 | tf_op jit(solution)/shard_map/broadcast_in_dim | solution.py:342
  (1 shorter events, 0.0 us)
Async XLA Ops:
  2.1 19.1 %collective-permute-start = (bf16[11,2,16,512]{3,2,1,0:T(8,128)(2,1)S(1)}, bf16[11,2,16,512]{3,2,1,0:T(8,128)(2,1)S(1)}, u32[]{:S(2)}, u32[]{:S(2)}) collective-permute-start(bf16[11,2,16,512]{3,2,1,0:T(8,128)(2,1)S(1)} %get-tuple-element.23), channel_id=1, source_target_pairs={{0,2},{1,3},{2,0},{3,1},{4,6},{5,7},{6,4},{7,5},{8,10},{9,11},{10,... | collective-permute-start | bytes 1081352 | tf_op jit(solution)/shard_map/ppermute | solution.py:291
  5.3 20.9 %collective-permute-start.1 = (bf16[11,2,16,512]{3,2,1,0:T(8,128)(2,1)S(1)}, bf16[11,2,16,512]{3,2,1,0:T(8,128)(2,1)S(1)}, u32[]{:S(2)}, u32[]{:S(2)}) collective-permute-start(bf16[11,2,16,512]{3,2,1,0:T(8,128)(2,1)S(1)} %get-tuple-element.24), channel_id=1, source_target_pairs={{0,1},{1,0},{2,3},{3,2},{4,5},{5,4},{6,7},{7,6},{8,9},{9,8},{10,11... | collective-permute-start | bytes 1081352 | tf_op jit(solution)/shard_map/ppermute | solution.py:291
  13.1 17.1 %collective-permute-start.2 = (bf16[11,2,16,512]{3,2,1,0:T(8,128)(2,1)S(1)}, bf16[11,2,16,512]{3,2,1,0:T(8,128)(2,1)S(1)}, u32[]{:S(2)}, u32[]{:S(2)}) collective-permute-start(bf16[11,2,16,512]{3,2,1,0:T(8,128)(2,1)S(1)} %get-tuple-element.26.refs_1_), channel_id=1, source_target_pairs={{4,8},{8,4},{5,9},{9,5},{6,10},{10,6},{7,11},{11,7},{20,24},{24,20... | collective-permute-start | bytes 1081352 | tf_op jit(solution)/shard_map/ppermute | solution.py:205
  17.4 12.9 %collective-permute-start.3 = (bf16[11,2,16,512]{3,2,1,0:T(8,128)(2,1)S(1)}, bf16[11,2,16,512]{3,2,1,0:T(8,128)(2,1)S(1)}, u32[]{:S(2)}, u32[]{:S(2)}) collective-permute-start(bf16[11,2,16,512]{3,2,1,0:T(8,128)(2,1)S(1)} %get-tuple-element.26.refs_1_), channel_id=1, source_target_pairs={{0,4},{8,12},{4,0},{12,8},{1,5},{9,13},{5,1},{13,9},{2,6},{10,14},... | collective-permute-start | bytes 1081352 | tf_op jit(solution)/shard_map/ppermute | solution.py:205
  17.5 16.1 %collective-permute-start.5 = (bf16[5,2,16,512]{3,2,1,0:T(8,128)(2,1)S(1)}, bf16[5,2,16,512]{3,2,1,0:T(8,128)(2,1)S(1)}, u32[]{:S(2)}, u32[]{:S(2)}) collective-permute-start(bf16[5,2,16,512]{3,2,1,0:T(8,128)(2,1)S(1)} %get-tuple-element.29), channel_id=1, source_target_pairs={{0,3},{1,2},{2,1},{3,0},{4,7},{5,6},{6,5},{7,4},{8,11},{9,10},{10,... | collective-permute-start | bytes 491528 | tf_op jit(solution)/shard_map/ppermute | solution.py:291
  21.2 14.3 %collective-permute-start.4 = (bf16[6,2,16,512]{3,2,1,0:T(8,128)(2,1)S(1)}, bf16[6,2,16,512]{3,2,1,0:T(8,128)(2,1)S(1)}, u32[]{:S(2)}, u32[]{:S(2)}) collective-permute-start(bf16[6,2,16,512]{3,2,1,0:T(8,128)(2,1)S(1)} %get-tuple-element.28), channel_id=1, source_target_pairs={{0,3},{1,2},{2,1},{3,0},{4,7},{5,6},{6,5},{7,4},{8,11},{9,10},{10,... | collective-permute-start | bytes 589832 | tf_op jit(solution)/shard_map/ppermute | solution.py:291
  26.2 13.2 %collective-permute-start.6 = (bf16[22,2,16,512]{3,2,1,0:T(8,128)(2,1)S(1)}, bf16[22,2,16,512]{3,2,1,0:T(8,128)(2,1)S(1)}, u32[]{:S(2)}, u32[]{:S(2)}) collective-permute-start(bf16[22,2,16,512]{3,2,1,0:T(8,128)(2,1)S(1)} %shard_map.39.refs_2_), channel_id=1, source_target_pairs={{4,8},{8,4},{5,9},{9,5},{6,10},{10,6},{7,11},{11,7},{20,24},{24,20... | collective-permute-start | bytes 2162696 | tf_op jit(solution)/shard_map/ppermute | solution.py:205
  30.3 9.1 %collective-permute-start.7 = (bf16[22,2,16,512]{3,2,1,0:T(8,128)(2,1)S(1)}, bf16[22,2,16,512]{3,2,1,0:T(8,128)(2,1)S(1)}, u32[]{:S(2)}, u32[]{:S(2)}) collective-permute-start(bf16[22,2,16,512]{3,2,1,0:T(8,128)(2,1)S(1)} %shard_map.39.refs_2_), channel_id=1, source_target_pairs={{0,4},{8,12},{4,0},{12,8},{1,5},{9,13},{5,1},{13,9},{2,6},{10,14},... | collective-permute-start | bytes 2162696 | tf_op jit(solution)/shard_map/ppermute | solution.py:205
  33.5 8.5 %collective-permute-start.10 = (bf16[5,2,16,512]{3,2,1,0:T(8,128)(2,1)S(1)}, bf16[5,2,16,512]{3,2,1,0:T(8,128)(2,1)S(1)}, u32[]{:S(2)}, u32[]{:S(2)}) collective-permute-start(bf16[5,2,16,512]{3,2,1,0:T(8,128)(2,1)S(1)} %collective-permute-done.5.refs_3_), channel_id=1, source_target_pairs={{4,8},{8,4},{5,9},{9,5},{6,10},{10,6},{7,11},{11,7},{20,24},{24,20... | collective-permute-start | bytes 491528 | tf_op jit(solution)/shard_map/ppermute | solution.py:205
  35.4 6.6 %collective-permute-start.11 = (bf16[5,2,16,512]{3,2,1,0:T(8,128)(2,1)S(1)}, bf16[5,2,16,512]{3,2,1,0:T(8,128)(2,1)S(1)}, u32[]{:S(2)}, u32[]{:S(2)}) collective-permute-start(bf16[5,2,16,512]{3,2,1,0:T(8,128)(2,1)S(1)} %collective-permute-done.5.refs_3_), channel_id=1, source_target_pairs={{0,4},{8,12},{4,0},{12,8},{1,5},{9,13},{5,1},{13,9},{2,6},{10,14},... | collective-permute-start | bytes 491528 | tf_op jit(solution)/shard_map/ppermute | solution.py:205
  35.5 7.5 %collective-permute-start.8 = (bf16[6,2,16,512]{3,2,1,0:T(8,128)(2,1)S(1)}, bf16[6,2,16,512]{3,2,1,0:T(8,128)(2,1)S(1)}, u32[]{:S(2)}, u32[]{:S(2)}) collective-permute-start(bf16[6,2,16,512]{3,2,1,0:T(8,128)(2,1)S(1)} %collective-permute-done.4.refs_2_), channel_id=1, source_target_pairs={{4,8},{8,4},{5,9},{9,5},{6,10},{10,6},{7,11},{11,7},{20,24},{24,20... | collective-permute-start | bytes 589832 | tf_op jit(solution)/shard_map/ppermute | solution.py:205
  39.4 3.7 %collective-permute-start.9 = (bf16[6,2,16,512]{3,2,1,0:T(8,128)(2,1)S(1)}, bf16[6,2,16,512]{3,2,1,0:T(8,128)(2,1)S(1)}, u32[]{:S(2)}, u32[]{:S(2)}) collective-permute-start(bf16[6,2,16,512]{3,2,1,0:T(8,128)(2,1)S(1)} %collective-permute-done.4.refs_2_), channel_id=1, source_target_pairs={{0,4},{8,12},{4,0},{12,8},{1,5},{9,13},{5,1},{13,9},{2,6},{10,14},... | collective-permute-start | bytes 589832 | tf_op jit(solution)/shard_map/ppermute | solution.py:205
